TPU v7x, 256 devices: a whole 4x4x8 slice. The times are simulated.
256 devices in a mesh: rollout: 8 (over y, z_lo), shard: 32 (over z_hi, x, core).
Axes of the slice: x: 4, y: 4, z: 8 (z_hi: 4, z_lo: 2; z = z_hi * 2 + z_lo), core: 2. Of those that a mesh axis runs over, the one named last changes fastest.
Arguments:
- updated: bfloat16 [12, 7168, 1024], P(None, 'shard', 'rollout'), may hold values from -6 to 6
- trainer_base: bfloat16 [12, 7168, 1024], P(None, 'shard', 'rollout'), may hold values from -6 to 6
- rollout_base: bfloat16 [32, 1792, 1024], P('shard'), may hold values from -6 to 6
- sync_ids: int32 [8], replicated, may hold values from 0 to 11, as said below
- owner_map: int32 [8], replicated, may hold values from 0 to 7, each once
Outputs:
- synced: bfloat16 [32, 1792, 1024], P('shard')
Inputs may be any that keep to these rules, and one draw needn't show every extreme that they name: `sync_ids`: the ids are distinct. `owner_map`: each position appears once.
All inputs are finite; a program needn't handle non-finite values.
Results may differ from a plain program's by a relative error of at most 0.001.
Values may be sent and summed in bfloat16 or wider, within the bound.
No kernel may reach another device: no remote copies, remote signals or barrier semaphores. Data moves between devices by JAX's collectives and lax.ppermute only.
A program may use at most 128 MiB of HBM per device.

v0:
```python
import jax
import jax.numpy as jnp
from jax import lax
from jax.sharding import PartitionSpec as P

BLOCK = 128


def block_scale(largest):
    scale = jnp.full_like(largest, 2.0 ** (-24))
    for power in range(-24, 8):
        scale = jnp.where(largest > 448.0 * 2.0**power, scale * 2.0, scale)
    return scale


def onto_grid(ratio):
    magnitude = jnp.abs(ratio)
    spacing = jnp.full_like(magnitude, 2.0 ** (-9))
    for power in range(-5, 9):
        spacing = jnp.where(magnitude >= 2.0**power, spacing * 2.0, spacing)
    return jnp.sign(ratio) * spacing * jnp.floor(magnitude / spacing + 0.5)


def per_device(updated, trainer_base, rollout_base, sync_ids, owner_map):
    placing = jnp.argsort(owner_map)
    picked = jnp.take(sync_ids, placing)
    fresh = jnp.take(updated, picked, axis=0).astype(jnp.float32)
    older = jnp.take(trainer_base, picked, axis=0).astype(jnp.float32)
    delta = fresh - older
    experts, rows, columns = delta.shape
    blocks = delta.reshape(experts, rows, columns // BLOCK, BLOCK)
    largest = jnp.max(jnp.abs(blocks), axis=3, keepdims=True)
    scale = block_scale(largest).astype(jnp.bfloat16)
    scale = lax.optimization_barrier(scale)
    codes = onto_grid(blocks / scale.astype(jnp.float32)).astype(jnp.bfloat16)
    split = lax.axis_size("shard") // experts
    piece = rows // split
    codes = codes.reshape(experts * split, piece, columns)
    scales = scale.reshape(experts * split, piece, columns // BLOCK)
    codes, scales = (
        lax.all_gather(codes, "rollout", axis=2, tiled=True),
        lax.all_gather(scales, "rollout", axis=2, tiled=True),
    )
    codes, scales = (
        lax.all_to_all(codes, "shard", split_axis=0, concat_axis=1, tiled=True),
        lax.all_to_all(scales, "shard", split_axis=0, concat_axis=1, tiled=True),
    )
    owned, height, width = codes.shape
    values = codes.reshape(owned, height, width // BLOCK, BLOCK).astype(jnp.float32)
    values = values * scales.astype(jnp.float32)[..., None]
    values = values.reshape(owned, height, width)
    return (rollout_base.astype(jnp.float32) + values).astype(jnp.bfloat16)


def solution(mesh):
    return jax.shard_map(
        per_device,
        mesh=mesh,
        in_specs=(
            P(None, "shard", "rollout"),
            P(None, "shard", "rollout"),
            P("shard", None, None),
            P(),
            P(),
        ),
        out_specs=P("shard", None, None),
        check_vma=False,
    )
```

profile of v0, /device:TPU:1, one launch (start us, length us, event | category | flops | bytes accessed | tf_op | source)
XLA Modules:
  0.0 214.5 jit_solution(357115125070844765)
XLA Ops:
  6.5 0.0 copy-start
  6.5 0.0 all-gather.2.cloned.1.call-start
  6.5 1.7 sort.17
  8.2 1.3 gather_fusion
  9.6 0.0 copy-done
  9.6 0.6 gather_fusion.1
  10.2 1.7 gather_fusion.2
  12.0 0.5 abs_reduce_fusion
  12.4 0.1 fusion.2
  12.5 2.8 %multiply_convert_fusion = bf16[8,224,128]{2,1,0:T(8,128)(2,1)} fusion(f32[8,224]{1,0:T(8,128)S(1)} %bitcast_convert_fusion, bf16[8,224,128]{2,1,0:T(8,128)(2,1)S(1)} %gather_fusion.1, pred[8]{0:T(512)(128)(4,1)S(1)} %get-tuple-element.8, bf16[8,224,128]{2,1,0:T(8,128)(2,1)S(1)} %gather_fusion.2), kind=kLoop, calls=%fused_computation.19 | loop fusion | flops 12615680 | bytes 1383432 | tf_op jit(solution)/shard_map/convert_element_type | solution.py:35
  15.3 0.0 all-gather.2.cloned.1.call-update
  15.3 0.1 reshape.673
  15.4 23.6 %all_gather.7 = bf16[32,56,8]{1,0,2:T(8,128)(2,1)S(1)} all-gather(bf16[32,56,1]{1,0,2:T(8,128)(2,1)S(1)} %reshape.673), channel_id=1, replica_groups=mesh['rollout'=8,'shard'=32] {'rollout'}, dimensions={2}, use_global_device_ids=true | all-gather | bytes 32256 | tf_op jit(solution)/shard_map/all_gather | solution.py:42
  39.0 0.1 reshape.708
  39.2 27.3 %all_to_all.8 = bf16[32,2,224]{2,1,0:T(2,128)(2,1)S(1)} all-to-all(bf16[32,2,224]{2,1,0:T(2,128)(2,1)S(1)} %reshape.708), channel_id=1, replica_groups=mesh['rollout'=8,'shard'=32] {'shard'}, dimensions={0} | all-to-all | bytes 57344 | tf_op jit(solution)/shard_map/all_to_all | solution.py:46
  66.5 36.3 %all-gather.2.cloned.1.call-done = bf16[32,56,1024]{2,1,0:T(8,128)(2,1)} async-done(((bf16[32,56,128]{2,1,0:T(8,128)(2,1)}), bf16[32,56,1024]{2,1,0:T(8,128)(2,1)}) %all-gather.2.cloned.1.call-update) | async-done | bytes 3670032 | tf_op jit(solution)/shard_map/all_gather | solution.py:41
  102.7 9.5 %all-to-all-start = ((bf16[32,56,1024]{2,1,0:T(8,128)(2,1)}), bf16[32,56,1024]{2,1,0:T(8,128)(2,1)}, u32[]{:S(2)}, u32[]{:S(2)}) async-start(bf16[32,56,1024]{2,1,0:T(8,128)(2,1)} %all-gather.2.cloned.1.call-done), calls=%async_computation | async-start | bytes 7340032 | tf_op jit(solution)/shard_map/all_to_all | solution.py:45
  112.2 0.1 reshape.709
  112.3 0.2 copy.12
  112.5 4.3 %mul.474 = f32[1792,8,128]{2,1,0:T(8,128)} broadcast(f32[1792,8]{1,0:T(8,128)S(1)} %bitcast.85), dimensions={0,1} | broadcast | bytes 7397376 | tf_op jit(solution)/shard_map/mul | solution.py:50
  116.9 8.9 %mul.475 = f32[1,1792,1024]{2,1,0:T(8,128)} reshape(f32[1792,8,128]{2,1,0:T(8,128)} %mul.474) | data formatting | bytes 14680064 | tf_op jit(solution)/shard_map/mul | solution.py:50
  125.8 72.6 %all-to-all-done = bf16[32,56,1024]{2,1,0:T(8,128)(2,1)} async-done(((bf16[32,56,1024]{2,1,0:T(8,128)(2,1)}), bf16[32,56,1024]{2,1,0:T(8,128)(2,1)}, u32[]{:S(2)}, u32[]{:S(2)}) %all-to-all-start) | async-done | bytes 3670048 | tf_op jit(solution)/shard_map/all_to_all | solution.py:45
  198.4 9.2 %fusion.1 = bf16[1,1792,1024]{2,1,0:T(8,128)(2,1)} fusion(f32[1,1792,1024]{2,1,0:T(8,128)} %mul.475, bf16[1,1792,1024]{2,1,0:T(8,128)(2,1)} %param.9, bf16[1,1792,1024]{2,1,0:T(8,128)(2,1)} %bitcast.84), kind=kLoop, calls=%fused_computation.5 | loop fusion | flops 9175040 | bytes 18350080 | tf_op jit(solution)/shard_map/convert_element_type | solution.py:52
  (7 shorter events, 0.1 us)
Async XLA Ops:
  6.5 3.0 %copy-start = (bf16[12,224,128]{2,1,0:T(8,128)(2,1)S(1)}, bf16[12,224,128]{2,1,0:T(8,128)(2,1)}, u32[]{:S(2)}) copy-start(bf16[12,224,128]{2,1,0:T(8,128)(2,1)} %param.7) | copy-start | bytes 2064388
  6.5 96.2 %all-gather.2.cloned.1.call-start = ((), (), s32[]{:S(2)}) async-start(), calls=%async_computation.2 | async-start | bytes 4128768 | tf_op jit(solution)/shard_map/all_gather | solution.py:41
  102.7 95.7 %all-to-all-start = ((bf16[32,56,1024]{2,1,0:T(8,128)(2,1)}), bf16[32,56,1024]{2,1,0:T(8,128)(2,1)}, u32[]{:S(2)}, u32[]{:S(2)}) async-start(bf16[32,56,1024]{2,1,0:T(8,128)(2,1)} %all-gather.2.cloned.1.call-done), calls=%async_computation | async-start | bytes 7340032 | tf_op jit(solution)/shard_map/all_to_all | solution.py:45
Sparse Core Ops, SparseCore 0:
  15.4 87.2 all-gather.1
where the time goes:
time: 215 us; the launch traced here: 214 us
  waiting for transfers between devices  109 us (51%)
  blocking collectives  50.9 us (24%)
  local copies, waits for them, and re-layouts  17.5 us (8%)
  other arithmetic  14.2 us (7%)
  between operations  13.5 us (6%)
  starting transfers between devices  9.49 us (4%)
    all_to_all x1, waiting for transfers between devices, per_device(): lax.all_to_all(codes, 'shard', split_axis=0, concat_axis=1, tiled=True)  72.6 us
    all_gather x1, waiting for transfers between devices, per_device(): lax.all_gather(codes, 'rollout', axis=2, tiled=True)  36.3 us
    all_to_all x1, blocking collectives, per_device(): lax.all_to_all(scales, 'shard', split_axis=0, concat_axis=1, tiled=True)  27.3 us
    all_gather x1, blocking collectives, per_device(): lax.all_gather(scales, 'rollout', axis=2, tiled=True)  23.6 us
    mul x2, local copies, waits for them, and re-layouts, per_device(): values = values * scales.astype(jnp.float32)[..., None]  13.3 us
    all_to_all x1, starting transfers between devices, per_device(): lax.all_to_all(codes, 'shard', split_axis=0, concat_axis=1, tiled=True)  9.49 us
    convert_element_type x1, other arithmetic, per_device(): return (rollout_base.astype(jnp.float32) + values).astype(jnp.bfloat16)  9.19 us
  transfers between devices with their start and end apart: 2, of which 2 were waited for; matrix products, arithmetic and copies ran while one was open for 6% of the time, Pallas kernels for 0%

commit v1 on v0

v1 whole, which is shorter than its diff:
```python
import jax
import jax.numpy as jnp
from jax import lax
from jax.experimental import pallas as pl
from jax.experimental.pallas import tpu as pltpu
from jax.sharding import PartitionSpec as P

EXPERTS = 8
ROWS = 224
BLOCK = 128
PIECE = 56
OWNED = 1792
WIDTH = 1024
HALF = OWNED // 2
CHUNK = 448


def floor_power(magnitude):
    spread = magnitude * (2.0**23 + 1.0)
    power = spread - (spread - magnitude)
    return jnp.where(power > magnitude, power * 0.5, power)


def quantize(fresh, older):
    delta = fresh.astype(jnp.float32) - older.astype(jnp.float32)
    magnitude = jnp.abs(delta)
    largest = jnp.max(magnitude, axis=-1, keepdims=True)
    power = floor_power(largest)
    scale = jnp.where(largest > 1.75 * power, power * 2.0**-7, power * 2.0**-8)
    scale = jnp.maximum(scale, 2.0**-24)
    binade = jnp.maximum(floor_power(magnitude), scale * 2.0**-6)
    shift = binade * (1.5 * 2.0**20)
    rounded = (magnitude + shift) - shift
    tie = (magnitude - rounded) >= binade * 2.0**-4
    rounded = jnp.where(tie, rounded + binade * 2.0**-3, rounded)
    return jnp.where(delta < 0.0, -rounded, rounded).astype(jnp.bfloat16)


def encode_kernel(ids_ref, owner_ref, fresh_ref, older_ref, value_ref):
    value_ref[...] = quantize(fresh_ref[...], older_ref[...])


def encode(updated, trainer_base, sync_ids, owner_map):
    picked = pl.BlockSpec((1, ROWS, BLOCK), lambda e, ids, owner: (ids[e], 0, 0))
    placed = pl.BlockSpec((1, ROWS, BLOCK), lambda e, ids, owner: (owner[e], 0, 0))
    return pl.pallas_call(
        encode_kernel,
        grid_spec=pltpu.PrefetchScalarGridSpec(
            num_scalar_prefetch=2,
            grid=(EXPERTS,),
            in_specs=[picked, picked],
            out_specs=placed,
        ),
        out_shape=jax.ShapeDtypeStruct((EXPERTS, ROWS, BLOCK), jnp.bfloat16),
        name="encode",
    )(sync_ids, owner_map, updated, trainer_base)


def shifted(block, dy=0, dz=0):
    pairs = []
    for y in range(4):
        for z in range(2):
            pairs.append((y * 2 + z, (y + dy) % 4 * 2 + (z + dz) % 2))
    return lax.ppermute(block, "rollout", pairs)


def add_kernel(where_ref, base_ref, *refs):
    blocks, out_ref = refs[:-1], refs[-1]
    first = pl.program_id(0) < 2

    def put(k, value):
        columns = pl.ds(pl.multiple_of(where_ref[k] * BLOCK, BLOCK), BLOCK)
        total = base_ref[:, columns].astype(jnp.float32) + value.astype(jnp.float32)
        out_ref[:, columns] = total.astype(jnp.bfloat16)

    for k in range(6):
        put(k, blocks[k][...])
    for k in (6, 7):
        a, b = blocks[2 * k - 6], blocks[2 * k - 5]

        @pl.when(first)
        def _():
            put(k, a[...])

        @pl.when(jnp.logical_not(first))
        def _():
            put(k, b[...])


def add(where, base, whole, halves):
    row = pl.BlockSpec((CHUNK, WIDTH), lambda i, w: (i, 0))
    full = pl.BlockSpec((CHUNK, BLOCK), lambda i, w: (i, 0))
    upper = pl.BlockSpec((CHUNK, BLOCK), lambda i, w: (jnp.minimum(i, 1), 0))
    lower = pl.BlockSpec((CHUNK, BLOCK), lambda i, w: (jnp.maximum(i - 2, 0), 0))
    return pl.pallas_call(
        add_kernel,
        grid_spec=pltpu.PrefetchScalarGridSpec(
            num_scalar_prefetch=1,
            grid=(OWNED // CHUNK,),
            in_specs=[row] + [full] * 6 + [upper, lower] * 2,
            out_specs=row,
        ),
        out_shape=jax.ShapeDtypeStruct((OWNED, WIDTH), jnp.bfloat16),
        compiler_params=pltpu.CompilerParams(vmem_limit_bytes=32 * 2**20),
        name="add",
    )(where, base, *whole, *halves)


def per_device(updated, trainer_base, rollout_base, sync_ids, owner_map):
    values = encode(updated, trainer_base, sync_ids, owner_map)
    values = values.reshape(32, PIECE, BLOCK)
    own = lax.all_to_all(values, "shard", split_axis=0, concat_axis=0, tiled=True)
    own = own.reshape(OWNED, BLOCK)
    below, above, beside = shifted(own, dy=1), shifted(own, dy=-1), shifted(own, dz=1)
    far_a, far_b = shifted(below[:HALF], dy=1), shifted(above[HALF:], dy=-1)
    beside_below, beside_above = shifted(beside, dy=1), shifted(beside, dy=-1)
    beside_a, beside_b = shifted(far_a, dz=1), shifted(far_b, dz=1)
    me = lax.axis_index("rollout")
    y, z = me // 2, me % 2
    at = lambda dy, dz: (y + dy) % 4 * 2 + (z + dz) % 2
    where = jnp.stack(
        [at(0, 0), at(-1, 0), at(1, 0), at(0, 1), at(-1, 1), at(1, 1), at(2, 0), at(2, 1)]
    ).astype(jnp.int32)
    whole = [own, below, above, beside, beside_below, beside_above]
    halves = [far_a, far_b, beside_a, beside_b]
    return add(where, rollout_base[0], whole, halves)[None]


def solution(mesh):
    return jax.shard_map(
        per_device,
        mesh=mesh,
        in_specs=(
            P(None, "shard", "rollout"),
            P(None, "shard", "rollout"),
            P("shard", None, None),
            P(),
            P(),
        ),
        out_specs=P("shard", None, None),
        check_vma=False,
    )
```

time: 215 us -> 83.4 us (0.39)
  waiting for transfers between devices: 109 us -> 31.1 us
  blocking collectives: 50.9 us -> 29.9 us
  local copies, waits for them, and re-layouts: 17.5 us -> 2.15 us
  other arithmetic: 14.2 us -> 0 us
  between operations: 13.5 us -> 0.04 us
  Pallas kernels: 0 us -> 11 us
    all_to_all x1 -> x0, waiting for transfers between devices: 72.6 us -> none  [per_device(): lax.all_to_all(codes, 'shard', split_axis=0, concat_axis=1, tiled=True)]
    all_gather x1 -> x0, waiting for transfers between devices: 36.3 us -> none  [per_device(): lax.all_gather(codes, 'rollout', axis=2, tiled=True)]
    ppermute x0 -> x9, waiting for transfers between devices: none -> 31.1 us  [shifted(): return lax.ppermute(block, 'rollout', pairs)]
    all_gather x1 -> x0, blocking collectives: 23.6 us -> none  [per_device(): lax.all_gather(scales, 'rollout', axis=2, tiled=True)]
    mul x2 -> x0, local copies, waits for them, and re-layouts: 13.3 us -> none  [per_device(): values = values * scales.astype(jnp.float32)[..., None]]
    convert_element_type x3 -> x0, other arithmetic: 12 us -> none  [the longest x1 9.19 us: per_device(): return (rollout_base.astype(jnp.float32) + values).astype(jnp.bfloat16)]
    pallas_call x0 -> x2, Pallas kernels: none -> 11 us  [the longest x1 6.2 us: encode(): pl.pallas_call(encode_kernel, grid_spec=pltpu.PrefetchScalarGridSpec(num_...]
    all_to_all x1 -> x0, starting transfers between devices: 9.49 us -> none  [per_device(): lax.all_to_all(codes, 'shard', split_axis=0, concat_axis=1, tiled=True)]
  transfers between devices with their start and end apart: 2 -> 9, of which waited for: 2 -> 4; matrix products, arithmetic and copies ran while one was open for 6% -> 0% of each run, Pallas kernels for 0% -> 0%
where the time goes in v1:
time: 83.4 us; the launch traced here: 82.8 us
  waiting for transfers between devices  31.1 us (37%)
  blocking collectives  29.9 us (36%)
  Pallas kernels  11 us (13%)
  starting transfers between devices  8.55 us (10%)
  local copies, waits for them, and re-layouts  2.15 us (3%)
    ppermute x9, waiting for transfers between devices, shifted(): return lax.ppermute(block, 'rollout', pairs)  31.1 us
    all_to_all x1, blocking collectives, per_device(): lax.all_to_all(values, 'shard', split_axis=0, concat_axis=0, tiled=True)  29.9 us
    ppermute x9, starting transfers between devices, shifted(): return lax.ppermute(block, 'rollout', pairs)  8.55 us
    pallas_call x1, Pallas kernels, encode(): pl.pallas_call(encode_kernel, grid_spec=pltpu.PrefetchScalarGridSpec(num_...  6.2 us
    pallas_call x1, Pallas kernels, add(): pl.pallas_call(add_kernel, grid_spec=pltpu.PrefetchScalarGridSpec(num_sca...  4.85 us
    unnamed x2, local copies, waits for them, and re-layouts  2.04 us
  transfers between devices with their start and end apart: 9, of which 4 were waited for; matrix products, arithmetic and copies ran while one was open for 0% of the time, Pallas kernels for 0%

profile of v1, /device:TPU:1, one launch (start us, length us, event | category | flops | bytes accessed | tf_op | source)
XLA Modules:
  0.0 82.8 jit_solution(2366049602604538709)
XLA Ops:
  0.0 6.2 %encode.1 = bf16[8,224,128]{2,1,0:T(8,128)(2,1)} custom-call(s32[8]{0:T(128)} %ids_ref.1, s32[8]{0:T(128)} %owner_ref.1, bf16[12,224,128]{2,1,0:T(8,128)(2,1)} %fresh_ref.1, bf16[12,224,128]{2,1,0:T(8,128)(2,1)} %older_ref.1), custom_call_target="tpu_custom_call" | custom-call | tf_op jit(solution)/shard_map/encode/pallas_call | solution.py:46
  6.2 29.9 %all_to_all.5 = bf16[32,56,128]{2,1,0:T(8,128)(2,1)S(1)} all-to-all(bf16[32,56,128]{2,1,0:T(8,128)(2,1)} %bitcast.17), channel_id=1, replica_groups=mesh['rollout'=8,'shard'=32] {'shard'}, dimensions={0} | all-to-all | bytes 917504 | tf_op jit(solution)/shard_map/all_to_all | solution.py:112
  36.1 2.7 %collective-permute-start.1 = (bf16[1792,128]{1,0:T(8,128)(2,1)S(1)}, bf16[1792,128]{1,0:T(8,128)(2,1)S(1)}, u32[]{:S(2)}, u32[]{:S(2)}) collective-permute-start(bf16[1792,128]{1,0:T(8,128)(2,1)S(1)} %bitcast.13), channel_id=1, source_target_pairs={{0,192},{32,224},{64,0},{96,32},{128,64},{160,96},{192,128},{224,1... | collective-permute-start | bytes 1376264 | tf_op jit(solution)/shard_map/ppermute | solution.py:64
  38.9 0.2 collective-permute-start.2
  39.0 0.0 collective-permute-start
  39.0 9.4 %collective-permute-done.1.refs_2_ = bf16[1792,128]{1,0:T(8,128)(2,1)S(1)} collective-permute-done((bf16[1792,128]{1,0:T(8,128)(2,1)S(1)}, bf16[1792,128]{1,0:T(8,128)(2,1)S(1)}, u32[]{:S(2)}, u32[]{:S(2)}) %collective-permute-start.1) | collective-permute-done | bytes 458784 | tf_op jit(solution)/shard_map/ppermute | solution.py:64
  48.4 3.2 %collective-permute-start.6 = (bf16[896,128]{1,0:T(8,128)(2,1)S(1)}, bf16[896,128]{1,0:T(8,128)(2,1)S(1)}, u32[]{:S(2)}, u32[]{:S(2)}) collective-permute-start(bf16[896,128]{1,0:T(8,128)(2,1)S(1)} %slice.9), channel_id=1, source_target_pairs={{0,192},{32,224},{64,0},{96,32},{128,64},{160,96},{192,128},{224,1... | collective-permute-start | bytes 688136 | tf_op jit(solution)/shard_map/ppermute | solution.py:64
  51.6 0.0 collective-permute-done.2.refs_3_
  51.6 0.1 collective-permute-start.4
  51.7 1.4 %collective-permute-start.3 = (bf16[1792,128]{1,0:T(8,128)(2,1)S(1)}, bf16[1792,128]{1,0:T(8,128)(2,1)S(1)}, u32[]{:S(2)}, u32[]{:S(2)}) collective-permute-start(bf16[1792,128]{1,0:T(8,128)(2,1)S(1)} %collective-permute-done.2.refs_3_), channel_id=1, source_target_pairs={{0,64},{32,96},{64,128},{96,160},{128,192},{160,224},{192,0},{224,... | collective-permute-start | bytes 1376264 | tf_op jit(solution)/shard_map/ppermute | solution.py:64
  53.1 0.0 collective-permute-done.refs_1_
  53.1 0.1 collective-permute-start.5
  53.2 3.5 %collective-permute-done.6.refs_7_ = bf16[896,128]{1,0:T(8,128)(2,1)S(1)} collective-permute-done((bf16[896,128]{1,0:T(8,128)(2,1)S(1)}, bf16[896,128]{1,0:T(8,128)(2,1)S(1)}, u32[]{:S(2)}, u32[]{:S(2)}) %collective-permute-start.6) | collective-permute-done | bytes 229408 | tf_op jit(solution)/shard_map/ppermute | solution.py:64
  56.7 0.5 collective-permute-start.8
  57.2 12.6 %collective-permute-done.5.refs_6_ = bf16[896,128]{1,0:T(8,128)(2,1)S(1)} collective-permute-done((bf16[896,128]{1,0:T(8,128)(2,1)S(1)}, bf16[896,128]{1,0:T(8,128)(2,1)S(1)}, u32[]{:S(2)}, u32[]{:S(2)}) %collective-permute-start.5) | collective-permute-done | bytes 229408 | tf_op jit(solution)/shard_map/ppermute | solution.py:64
  69.8 0.5 collective-permute-start.7
  70.2 0.1 stack.35.where_ref
  70.3 0.0 collective-permute-done.4.refs_5_
  70.3 0.0 collective-permute-done.3.refs_4_
  70.3 0.0 collective-permute-done.8.refs_9_
  70.3 5.6 %collective-permute-done.7.refs_8_ = bf16[896,128]{1,0:T(8,128)(2,1)} collective-permute-done((bf16[896,128]{1,0:T(8,128)(2,1)S(1)}, bf16[896,128]{1,0:T(8,128)(2,1)}, u32[]{:S(2)}, u32[]{:S(2)}) %collective-permute-start.7) | collective-permute-done | bytes 229408 | tf_op jit(solution)/shard_map/ppermute | solution.py:64
  75.9 0.0 copy-start
  75.9 2.0 %copy-done = bf16[1,1792,1024]{2,1,0:T(8,128)(2,1)S(1)} copy-done((bf16[1,1792,1024]{2,1,0:T(8,128)(2,1)S(1)}, bf16[1,1792,1024]{2,1,0:T(8,128)(2,1)}, u32[]{:S(2)}) %copy-start) | copy-done | bytes 3670040
  78.0 4.8 %add.95 = bf16[1792,1024]{1,0:T(8,128)(2,1)} custom-call(s32[8]{0:T(128)S(1)} %stack.35.where_ref, bf16[1792,1024]{1,0:T(8,128)(2,1)S(1)} %bitcast.12, bf16[1792,128]{1,0:T(8,128)(2,1)S(1)} %bitcast.16, bf16[1792,128]{1,0:T(8,128)(2,1)S(1)} %collective-permute-done.refs_1_, bf16[1792,128]{1,0:T(8,128)(2,1)S(1)} %collective-permute-done.1.refs_2_, ...), custom_call_target="tpu_custom_call" | custom-call | tf_op jit(solution)/shard_map/add/pallas_call | solution.py:95
  (2 shorter events, 0.0 us)
Async XLA Ops:
  36.1 12.3 %collective-permute-start.1 = (bf16[1792,128]{1,0:T(8,128)(2,1)S(1)}, bf16[1792,128]{1,0:T(8,128)(2,1)S(1)}, u32[]{:S(2)}, u32[]{:S(2)}) collective-permute-start(bf16[1792,128]{1,0:T(8,128)(2,1)S(1)} %bitcast.13), channel_id=1, source_target_pairs={{0,192},{32,224},{64,0},{96,32},{128,64},{160,96},{192,128},{224,1... | collective-permute-start | bytes 1376264 | tf_op jit(solution)/shard_map/ppermute | solution.py:64
  38.9 12.8 %collective-permute-start.2 = (bf16[1792,128]{1,0:T(8,128)(2,1)S(1)}, bf16[1792,128]{1,0:T(8,128)(2,1)S(1)}, u32[]{:S(2)}, u32[]{:S(2)}) collective-permute-start(bf16[1792,128]{1,0:T(8,128)(2,1)S(1)} %bitcast.14), channel_id=1, source_target_pairs={{0,32},{32,0},{64,96},{96,64},{128,160},{160,128},{192,224},{224,1... | collective-permute-start | bytes 1376264 | tf_op jit(solution)/shard_map/ppermute | solution.py:64
  39.0 14.1 %collective-permute-start = (bf16[1792,128]{1,0:T(8,128)(2,1)S(1)}, bf16[1792,128]{1,0:T(8,128)(2,1)S(1)}, u32[]{:S(2)}, u32[]{:S(2)}) collective-permute-start(bf16[1792,128]{1,0:T(8,128)(2,1)S(1)} %bitcast.15), channel_id=1, source_target_pairs={{0,64},{32,96},{64,128},{96,160},{128,192},{160,224},{192,0},{224,... | collective-permute-start | bytes 1376264 | tf_op jit(solution)/shard_map/ppermute | solution.py:64
  48.4 8.3 %collective-permute-start.6 = (bf16[896,128]{1,0:T(8,128)(2,1)S(1)}, bf16[896,128]{1,0:T(8,128)(2,1)S(1)}, u32[]{:S(2)}, u32[]{:S(2)}) collective-permute-start(bf16[896,128]{1,0:T(8,128)(2,1)S(1)} %slice.9), channel_id=1, source_target_pairs={{0,192},{32,224},{64,0},{96,32},{128,64},{160,96},{192,128},{224,1... | collective-permute-start | bytes 688136 | tf_op jit(solution)/shard_map/ppermute | solution.py:64
  51.6 18.7 %collective-permute-start.4 = (bf16[1792,128]{1,0:T(8,128)(2,1)S(1)}, bf16[1792,128]{1,0:T(8,128)(2,1)S(1)}, u32[]{:S(2)}, u32[]{:S(2)}) collective-permute-start(bf16[1792,128]{1,0:T(8,128)(2,1)S(1)} %collective-permute-done.2.refs_3_), channel_id=1, source_target_pairs={{0,192},{32,224},{64,0},{96,32},{128,64},{160,96},{192,128},{224,1... | collective-permute-start | bytes 1376264 | tf_op jit(solution)/shard_map/ppermute | solution.py:64
  51.7 18.6 %collective-permute-start.3 = (bf16[1792,128]{1,0:T(8,128)(2,1)S(1)}, bf16[1792,128]{1,0:T(8,128)(2,1)S(1)}, u32[]{:S(2)}, u32[]{:S(2)}) collective-permute-start(bf16[1792,128]{1,0:T(8,128)(2,1)S(1)} %collective-permute-done.2.refs_3_), channel_id=1, source_target_pairs={{0,64},{32,96},{64,128},{96,160},{128,192},{160,224},{192,0},{224,... | collective-permute-start | bytes 1376264 | tf_op jit(solution)/shard_map/ppermute | solution.py:64
  53.1 16.6 %collective-permute-start.5 = (bf16[896,128]{1,0:T(8,128)(2,1)S(1)}, bf16[896,128]{1,0:T(8,128)(2,1)S(1)}, u32[]{:S(2)}, u32[]{:S(2)}) collective-permute-start(bf16[896,128]{1,0:T(8,128)(2,1)S(1)} %slice.8), channel_id=1, source_target_pairs={{0,64},{32,96},{64,128},{96,160},{128,192},{160,224},{192,0},{224,... | collective-permute-start | bytes 688136 | tf_op jit(solution)/shard_map/ppermute | solution.py:64
  56.7 13.6 %collective-permute-start.8 = (bf16[896,128]{1,0:T(8,128)(2,1)S(1)}, bf16[896,128]{1,0:T(8,128)(2,1)S(1)}, u32[]{:S(2)}, u32[]{:S(2)}) collective-permute-start(bf16[896,128]{1,0:T(8,128)(2,1)S(1)} %collective-permute-done.6.refs_7_), channel_id=1, source_target_pairs={{0,32},{32,0},{64,96},{96,64},{128,160},{160,128},{192,224},{224,1... | collective-permute-start | bytes 688136 | tf_op jit(solution)/shard_map/ppermute | solution.py:64
  69.8 6.2 %collective-permute-start.7 = (bf16[896,128]{1,0:T(8,128)(2,1)S(1)}, bf16[896,128]{1,0:T(8,128)(2,1)}, u32[]{:S(2)}, u32[]{:S(2)}) collective-permute-start(bf16[896,128]{1,0:T(8,128)(2,1)S(1)} %collective-permute-done.5.refs_6_), channel_id=1, source_target_pairs={{0,32},{32,0},{64,96},{96,64},{128,160},{160,128},{192,224},{224,1... | collective-permute-start | bytes 688136 | tf_op jit(solution)/shard_map/ppermute | solution.py:64
  75.9 2.0 %copy-start = (bf16[1,1792,1024]{2,1,0:T(8,128)(2,1)S(1)}, bf16[1,1792,1024]{2,1,0:T(8,128)(2,1)}, u32[]{:S(2)}) copy-start(bf16[1,1792,1024]{2,1,0:T(8,128)(2,1)} %param.7) | copy-start | bytes 11010052

commit v2 on v1

v2 whole, which is shorter than its diff:
```python
import jax
import jax.numpy as jnp
from jax import lax
from jax.experimental import pallas as pl
from jax.experimental.pallas import tpu as pltpu
from jax.sharding import PartitionSpec as P

EXPERTS = 8
ROWS = 224
BLOCK = 128
PIECE = 56
OWNED = 1792
WIDTH = 1024
CHUNK = 448
HALF = OWNED // 2
FIRST = 4


def floor_power(magnitude):
    spread = magnitude * (2.0**23 + 1.0)
    power = spread - (spread - magnitude)
    return jnp.where(power > magnitude, power * 0.5, power)


def quantize(fresh, older):
    delta = fresh.astype(jnp.float32) - older.astype(jnp.float32)
    magnitude = jnp.abs(delta)
    largest = jnp.max(magnitude, axis=-1, keepdims=True)
    power = floor_power(largest)
    scale = jnp.where(largest > 1.75 * power, power * 2.0**-7, power * 2.0**-8)
    scale = jnp.maximum(scale, 2.0**-24)
    binade = jnp.maximum(floor_power(magnitude), scale * 2.0**-6)
    shift = binade * (1.5 * 2.0**20)
    rounded = (magnitude + shift) - shift
    tie = (magnitude - rounded) >= binade * 2.0**-4
    rounded = jnp.where(tie, rounded + binade * 2.0**-3, rounded)
    return jnp.where(delta < 0.0, -rounded, rounded)


def encode_kernel(ids_ref, owner_ref, fresh_hbm, older_hbm, value_ref, fresh_ref, older_ref, sems):
    def copies(e):
        slot = ids_ref[e]
        return (
            pltpu.make_async_copy(fresh_hbm.at[slot], fresh_ref.at[e], sems.at[0, e]),
            pltpu.make_async_copy(older_hbm.at[slot], older_ref.at[e], sems.at[1, e]),
        )

    for e in range(EXPERTS):
        for copy in copies(e):
            copy.start()

    @pl.loop(0, EXPERTS)
    def _(e):
        for copy in copies(e):
            copy.wait()
        value_ref[owner_ref[e]] = quantize(fresh_ref[e], older_ref[e]).astype(jnp.bfloat16)


def encode(updated, trainer_base, sync_ids, owner_map):
    return pl.pallas_call(
        encode_kernel,
        in_specs=[pl.BlockSpec(memory_space=pltpu.SMEM)] * 2 + [pl.BlockSpec(memory_space=pl.ANY)] * 2,
        out_specs=pl.BlockSpec(memory_space=pltpu.VMEM),
        out_shape=jax.ShapeDtypeStruct((EXPERTS, ROWS, BLOCK), jnp.bfloat16),
        scratch_shapes=[
            pltpu.VMEM((EXPERTS, ROWS, BLOCK), jnp.bfloat16),
            pltpu.VMEM((EXPERTS, ROWS, BLOCK), jnp.bfloat16),
            pltpu.SemaphoreType.DMA((2, EXPERTS)),
        ],
        name="encode",
    )(sync_ids, owner_map, updated, trainer_base)


def shifted(block, dy=0, dz=0):
    pairs = []
    for y in range(4):
        for z in range(2):
            pairs.append((y * 2 + z, (y + dy) % 4 * 2 + (z + dz) % 2))
    return lax.ppermute(block, "rollout", pairs)


def add_kernel(where_ref, base_ref, *refs):
    out_ref, rest_ref = refs[-2:]
    step = pl.program_id(0)
    rows = pl.ds(pl.multiple_of(step % 2 * CHUNK, CHUNK), CHUNK)

    def columns(k):
        return pl.ds(pl.multiple_of(where_ref[k] * BLOCK, BLOCK), BLOCK)

    for k in range(FIRST, 8):
        rest_ref[k - FIRST] = base_ref[:, columns(k)]
    for half in range(2):

        @pl.when(step // 2 == half)
        def _():
            for k in range(FIRST):
                out_ref[:, columns(k)] = base_ref[:, columns(k)] + refs[2 * k + half][rows, :]


def add(where, base, parts):
    band = pl.BlockSpec((CHUNK, WIDTH), lambda i, w: (i, 0))
    return pl.pallas_call(
        add_kernel,
        grid_spec=pltpu.PrefetchScalarGridSpec(
            num_scalar_prefetch=1,
            grid=(OWNED // CHUNK,),
            in_specs=[band] + [pl.BlockSpec(memory_space=pltpu.VMEM)] * len(parts),
            out_specs=[band, pl.BlockSpec((8 - FIRST, CHUNK, BLOCK), lambda i, w: (0, i, 0))],
        ),
        out_shape=[
            jax.ShapeDtypeStruct((OWNED, WIDTH), jnp.bfloat16),
            jax.ShapeDtypeStruct((8 - FIRST, OWNED, BLOCK), jnp.bfloat16),
        ],
        compiler_params=pltpu.CompilerParams(vmem_limit_bytes=12 * 2**20),
        cost_estimate=pl.CostEstimate(flops=OWNED * WIDTH, bytes_accessed=6 * OWNED * WIDTH, transcendentals=0),
        name="add",
    )(where, base, *parts)


def finish_kernel(where_ref, rest_ref, *refs):
    parts, (out_hbm, total_ref, sems) = refs[:-4], refs[-3:]
    copies = []
    for k in range(FIRST, 8):
        column = pl.ds(pl.multiple_of(where_ref[k] * BLOCK, BLOCK), BLOCK)
        n = k - FIRST
        for half in range(2):
            rows = pl.ds(half * HALF, HALF)
            total_ref[n, rows, :] = rest_ref[n, rows, :] + parts[2 * n + half][...]
            copies.append(pltpu.make_async_copy(total_ref.at[n, rows], out_hbm.at[rows, column], sems.at[n, half]))
            copies[-1].start()
    for copy in copies:
        copy.wait()


def finish(where, rest, parts, made):
    whole = pl.BlockSpec(memory_space=pltpu.VMEM)
    return pl.pallas_call(
        finish_kernel,
        in_specs=[pl.BlockSpec(memory_space=pltpu.SMEM), whole] + [whole] * len(parts) + [pl.BlockSpec(memory_space=pl.ANY)],
        out_specs=pl.BlockSpec(memory_space=pl.ANY),
        out_shape=jax.ShapeDtypeStruct((OWNED, WIDTH), jnp.bfloat16),
        scratch_shapes=[pltpu.VMEM((8 - FIRST, OWNED, BLOCK), jnp.bfloat16), pltpu.SemaphoreType.DMA((8 - FIRST, 2))],
        input_output_aliases={2 + len(parts): 0},
        compiler_params=pltpu.CompilerParams(vmem_limit_bytes=8 * 2**20),
        name="finish",
    )(where, rest, *parts, made)


def gather(own):
    own_a, own_b = own[:HALF], own[HALF:]
    beside_a, beside_b = shifted(own_a, dz=1), shifted(own_b, dz=1)
    below_a, above_b = shifted(own_a, dy=1), shifted(own_b, dy=-1)
    below_b, above_a = shifted(own_b, dy=1), shifted(own_a, dy=-1)
    bb_a, ba_b = shifted(beside_a, dy=1), shifted(beside_b, dy=-1)
    far_a, far_b = shifted(below_a, dy=1), shifted(above_b, dy=-1)
    bb_b, ba_a = shifted(below_b, dz=1), shifted(above_a, dz=1)
    fz_a, fz_b = shifted(bb_a, dy=1), shifted(ba_b, dy=-1)
    early = [own_a, own_b, below_a, below_b, above_a, above_b, beside_a, beside_b]
    return early, [far_a, far_b, bb_a, bb_b, ba_a, ba_b, fz_a, fz_b]


def per_device(updated, trainer_base, rollout_base, sync_ids, owner_map):
    values = encode(updated, trainer_base, sync_ids, owner_map).reshape(32, PIECE, BLOCK)
    own = lax.all_to_all(values, "shard", split_axis=0, concat_axis=0, tiled=True)
    early, late = gather(own.reshape(OWNED, BLOCK))
    me = lax.axis_index("rollout")
    y, z = me // 2, me % 2
    moves = [(0, 0), (-1, 0), (1, 0), (0, 1), (2, 0), (-1, 1), (1, 1), (2, 1)]
    where = jnp.stack([(y + dy) % 4 * 2 + (z + dz) % 2 for dy, dz in moves]).astype(jnp.int32)
    made, rest = add(where, rollout_base[0], early)
    return finish(where, rest, late, made)[None]


def solution(mesh):
    return jax.shard_map(
        per_device,
        mesh=mesh,
        in_specs=(
            P(None, "shard", "rollout"),
            P(None, "shard", "rollout"),
            P("shard", None, None),
            P(),
            P(),
        ),
        out_specs=P("shard", None, None),
        check_vma=False,
    )
```

time: 83.4 us -> 67.7 us (0.81)
  waiting for transfers between devices: 31.1 us -> 7.73 us
  starting transfers between devices: 8.55 us -> 18 us
  Pallas kernels: 11 us -> 9.54 us
    ppermute x9 -> x14, waiting for transfers between devices: 31.1 us -> 7.73 us  [shifted(): return lax.ppermute(block, 'rollout', pairs)]
    ppermute x9 -> x14, starting transfers between devices: 8.55 us -> 18 us  [shifted(): return lax.ppermute(block, 'rollout', pairs)]
    pallas_call x1, Pallas kernels: 4.85 us -> 3.27 us  [add(): pl.pallas_call(add_kernel, grid_spec=pltpu.PrefetchScalarGridSpec(num_sca...]
    pallas_call x1 -> x2, Pallas kernels: 6.2 us -> 6.27 us  [the longest x1 3.98 us: encode(): pl.pallas_call(encode_kernel, in_specs=[pl.BlockSpec(memory_space=pltpu.S...]
  transfers between devices with their start and end apart: 9 -> 14, of which waited for: 4 -> 5; matrix products, arithmetic and copies ran while one was open for 0% -> 0% of each run, Pallas kernels for 0% -> 5%
where the time goes in v2:
time: 67.7 us; the launch traced here: 67.4 us
  blocking collectives  29.9 us (44%)
  starting transfers between devices  18 us (27%)
  Pallas kernels  9.54 us (14%)
  waiting for transfers between devices  7.73 us (11%)
  local copies, waits for them, and re-layouts  2.16 us (3%)
    all_to_all x1, blocking collectives, per_device(): lax.all_to_all(values, 'shard', split_axis=0, concat_axis=0, tiled=True)  29.9 us
    ppermute x14, starting transfers between devices, shifted(): return lax.ppermute(block, 'rollout', pairs)  18 us
    ppermute x14, waiting for transfers between devices, shifted(): return lax.ppermute(block, 'rollout', pairs)  7.73 us
    pallas_call x1, Pallas kernels, encode(): pl.pallas_call(encode_kernel, in_specs=[pl.BlockSpec(memory_space=pltpu.S...  3.98 us
    pallas_call x1, Pallas kernels, add(): pl.pallas_call(add_kernel, grid_spec=pltpu.PrefetchScalarGridSpec(num_sca...  3.27 us
    pallas_call x1, Pallas kernels, finish(): pl.pallas_call(finish_kernel, in_specs=[pl.BlockSpec(memory_space=pltpu.S...  2.29 us
    unnamed x2, local copies, waits for them, and re-layouts  2.04 us
  transfers between devices with their start and end apart: 14, of which 5 were waited for; matrix products, arithmetic and copies ran while one was open for 0% of the time, Pallas kernels for 5%

profile of v2, /device:TPU:1, one launch (start us, length us, event | category | flops | bytes accessed | tf_op | source)
XLA Modules:
  0.0 67.4 jit_solution(14713274924355669237)
XLA Ops:
  0.0 4.0 %encode.1 = bf16[8,224,128]{2,1,0:T(8,128)(2,1)} custom-call(s32[8]{0:T(128)} %ids_ref.1, s32[8]{0:T(128)} %owner_ref.1, bf16[12,224,128]{2,1,0:T(8,128)(2,1)} %fresh_hbm.1, bf16[12,224,128]{2,1,0:T(8,128)(2,1)} %older_hbm.1), custom_call_target="tpu_custom_call" | custom-call | tf_op jit(solution)/shard_map/encode/pallas_call | solution.py:60
  4.0 29.9 %all_to_all.5 = bf16[32,56,128]{2,1,0:T(8,128)(2,1)S(1)} all-to-all(bf16[32,56,128]{2,1,0:T(8,128)(2,1)} %bitcast.22), channel_id=1, replica_groups=mesh['rollout'=8,'shard'=32] {'shard'}, dimensions={0} | all-to-all | bytes 917504 | tf_op jit(solution)/shard_map/all_to_all | solution.py:164
  34.0 0.2 collective-permute-start.4
  34.2 2.7 %collective-permute-start.2 = (bf16[896,128]{1,0:T(8,128)(2,1)S(1)}, bf16[896,128]{1,0:T(8,128)(2,1)S(1)}, u32[]{:S(2)}, u32[]{:S(2)}) collective-permute-start(bf16[896,128]{1,0:T(8,128)(2,1)S(1)} %bitcast.19), channel_id=1, source_target_pairs={{0,192},{32,224},{64,0},{96,32},{128,64},{160,96},{192,128},{224,1... | collective-permute-start | bytes 688136 | tf_op jit(solution)/shard_map/ppermute | solution.py:79
  36.9 0.0 collective-permute-start
  36.9 1.3 %collective-permute-start.5 = (bf16[896,128]{1,0:T(8,128)(2,1)S(1)}, bf16[896,128]{1,0:T(8,128)(2,1)S(1)}, u32[]{:S(2)}, u32[]{:S(2)}) collective-permute-start(bf16[896,128]{1,0:T(8,128)(2,1)S(1)} %bitcast.14), channel_id=1, source_target_pairs={{0,32},{32,0},{64,96},{96,64},{128,160},{160,128},{192,224},{224,1... | collective-permute-start | bytes 688136 | tf_op jit(solution)/shard_map/ppermute | solution.py:79
  38.3 2.7 %collective-permute-start.3 = (bf16[896,128]{1,0:T(8,128)(2,1)S(1)}, bf16[896,128]{1,0:T(8,128)(2,1)S(1)}, u32[]{:S(2)}, u32[]{:S(2)}) collective-permute-start(bf16[896,128]{1,0:T(8,128)(2,1)S(1)} %bitcast.15), channel_id=1, source_target_pairs={{0,192},{32,224},{64,0},{96,32},{128,64},{160,96},{192,128},{224,1... | collective-permute-start | bytes 688136 | tf_op jit(solution)/shard_map/ppermute | solution.py:79
  40.9 0.7 %collective-permute-done.4.refs_6_ = bf16[896,128]{1,0:T(8,128)(2,1)S(1)} collective-permute-done((bf16[896,128]{1,0:T(8,128)(2,1)S(1)}, bf16[896,128]{1,0:T(8,128)(2,1)S(1)}, u32[]{:S(2)}, u32[]{:S(2)}) %collective-permute-start.4) | collective-permute-done | bytes 229408 | tf_op jit(solution)/shard_map/ppermute | solution.py:79
  41.6 1.3 %collective-permute-start.1 = (bf16[896,128]{1,0:T(8,128)(2,1)S(1)}, bf16[896,128]{1,0:T(8,128)(2,1)S(1)}, u32[]{:S(2)}, u32[]{:S(2)}) collective-permute-start(bf16[896,128]{1,0:T(8,128)(2,1)S(1)} %bitcast.16), channel_id=1, source_target_pairs={{0,64},{32,96},{64,128},{96,160},{128,192},{160,224},{192,0},{224,... | collective-permute-start | bytes 688136 | tf_op jit(solution)/shard_map/ppermute | solution.py:79
  42.9 0.0 collective-permute-done.2.refs_4_
  42.9 1.3 %collective-permute-start.8 = (bf16[896,128]{1,0:T(8,128)(2,1)S(1)}, bf16[896,128]{1,0:T(8,128)(2,1)S(1)}, u32[]{:S(2)}, u32[]{:S(2)}) collective-permute-start(bf16[896,128]{1,0:T(8,128)(2,1)S(1)} %collective-permute-done.4.refs_6_), channel_id=1, source_target_pairs={{0,64},{32,96},{64,128},{96,160},{128,192},{160,224},{192,0},{224,... | collective-permute-start | bytes 688136 | tf_op jit(solution)/shard_map/ppermute | solution.py:79
  44.2 1.2 %collective-permute-done.refs_2_ = bf16[896,128]{1,0:T(8,128)(2,1)S(1)} collective-permute-done((bf16[896,128]{1,0:T(8,128)(2,1)S(1)}, bf16[896,128]{1,0:T(8,128)(2,1)S(1)}, u32[]{:S(2)}, u32[]{:S(2)}) %collective-permute-start) | collective-permute-done | bytes 229408 | tf_op jit(solution)/shard_map/ppermute | solution.py:79
  45.4 1.7 %collective-permute-start.10 = (bf16[896,128]{1,0:T(8,128)(2,1)S(1)}, bf16[896,128]{1,0:T(8,128)(2,1)S(1)}, u32[]{:S(2)}, u32[]{:S(2)}) collective-permute-start(bf16[896,128]{1,0:T(8,128)(2,1)S(1)} %collective-permute-done.2.refs_4_), channel_id=1, source_target_pairs={{0,32},{32,0},{64,96},{96,64},{128,160},{160,128},{192,224},{224,1... | collective-permute-start | bytes 688136 | tf_op jit(solution)/shard_map/ppermute | solution.py:79
  47.1 0.0 collective-permute-done.5.refs_7_
  47.1 1.5 %collective-permute-start.11 = (bf16[896,128]{1,0:T(8,128)(2,1)S(1)}, bf16[896,128]{1,0:T(8,128)(2,1)S(1)}, u32[]{:S(2)}, u32[]{:S(2)}) collective-permute-start(bf16[896,128]{1,0:T(8,128)(2,1)S(1)} %collective-permute-done.5.refs_7_), channel_id=1, source_target_pairs={{0,192},{32,224},{64,0},{96,32},{128,64},{160,96},{192,128},{224,1... | collective-permute-start | bytes 688136 | tf_op jit(solution)/shard_map/ppermute | solution.py:79
  48.5 0.0 collective-permute-done.3.refs_5_
  48.6 0.0 collective-permute-start.6
  48.6 2.0 %collective-permute-done.1.refs_3_ = bf16[896,128]{1,0:T(8,128)(2,1)S(1)} collective-permute-done((bf16[896,128]{1,0:T(8,128)(2,1)S(1)}, bf16[896,128]{1,0:T(8,128)(2,1)S(1)}, u32[]{:S(2)}, u32[]{:S(2)}) %collective-permute-start.1) | collective-permute-done | bytes 229408 | tf_op jit(solution)/shard_map/ppermute | solution.py:79
  50.5 1.2 %collective-permute-start.7 = (bf16[896,128]{1,0:T(8,128)(2,1)S(1)}, bf16[896,128]{1,0:T(8,128)(2,1)S(1)}, u32[]{:S(2)}, u32[]{:S(2)}) collective-permute-start(bf16[896,128]{1,0:T(8,128)(2,1)S(1)} %collective-permute-done.3.refs_5_), channel_id=1, source_target_pairs={{0,192},{32,224},{64,0},{96,32},{128,64},{160,96},{192,128},{224,1... | collective-permute-start | bytes 688136 | tf_op jit(solution)/shard_map/ppermute | solution.py:79
  51.7 3.8 %collective-permute-done.8.refs_2_ = bf16[896,128]{1,0:T(8,128)(2,1)S(1)} collective-permute-done((bf16[896,128]{1,0:T(8,128)(2,1)S(1)}, bf16[896,128]{1,0:T(8,128)(2,1)S(1)}, u32[]{:S(2)}, u32[]{:S(2)}) %collective-permute-start.8) | collective-permute-done | bytes 229408 | tf_op jit(solution)/shard_map/ppermute | solution.py:79
  55.5 1.5 %collective-permute-start.9 = (bf16[896,128]{1,0:T(8,128)(2,1)S(1)}, bf16[896,128]{1,0:T(8,128)(2,1)S(1)}, u32[]{:S(2)}, u32[]{:S(2)}) collective-permute-start(bf16[896,128]{1,0:T(8,128)(2,1)S(1)} %collective-permute-done.1.refs_3_), channel_id=1, source_target_pairs={{0,32},{32,0},{64,96},{96,64},{128,160},{160,128},{192,224},{224,1... | collective-permute-start | bytes 688136 | tf_op jit(solution)/shard_map/ppermute | solution.py:79
  56.9 0.0 collective-permute-done.10.refs_4_
  56.9 0.0 collective-permute-start.12
  56.9 0.0 collective-permute-done.11.refs_5_
  56.9 2.7 %collective-permute-start.13 = (bf16[896,128]{1,0:T(8,128)(2,1)S(1)}, bf16[896,128]{1,0:T(8,128)(2,1)}, u32[]{:S(2)}, u32[]{:S(2)}) collective-permute-start(bf16[896,128]{1,0:T(8,128)(2,1)S(1)} %collective-permute-done.11.refs_5_), channel_id=1, source_target_pairs={{0,192},{32,224},{64,0},{96,32},{128,64},{160,96},{192,128},{224,1... | collective-permute-start | bytes 688136 | tf_op jit(solution)/shard_map/ppermute | solution.py:79
  59.6 0.1 stack.35.where_ref
  59.7 0.0 copy-start
  59.7 2.0 %copy-done = bf16[1,1792,1024]{2,1,0:T(8,128)(2,1)S(1)} copy-done((bf16[1,1792,1024]{2,1,0:T(8,128)(2,1)S(1)}, bf16[1,1792,1024]{2,1,0:T(8,128)(2,1)}, u32[]{:S(2)}) %copy-start) | copy-done | bytes 3670040
  61.7 3.3 %add.95 = (bf16[1792,1024]{1,0:T(8,128)(2,1)}, bf16[4,1792,128]{2,1,0:T(8,128)(2,1)S(1)}) custom-call(s32[8]{0:T(128)S(1)} %stack.35.where_ref, bf16[1792,1024]{1,0:T(8,128)(2,1)S(1)} %bitcast.13, bf16[896,128]{1,0:T(8,128)(2,1)S(1)} %bitcast.21, bf16[896,128]{1,0:T(8,128)(2,1)S(1)} %bitcast.17, bf16[896,128]{1,0:T(8,128)(2,1)S(1)} %collective-permute-done.refs_2_, ...), custom_call_target="tpu_custom_call" | custom-call | flops 1835008 | bytes 11010048 | tf_op jit(solution)/shard_map/add/pallas_call | solution.py:102
  65.0 0.0 collective-permute-done.6.refs_0_
  65.0 0.0 collective-permute-done.7.refs_1_
  65.0 0.0 collective-permute-done.9.refs_3_
  65.0 0.1 collective-permute-done.12.refs_6_
  65.1 0.0 collective-permute-done.13.refs_7_
  65.1 2.3 %finish.1 = bf16[1792,1024]{1,0:T(8,128)(2,1)} custom-call(s32[8]{0:T(128)S(1)} %stack.35.where_ref, bf16[4,1792,128]{2,1,0:T(8,128)(2,1)S(1)} %get-tuple-element.7.rest_ref, bf16[896,128]{1,0:T(8,128)(2,1)S(1)} %collective-permute-done.6.refs_0_, bf16[896,128]{1,0:T(8,128)(2,1)S(1)} %collective-permute-done.7.refs_1_, ...), custom_call_target="tpu_custom_call", output_to_operand_aliasing={{}: (10, {})} | custom-call | tf_op jit(solution)/shard_map/finish/pallas_call | solution.py:137
  (1 shorter events, 0.0 us)
Async XLA Ops:
  34.0 7.7 %collective-permute-start.4 = (bf16[896,128]{1,0:T(8,128)(2,1)S(1)}, bf16[896,128]{1,0:T(8,128)(2,1)S(1)}, u32[]{:S(2)}, u32[]{:S(2)}) collective-permute-start(bf16[896,128]{1,0:T(8,128)(2,1)S(1)} %bitcast.18), channel_id=1, source_target_pairs={{0,32},{32,0},{64,96},{96,64},{128,160},{160,128},{192,224},{224,1... | collective-permute-start | bytes 688136 | tf_op jit(solution)/shard_map/ppermute | solution.py:79
  34.2 8.7 %collective-permute-start.2 = (bf16[896,128]{1,0:T(8,128)(2,1)S(1)}, bf16[896,128]{1,0:T(8,128)(2,1)S(1)}, u32[]{:S(2)}, u32[]{:S(2)}) collective-permute-start(bf16[896,128]{1,0:T(8,128)(2,1)S(1)} %bitcast.19), channel_id=1, source_target_pairs={{0,192},{32,224},{64,0},{96,32},{128,64},{160,96},{192,128},{224,1... | collective-permute-start | bytes 688136 | tf_op jit(solution)/shard_map/ppermute | solution.py:79
  36.9 8.5 %collective-permute-start = (bf16[896,128]{1,0:T(8,128)(2,1)S(1)}, bf16[896,128]{1,0:T(8,128)(2,1)S(1)}, u32[]{:S(2)}, u32[]{:S(2)}) collective-permute-start(bf16[896,128]{1,0:T(8,128)(2,1)S(1)} %bitcast.20), channel_id=1, source_target_pairs={{0,64},{32,96},{64,128},{96,160},{128,192},{160,224},{192,0},{224,... | collective-permute-start | bytes 688136 | tf_op jit(solution)/shard_map/ppermute | solution.py:79
  36.9 10.1 %collective-permute-start.5 = (bf16[896,128]{1,0:T(8,128)(2,1)S(1)}, bf16[896,128]{1,0:T(8,128)(2,1)S(1)}, u32[]{:S(2)}, u32[]{:S(2)}) collective-permute-start(bf16[896,128]{1,0:T(8,128)(2,1)S(1)} %bitcast.14), channel_id=1, source_target_pairs={{0,32},{32,0},{64,96},{96,64},{128,160},{160,128},{192,224},{224,1... | collective-permute-start | bytes 688136 | tf_op jit(solution)/shard_map/ppermute | solution.py:79
  38.3 10.3 %collective-permute-start.3 = (bf16[896,128]{1,0:T(8,128)(2,1)S(1)}, bf16[896,128]{1,0:T(8,128)(2,1)S(1)}, u32[]{:S(2)}, u32[]{:S(2)}) collective-permute-start(bf16[896,128]{1,0:T(8,128)(2,1)S(1)} %bitcast.15), channel_id=1, source_target_pairs={{0,192},{32,224},{64,0},{96,32},{128,64},{160,96},{192,128},{224,1... | collective-permute-start | bytes 688136 | tf_op jit(solution)/shard_map/ppermute | solution.py:79
  41.6 8.9 %collective-permute-start.1 = (bf16[896,128]{1,0:T(8,128)(2,1)S(1)}, bf16[896,128]{1,0:T(8,128)(2,1)S(1)}, u32[]{:S(2)}, u32[]{:S(2)}) collective-permute-start(bf16[896,128]{1,0:T(8,128)(2,1)S(1)} %bitcast.16), channel_id=1, source_target_pairs={{0,64},{32,96},{64,128},{96,160},{128,192},{160,224},{192,0},{224,... | collective-permute-start | bytes 688136 | tf_op jit(solution)/shard_map/ppermute | solution.py:79
  42.9 12.5 %collective-permute-start.8 = (bf16[896,128]{1,0:T(8,128)(2,1)S(1)}, bf16[896,128]{1,0:T(8,128)(2,1)S(1)}, u32[]{:S(2)}, u32[]{:S(2)}) collective-permute-start(bf16[896,128]{1,0:T(8,128)(2,1)S(1)} %collective-permute-done.4.refs_6_), channel_id=1, source_target_pairs={{0,64},{32,96},{64,128},{96,160},{128,192},{160,224},{192,0},{224,... | collective-permute-start | bytes 688136 | tf_op jit(solution)/shard_map/ppermute | solution.py:79
  45.4 11.5 %collective-permute-start.10 = (bf16[896,128]{1,0:T(8,128)(2,1)S(1)}, bf16[896,128]{1,0:T(8,128)(2,1)S(1)}, u32[]{:S(2)}, u32[]{:S(2)}) collective-permute-start(bf16[896,128]{1,0:T(8,128)(2,1)S(1)} %collective-permute-done.2.refs_4_), channel_id=1, source_target_pairs={{0,32},{32,0},{64,96},{96,64},{128,160},{160,128},{192,224},{224,1... | collective-permute-start | bytes 688136 | tf_op jit(solution)/shard_map/ppermute | solution.py:79
  47.1 9.8 %collective-permute-start.11 = (bf16[896,128]{1,0:T(8,128)(2,1)S(1)}, bf16[896,128]{1,0:T(8,128)(2,1)S(1)}, u32[]{:S(2)}, u32[]{:S(2)}) collective-permute-start(bf16[896,128]{1,0:T(8,128)(2,1)S(1)} %collective-permute-done.5.refs_7_), channel_id=1, source_target_pairs={{0,192},{32,224},{64,0},{96,32},{128,64},{160,96},{192,128},{224,1... | collective-permute-start | bytes 688136 | tf_op jit(solution)/shard_map/ppermute | solution.py:79
  48.6 16.5 %collective-permute-start.6 = (bf16[896,128]{1,0:T(8,128)(2,1)S(1)}, bf16[896,128]{1,0:T(8,128)(2,1)S(1)}, u32[]{:S(2)}, u32[]{:S(2)}) collective-permute-start(bf16[896,128]{1,0:T(8,128)(2,1)S(1)} %collective-permute-done.refs_2_), channel_id=1, source_target_pairs={{0,64},{32,96},{64,128},{96,160},{128,192},{160,224},{192,0},{224,... | collective-permute-start | bytes 688136 | tf_op jit(solution)/shard_map/ppermute | solution.py:79
  50.5 14.5 %collective-permute-start.7 = (bf16[896,128]{1,0:T(8,128)(2,1)S(1)}, bf16[896,128]{1,0:T(8,128)(2,1)S(1)}, u32[]{:S(2)}, u32[]{:S(2)}) collective-permute-start(bf16[896,128]{1,0:T(8,128)(2,1)S(1)} %collective-permute-done.3.refs_5_), channel_id=1, source_target_pairs={{0,192},{32,224},{64,0},{96,32},{128,64},{160,96},{192,128},{224,1... | collective-permute-start | bytes 688136 | tf_op jit(solution)/shard_map/ppermute | solution.py:79
  55.5 9.6 %collective-permute-start.9 = (bf16[896,128]{1,0:T(8,128)(2,1)S(1)}, bf16[896,128]{1,0:T(8,128)(2,1)S(1)}, u32[]{:S(2)}, u32[]{:S(2)}) collective-permute-start(bf16[896,128]{1,0:T(8,128)(2,1)S(1)} %collective-permute-done.1.refs_3_), channel_id=1, source_target_pairs={{0,32},{32,0},{64,96},{96,64},{128,160},{160,128},{192,224},{224,1... | collective-permute-start | bytes 688136 | tf_op jit(solution)/shard_map/ppermute | solution.py:79
  56.9 8.2 %collective-permute-start.12 = (bf16[896,128]{1,0:T(8,128)(2,1)S(1)}, bf16[896,128]{1,0:T(8,128)(2,1)S(1)}, u32[]{:S(2)}, u32[]{:S(2)}) collective-permute-start(bf16[896,128]{1,0:T(8,128)(2,1)S(1)} %collective-permute-done.8.refs_2_), channel_id=1, source_target_pairs={{0,64},{32,96},{64,128},{96,160},{128,192},{160,224},{192,0},{224,... | collective-permute-start | bytes 688136 | tf_op jit(solution)/shard_map/ppermute | solution.py:79
  56.9 8.2 %collective-permute-start.13 = (bf16[896,128]{1,0:T(8,128)(2,1)S(1)}, bf16[896,128]{1,0:T(8,128)(2,1)}, u32[]{:S(2)}, u32[]{:S(2)}) collective-permute-start(bf16[896,128]{1,0:T(8,128)(2,1)S(1)} %collective-permute-done.11.refs_5_), channel_id=1, source_target_pairs={{0,192},{32,224},{64,0},{96,32},{128,64},{160,96},{192,128},{224,1... | collective-permute-start | bytes 688136 | tf_op jit(solution)/shard_map/ppermute | solution.py:79
  59.7 2.0 %copy-start = (bf16[1,1792,1024]{2,1,0:T(8,128)(2,1)S(1)}, bf16[1,1792,1024]{2,1,0:T(8,128)(2,1)}, u32[]{:S(2)}) copy-start(bf16[1,1792,1024]{2,1,0:T(8,128)(2,1)} %param.7) | copy-start | bytes 11010052

commit v3 on v2

v3 whole, which is shorter than its diff:
```python
import functools

import jax
import jax.numpy as jnp
from jax import lax
from jax.experimental import pallas as pl
from jax.experimental.pallas import tpu as pltpu
from jax.sharding import PartitionSpec as P

EXPERTS = 8
ROWS = 224
BLOCK = 128
PIECE = 56
OWNED = 1792
WIDTH = 1024
BAND = 448
SPLIT = 896
FIRST = 4
MOVES = [(0, 0), (-1, 0), (1, 0), (0, 1), (2, 0), (-1, 1), (1, 1), (2, 1)]


def floor_power(magnitude):
    spread = magnitude * (2.0**23 + 1.0)
    power = spread - (spread - magnitude)
    return jnp.where(power > magnitude, power * 0.5, power)


def quantize(fresh, older):
    delta = fresh.astype(jnp.float32) - older.astype(jnp.float32)
    magnitude = jnp.abs(delta)
    largest = jnp.max(magnitude, axis=-1, keepdims=True)
    power = floor_power(largest)
    scale = jnp.where(largest > 1.75 * power, power * 2.0**-7, power * 2.0**-8)
    scale = jnp.maximum(scale, 2.0**-24)
    binade = jnp.maximum(floor_power(magnitude), scale * 2.0**-6)
    shift = binade * (1.5 * 2.0**20)
    rounded = (magnitude + shift) - shift
    tie = (magnitude - rounded) >= binade * 2.0**-4
    rounded = jnp.where(tie, rounded + binade * 2.0**-3, rounded)
    return jnp.where(delta < 0.0, -rounded, rounded)


def encode_kernel(ids_hbm, owner_hbm, fresh_hbm, older_hbm, value_ref, ids_ref, owner_ref, fresh_ref, older_ref, sems, few):
    ids = pltpu.make_async_copy(ids_hbm, ids_ref, few.at[0])
    owner = pltpu.make_async_copy(owner_hbm, owner_ref, few.at[1])
    ids.start()
    owner.start()
    slots = fresh_ref.shape[0]
    copies = []
    for slot in range(slots):
        fresh = pltpu.make_async_copy(fresh_hbm.at[slot], fresh_ref.at[slot], sems.at[0, slot])
        older = pltpu.make_async_copy(older_hbm.at[slot], older_ref.at[slot], sems.at[1, slot])
        fresh.start()
        older.start()
        copies += [fresh, older]
    ids.wait()
    owner.wait()
    for copy in copies:
        copy.wait()

    @pl.loop(0, EXPERTS)
    def _(e):
        slot = ids_ref[e]
        value_ref[owner_ref[e]] = quantize(fresh_ref[slot], older_ref[slot]).astype(jnp.bfloat16)


def encode(updated, trainer_base, sync_ids, owner_map):
    return pl.pallas_call(
        encode_kernel,
        in_specs=[pl.BlockSpec(memory_space=pl.ANY)] * 4,
        out_specs=pl.BlockSpec(memory_space=pltpu.VMEM),
        out_shape=jax.ShapeDtypeStruct((EXPERTS, ROWS, BLOCK), jnp.bfloat16),
        scratch_shapes=[
            pltpu.SMEM((EXPERTS,), jnp.int32),
            pltpu.SMEM((EXPERTS,), jnp.int32),
            pltpu.VMEM(updated.shape, jnp.bfloat16),
            pltpu.VMEM(updated.shape, jnp.bfloat16),
            pltpu.SemaphoreType.DMA((2, updated.shape[0])),
            pltpu.SemaphoreType.DMA((2,)),
        ],
        name="encode",
    )(sync_ids, owner_map, updated, trainer_base)


def swaps(zh):
    return (zh + 1) // 2 % 2


def exchange(values):
    groups = []
    for y in range(4):
        for group in range(2):
            groups.append(
                [(y * 2 + (group ^ swaps(s // 8))) * 32 + s for s in range(32)]
            )
    return lax.all_to_all(
        values, ("rollout", "shard"), split_axis=0, concat_axis=0, axis_index_groups=groups, tiled=True
    )


def shifted(block, dy=0, dz=0):
    pairs = []
    for y in range(4):
        for z in range(2):
            pairs.append((y * 2 + z, (y + dy) % 4 * 2 + (z + dz) % 2))
    return lax.ppermute(block, "rollout", pairs)


def column_of(k, band):
    rollout, zh = lax.axis_index("rollout"), lax.axis_index("shard") // 8
    dy, dz = MOVES[k]
    y = (rollout // 2 + dy + 4) % 4
    z = (rollout + dz + swaps(zh) + swaps(band)) % 2
    return pl.ds(pl.multiple_of((y * 2 + z) * BLOCK, BLOCK), BLOCK)


def cut(spans, low, high):
    found = []
    for n, (start, stop) in enumerate(spans):
        a, b = max(start, low), min(stop, high)
        if a < b:
            found.append((n, pl.ds(a - start, b - a), a, b - a))
    return found


def add_kernel(spans, base_ref, *refs):
    parts, (out_ref, rest_ref) = refs[:-2], refs[-2:]
    band = pl.program_id(0)
    for k in range(FIRST, 8):
        rest_ref[k - FIRST] = base_ref[:, column_of(k, band)]
    for n in range(4):

        @pl.when(band == n)
        def _():
            first = 0
            for k in range(FIRST):
                columns = column_of(k, band)
                for which, rows, a, size in cut(spans[k], n * BAND, (n + 1) * BAND):
                    at = pl.ds(a - n * BAND, size)
                    out_ref[at, columns] = base_ref[at, columns] + parts[first + which][rows, :]
                first += len(spans[k])


def add(base, spans, parts):
    rows = pl.BlockSpec((BAND, WIDTH), lambda i: (i, 0))
    return pl.pallas_call(
        functools.partial(add_kernel, spans),
        grid=(OWNED // BAND,),
        in_specs=[rows] + [pl.BlockSpec(memory_space=pltpu.VMEM)] * len(parts),
        out_specs=[rows, pl.BlockSpec((8 - FIRST, BAND, BLOCK), lambda i: (0, i, 0))],
        out_shape=[
            jax.ShapeDtypeStruct((OWNED, WIDTH), jnp.bfloat16),
            jax.ShapeDtypeStruct((8 - FIRST, OWNED, BLOCK), jnp.bfloat16),
        ],
        compiler_params=pltpu.CompilerParams(vmem_limit_bytes=12 * 2**20),
        cost_estimate=pl.CostEstimate(flops=OWNED * WIDTH, bytes_accessed=6 * OWNED * WIDTH, transcendentals=0),
        name="add",
    )(base, *parts)


def finish_kernel(spans, rest_ref, *refs):
    parts, (out_hbm, total_ref, sems) = refs[:-4], refs[-3:]
    copies = []
    first = 0
    for n in range(8 - FIRST):
        for band in range(4):
            for which, rows, a, size in cut(spans[n], band * BAND, (band + 1) * BAND):
                total_ref[n, pl.ds(a, size), :] = rest_ref[n, pl.ds(a, size), :] + parts[first + which][rows, :]
            rows = pl.ds(band * BAND, BAND)
            to = out_hbm.at[rows, column_of(n + FIRST, band)]
            copies.append(pltpu.make_async_copy(total_ref.at[n, rows], to, sems.at[n, band]))
            copies[-1].start()
        first += len(spans[n])
    for copy in copies:
        copy.wait()


def finish(rest, spans, parts, made):
    whole = pl.BlockSpec(memory_space=pltpu.VMEM)
    return pl.pallas_call(
        functools.partial(finish_kernel, spans),
        in_specs=[whole] * (1 + len(parts)) + [pl.BlockSpec(memory_space=pl.ANY)],
        out_specs=pl.BlockSpec(memory_space=pl.ANY),
        out_shape=jax.ShapeDtypeStruct((OWNED, WIDTH), jnp.bfloat16),
        scratch_shapes=[pltpu.VMEM((8 - FIRST, OWNED, BLOCK), jnp.bfloat16), pltpu.SemaphoreType.DMA((8 - FIRST, 4))],
        input_output_aliases={1 + len(parts): 0},
        compiler_params=pltpu.CompilerParams(vmem_limit_bytes=8 * 2**20),
        name="finish",
    )(rest, *parts, made)


def gather(own):
    own_a, own_b = own[:SPLIT], own[SPLIT:]
    beside_a, beside_b = shifted(own_a, dz=1), shifted(own_b, dz=1)
    below_a, above_b = shifted(own_a, dy=1), shifted(own_b, dy=-1)
    below_b, above_a = shifted(own_b, dy=1), shifted(own_a, dy=-1)
    bb_a, ba_b = shifted(beside_a, dy=1), shifted(beside_b, dy=-1)
    far_a, far_b = shifted(below_a, dy=1), shifted(above_b, dy=-1)
    bb_b, ba_a = shifted(below_b, dz=1), shifted(above_a, dz=1)
    fz_a, fz_b = shifted(bb_a, dy=1), shifted(ba_b, dy=-1)
    parts = [[own_a, own_b], [below_a, below_b], [above_a, above_b], [beside_a, beside_b], [far_a, far_b], [bb_a, bb_b], [ba_a, ba_b], [fz_a, fz_b]]
    spans = []
    for pieces in parts:
        ends = [sum(piece.shape[0] for piece in pieces[:n]) for n in range(len(pieces) + 1)]
        spans.append(list(zip(ends[:-1], ends[1:])))
    return parts, spans


def per_device(updated, trainer_base, rollout_base, sync_ids, owner_map):
    values = encode(updated, trainer_base, sync_ids, owner_map).reshape(32, PIECE, BLOCK)
    parts, spans = gather(exchange(values).reshape(OWNED, BLOCK))
    flat = lambda some: [piece for pieces in some for piece in pieces]
    made, rest = add(rollout_base[0], spans[:FIRST], flat(parts[:FIRST]))
    return finish(rest, spans[FIRST:], flat(parts[FIRST:]), made)[None]


def solution(mesh):
    return jax.shard_map(
        per_device,
        mesh=mesh,
        in_specs=(
            P(None, "shard", "rollout"),
            P(None, "shard", "rollout"),
            P("shard", None, None),
            P(),
            P(),
        ),
        out_specs=P("shard", None, None),
        check_vma=False,
    )
```

time: 67.7 us -> 65.1 us (0.962)
  Pallas kernels: 9.54 us -> 8.03 us
  blocking collectives: 29.9 us -> 28.5 us
  waiting for transfers between devices: 7.73 us -> 8.99 us
  starting transfers between devices: 18 us -> 17.1 us
    pallas_call x3, Pallas kernels: 9.54 us -> 8.03 us  [the longest x1 3.85 us: encode(): pl.pallas_call(encode_kernel, in_specs=[pl.BlockSpec(memory_space=pl.ANY)...]
    all_to_all x1, blocking collectives: 29.9 us -> 28.5 us  [exchange(): lax.all_to_all(values, ('rollout', 'shard'), split_axis=0, concat_axis=0,...]
    ppermute x14, waiting for transfers between devices: 7.73 us -> 8.99 us  [shifted(): return lax.ppermute(block, 'rollout', pairs)]
    ppermute x14, starting transfers between devices: 18 us -> 17.1 us  [shifted(): return lax.ppermute(block, 'rollout', pairs)]
  transfers between devices with their start and end apart: 14 -> 14, of which waited for: 5 -> 5; matrix products, arithmetic and copies ran while one was open for 0% -> 0% of each run, Pallas kernels for 5% -> 4%
where the time goes in v3:
time: 65.1 us; the launch traced here: 64.8 us
  blocking collectives  28.5 us (44%)
  starting transfers between devices  17.1 us (26%)
  waiting for transfers between devices  8.99 us (14%)
  Pallas kernels  8.03 us (12%)
  local copies, waits for them, and re-layouts  2.08 us (3%)
    all_to_all x1, blocking collectives, exchange(): lax.all_to_all(values, ('rollout', 'shard'), split_axis=0, concat_axis=0,...  28.5 us
    ppermute x14, starting transfers between devices, shifted(): return lax.ppermute(block, 'rollout', pairs)  17.1 us
    ppermute x14, waiting for transfers between devices, shifted(): return lax.ppermute(block, 'rollout', pairs)  8.99 us
    pallas_call x1, Pallas kernels, encode(): pl.pallas_call(encode_kernel, in_specs=[pl.BlockSpec(memory_space=pl.ANY)...  3.85 us
    pallas_call x1, Pallas kernels, add(): pl.pallas_call(functools.partial(add_kernel, spans), grid=(OWNED // BAND,...  2.78 us
    unnamed x2, local copies, waits for them, and re-layouts  2.04 us
    pallas_call x1, Pallas kernels, finish(): pl.pallas_call(functools.partial(finish_kernel, spans), in_specs=[whole]...  1.4 us
  transfers between devices with their start and end apart: 14, of which 5 were waited for; matrix products, arithmetic and copies ran while one was open for 0% of the time, Pallas kernels for 4%

profile of v3, /device:TPU:1, one launch (start us, length us, event | category | flops | bytes accessed | tf_op | source)
XLA Modules:
  0.0 64.8 jit_solution(16575549085081737358)
XLA Ops:
  0.0 3.8 %encode.1 = bf16[8,224,128]{2,1,0:T(8,128)(2,1)} custom-call(s32[8]{0:T(128)} %ids_hbm.1, s32[8]{0:T(128)} %owner_hbm.1, bf16[12,224,128]{2,1,0:T(8,128)(2,1)} %fresh_hbm.1, bf16[12,224,128]{2,1,0:T(8,128)(2,1)} %older_hbm.1), custom_call_target="tpu_custom_call" | custom-call | tf_op jit(solution)/shard_map/encode/pallas_call | solution.py:68
  3.9 28.5 %all_to_all.5 = bf16[32,56,128]{2,1,0:T(8,128)(2,1)S(1)} all-to-all(bf16[32,56,128]{2,1,0:T(8,128)(2,1)} %bitcast.14), channel_id=1, replica_groups={{0,1,2,3,4,5,6,7,40,41,42,43,44,45,46,47,48,49,50,51,52,53,54,55,24,25,..., dimensions={0} | all-to-all | bytes 917504 | tf_op jit(solution)/shard_map/all_to_all | solution.py:96
  32.4 1.0 %collective-permute-start.4 = (bf16[896,128]{1,0:T(8,128)(2,1)S(1)}, bf16[896,128]{1,0:T(8,128)(2,1)S(1)}, u32[]{:S(2)}, u32[]{:S(2)}) collective-permute-start(bf16[896,128]{1,0:T(8,128)(2,1)S(1)} %bitcast.10), channel_id=1, source_target_pairs={{0,32},{32,0},{64,96},{96,64},{128,160},{160,128},{192,224},{224,1... | collective-permute-start | bytes 688136 | tf_op jit(solution)/shard_map/ppermute | solution.py:106
  33.5 2.7 %collective-permute-start.2 = (bf16[896,128]{1,0:T(8,128)(2,1)S(1)}, bf16[896,128]{1,0:T(8,128)(2,1)S(1)}, u32[]{:S(2)}, u32[]{:S(2)}) collective-permute-start(bf16[896,128]{1,0:T(8,128)(2,1)S(1)} %bitcast.11), channel_id=1, source_target_pairs={{0,192},{32,224},{64,0},{96,32},{128,64},{160,96},{192,128},{224,1... | collective-permute-start | bytes 688136 | tf_op jit(solution)/shard_map/ppermute | solution.py:106
  36.2 0.0 collective-permute-start
  36.2 0.5 collective-permute-start.5
  36.7 2.7 %collective-permute-start.3 = (bf16[896,128]{1,0:T(8,128)(2,1)S(1)}, bf16[896,128]{1,0:T(8,128)(2,1)S(1)}, u32[]{:S(2)}, u32[]{:S(2)}) collective-permute-start(bf16[896,128]{1,0:T(8,128)(2,1)S(1)} %bitcast.7), channel_id=1, source_target_pairs={{0,192},{32,224},{64,0},{96,32},{128,64},{160,96},{192,128},{224,1... | collective-permute-start | bytes 688136 | tf_op jit(solution)/shard_map/ppermute | solution.py:106
  39.4 0.7 %collective-permute-done.4.refs_6_ = bf16[896,128]{1,0:T(8,128)(2,1)S(1)} collective-permute-done((bf16[896,128]{1,0:T(8,128)(2,1)S(1)}, bf16[896,128]{1,0:T(8,128)(2,1)S(1)}, u32[]{:S(2)}, u32[]{:S(2)}) %collective-permute-start.4) | collective-permute-done | bytes 229408 | tf_op jit(solution)/shard_map/ppermute | solution.py:106
  40.1 1.3 %collective-permute-start.1 = (bf16[896,128]{1,0:T(8,128)(2,1)S(1)}, bf16[896,128]{1,0:T(8,128)(2,1)S(1)}, u32[]{:S(2)}, u32[]{:S(2)}) collective-permute-start(bf16[896,128]{1,0:T(8,128)(2,1)S(1)} %bitcast.8), channel_id=1, source_target_pairs={{0,64},{32,96},{64,128},{96,160},{128,192},{160,224},{192,0},{224,... | collective-permute-start | bytes 688136 | tf_op jit(solution)/shard_map/ppermute | solution.py:106
  41.4 0.0 collective-permute-done.2.refs_4_
  41.4 1.3 %collective-permute-start.8 = (bf16[896,128]{1,0:T(8,128)(2,1)S(1)}, bf16[896,128]{1,0:T(8,128)(2,1)S(1)}, u32[]{:S(2)}, u32[]{:S(2)}) collective-permute-start(bf16[896,128]{1,0:T(8,128)(2,1)S(1)} %collective-permute-done.4.refs_6_), channel_id=1, source_target_pairs={{0,64},{32,96},{64,128},{96,160},{128,192},{160,224},{192,0},{224,... | collective-permute-start | bytes 688136 | tf_op jit(solution)/shard_map/ppermute | solution.py:106
  42.7 1.7 %collective-permute-done.refs_2_ = bf16[896,128]{1,0:T(8,128)(2,1)S(1)} collective-permute-done((bf16[896,128]{1,0:T(8,128)(2,1)S(1)}, bf16[896,128]{1,0:T(8,128)(2,1)S(1)}, u32[]{:S(2)}, u32[]{:S(2)}) %collective-permute-start) | collective-permute-done | bytes 229408 | tf_op jit(solution)/shard_map/ppermute | solution.py:106
  44.4 0.5 collective-permute-start.10
  45.0 0.0 collective-permute-done.5.refs_7_
  45.0 2.7 %collective-permute-start.11 = (bf16[896,128]{1,0:T(8,128)(2,1)S(1)}, bf16[896,128]{1,0:T(8,128)(2,1)S(1)}, u32[]{:S(2)}, u32[]{:S(2)}) collective-permute-start(bf16[896,128]{1,0:T(8,128)(2,1)S(1)} %collective-permute-done.5.refs_7_), channel_id=1, source_target_pairs={{0,192},{32,224},{64,0},{96,32},{128,64},{160,96},{192,128},{224,1... | collective-permute-start | bytes 688136 | tf_op jit(solution)/shard_map/ppermute | solution.py:106
  47.7 0.0 collective-permute-done.3.refs_5_
  47.7 0.0 collective-permute-start.6
  47.7 1.6 %collective-permute-done.1.refs_3_ = bf16[896,128]{1,0:T(8,128)(2,1)S(1)} collective-permute-done((bf16[896,128]{1,0:T(8,128)(2,1)S(1)}, bf16[896,128]{1,0:T(8,128)(2,1)S(1)}, u32[]{:S(2)}, u32[]{:S(2)}) %collective-permute-start.1) | collective-permute-done | bytes 229408 | tf_op jit(solution)/shard_map/ppermute | solution.py:106
  49.4 1.1 %collective-permute-start.7 = (bf16[896,128]{1,0:T(8,128)(2,1)S(1)}, bf16[896,128]{1,0:T(8,128)(2,1)S(1)}, u32[]{:S(2)}, u32[]{:S(2)}) collective-permute-start(bf16[896,128]{1,0:T(8,128)(2,1)S(1)} %collective-permute-done.3.refs_5_), channel_id=1, source_target_pairs={{0,192},{32,224},{64,0},{96,32},{128,64},{160,96},{192,128},{224,1... | collective-permute-start | bytes 688136 | tf_op jit(solution)/shard_map/ppermute | solution.py:106
  50.4 3.8 %collective-permute-done.8.refs_2_ = bf16[896,128]{1,0:T(8,128)(2,1)S(1)} collective-permute-done((bf16[896,128]{1,0:T(8,128)(2,1)S(1)}, bf16[896,128]{1,0:T(8,128)(2,1)S(1)}, u32[]{:S(2)}, u32[]{:S(2)}) %collective-permute-start.8) | collective-permute-done | bytes 229408 | tf_op jit(solution)/shard_map/ppermute | solution.py:106
  54.3 0.5 collective-permute-start.9
  54.8 0.0 collective-permute-done.10.refs_4_
  54.8 0.0 collective-permute-start.12
  54.8 0.0 collective-permute-done.11.refs_5_
  54.8 2.7 %collective-permute-start.13 = (bf16[896,128]{1,0:T(8,128)(2,1)S(1)}, bf16[896,128]{1,0:T(8,128)(2,1)S(1)}, u32[]{:S(2)}, u32[]{:S(2)}) collective-permute-start(bf16[896,128]{1,0:T(8,128)(2,1)S(1)} %collective-permute-done.11.refs_5_), channel_id=1, source_target_pairs={{0,192},{32,224},{64,0},{96,32},{128,64},{160,96},{192,128},{224,1... | collective-permute-start | bytes 688136 | tf_op jit(solution)/shard_map/ppermute | solution.py:106
  57.5 0.0 copy-start
  57.5 2.0 %copy-done = bf16[1,1792,1024]{2,1,0:T(8,128)(2,1)S(1)} copy-done((bf16[1,1792,1024]{2,1,0:T(8,128)(2,1)S(1)}, bf16[1,1792,1024]{2,1,0:T(8,128)(2,1)}, u32[]{:S(2)}) %copy-start) | copy-done | bytes 3670040
  59.5 2.8 %add.1 = (bf16[1792,1024]{1,0:T(8,128)(2,1)}, bf16[4,1792,128]{2,1,0:T(8,128)(2,1)S(1)}) custom-call(bf16[1792,1024]{1,0:T(8,128)(2,1)S(1)} %bitcast.5, bf16[896,128]{1,0:T(8,128)(2,1)S(1)} %bitcast.13, bf16[896,128]{1,0:T(8,128)(2,1)S(1)} %bitcast.9, bf16[896,128]{1,0:T(8,128)(2,1)S(1)} %collective-permute-done.refs_2_, ...), custom_call_target="tpu_custom_call" | custom-call | flops 1835008 | bytes 11010048 | tf_op jit(solution)/shard_map/add/pallas_call | solution.py:146
  62.3 0.0 collective-permute-done.6.refs_0_
  62.3 0.0 collective-permute-done.7.refs_1_
  62.3 0.0 collective-permute-done.9.refs_3_
  62.3 1.1 %collective-permute-done.12.refs_6_ = bf16[896,128]{1,0:T(8,128)(2,1)S(1)} collective-permute-done((bf16[896,128]{1,0:T(8,128)(2,1)S(1)}, bf16[896,128]{1,0:T(8,128)(2,1)S(1)}, u32[]{:S(2)}, u32[]{:S(2)}) %collective-permute-start.12) | collective-permute-done | bytes 229408 | tf_op jit(solution)/shard_map/ppermute | solution.py:106
  63.4 0.0 collective-permute-done.13.refs_7_
  63.4 1.4 %finish.1 = bf16[1792,1024]{1,0:T(8,128)(2,1)} custom-call(bf16[4,1792,128]{2,1,0:T(8,128)(2,1)S(1)} %get-tuple-element.7.rest_ref, bf16[896,128]{1,0:T(8,128)(2,1)S(1)} %collective-permute-done.6.refs_0_, bf16[896,128]{1,0:T(8,128)(2,1)S(1)} %collective-permute-done.7.refs_1_, ...), custom_call_target="tpu_custom_call", output_to_operand_aliasing={{}: (9, {})} | custom-call | tf_op jit(solution)/shard_map/finish/pallas_call | solution.py:180
  (1 shorter events, 0.0 us)
Async XLA Ops:
  32.4 7.7 %collective-permute-start.4 = (bf16[896,128]{1,0:T(8,128)(2,1)S(1)}, bf16[896,128]{1,0:T(8,128)(2,1)S(1)}, u32[]{:S(2)}, u32[]{:S(2)}) collective-permute-start(bf16[896,128]{1,0:T(8,128)(2,1)S(1)} %bitcast.10), channel_id=1, source_target_pairs={{0,32},{32,0},{64,96},{96,64},{128,160},{160,128},{192,224},{224,1... | collective-permute-start | bytes 688136 | tf_op jit(solution)/shard_map/ppermute | solution.py:106
  33.5 7.9 %collective-permute-start.2 = (bf16[896,128]{1,0:T(8,128)(2,1)S(1)}, bf16[896,128]{1,0:T(8,128)(2,1)S(1)}, u32[]{:S(2)}, u32[]{:S(2)}) collective-permute-start(bf16[896,128]{1,0:T(8,128)(2,1)S(1)} %bitcast.11), channel_id=1, source_target_pairs={{0,192},{32,224},{64,0},{96,32},{128,64},{160,96},{192,128},{224,1... | collective-permute-start | bytes 688136 | tf_op jit(solution)/shard_map/ppermute | solution.py:106
  36.2 8.2 %collective-permute-start = (bf16[896,128]{1,0:T(8,128)(2,1)S(1)}, bf16[896,128]{1,0:T(8,128)(2,1)S(1)}, u32[]{:S(2)}, u32[]{:S(2)}) collective-permute-start(bf16[896,128]{1,0:T(8,128)(2,1)S(1)} %bitcast.12), channel_id=1, source_target_pairs={{0,64},{32,96},{64,128},{96,160},{128,192},{160,224},{192,0},{224,... | collective-permute-start | bytes 688136 | tf_op jit(solution)/shard_map/ppermute | solution.py:106
  36.2 8.8 %collective-permute-start.5 = (bf16[896,128]{1,0:T(8,128)(2,1)S(1)}, bf16[896,128]{1,0:T(8,128)(2,1)S(1)}, u32[]{:S(2)}, u32[]{:S(2)}) collective-permute-start(bf16[896,128]{1,0:T(8,128)(2,1)S(1)} %bitcast.6), channel_id=1, source_target_pairs={{0,32},{32,0},{64,96},{96,64},{128,160},{160,128},{192,224},{224,1... | collective-permute-start | bytes 688136 | tf_op jit(solution)/shard_map/ppermute | solution.py:106
  36.7 11.0 %collective-permute-start.3 = (bf16[896,128]{1,0:T(8,128)(2,1)S(1)}, bf16[896,128]{1,0:T(8,128)(2,1)S(1)}, u32[]{:S(2)}, u32[]{:S(2)}) collective-permute-start(bf16[896,128]{1,0:T(8,128)(2,1)S(1)} %bitcast.7), channel_id=1, source_target_pairs={{0,192},{32,224},{64,0},{96,32},{128,64},{160,96},{192,128},{224,1... | collective-permute-start | bytes 688136 | tf_op jit(solution)/shard_map/ppermute | solution.py:106
  40.1 9.3 %collective-permute-start.1 = (bf16[896,128]{1,0:T(8,128)(2,1)S(1)}, bf16[896,128]{1,0:T(8,128)(2,1)S(1)}, u32[]{:S(2)}, u32[]{:S(2)}) collective-permute-start(bf16[896,128]{1,0:T(8,128)(2,1)S(1)} %bitcast.8), channel_id=1, source_target_pairs={{0,64},{32,96},{64,128},{96,160},{128,192},{160,224},{192,0},{224,... | collective-permute-start | bytes 688136 | tf_op jit(solution)/shard_map/ppermute | solution.py:106
  41.4 12.9 %collective-permute-start.8 = (bf16[896,128]{1,0:T(8,128)(2,1)S(1)}, bf16[896,128]{1,0:T(8,128)(2,1)S(1)}, u32[]{:S(2)}, u32[]{:S(2)}) collective-permute-start(bf16[896,128]{1,0:T(8,128)(2,1)S(1)} %collective-permute-done.4.refs_6_), channel_id=1, source_target_pairs={{0,64},{32,96},{64,128},{96,160},{128,192},{160,224},{192,0},{224,... | collective-permute-start | bytes 688136 | tf_op jit(solution)/shard_map/ppermute | solution.py:106
  44.4 10.4 %collective-permute-start.10 = (bf16[896,128]{1,0:T(8,128)(2,1)S(1)}, bf16[896,128]{1,0:T(8,128)(2,1)S(1)}, u32[]{:S(2)}, u32[]{:S(2)}) collective-permute-start(bf16[896,128]{1,0:T(8,128)(2,1)S(1)} %collective-permute-done.2.refs_4_), channel_id=1, source_target_pairs={{0,32},{32,0},{64,96},{96,64},{128,160},{160,128},{192,224},{224,1... | collective-permute-start | bytes 688136 | tf_op jit(solution)/shard_map/ppermute | solution.py:106
  45.0 9.8 %collective-permute-start.11 = (bf16[896,128]{1,0:T(8,128)(2,1)S(1)}, bf16[896,128]{1,0:T(8,128)(2,1)S(1)}, u32[]{:S(2)}, u32[]{:S(2)}) collective-permute-start(bf16[896,128]{1,0:T(8,128)(2,1)S(1)} %collective-permute-done.5.refs_7_), channel_id=1, source_target_pairs={{0,192},{32,224},{64,0},{96,32},{128,64},{160,96},{192,128},{224,1... | collective-permute-start | bytes 688136 | tf_op jit(solution)/shard_map/ppermute | solution.py:106
  47.7 14.6 %collective-permute-start.6 = (bf16[896,128]{1,0:T(8,128)(2,1)S(1)}, bf16[896,128]{1,0:T(8,128)(2,1)S(1)}, u32[]{:S(2)}, u32[]{:S(2)}) collective-permute-start(bf16[896,128]{1,0:T(8,128)(2,1)S(1)} %collective-permute-done.refs_2_), channel_id=1, source_target_pairs={{0,64},{32,96},{64,128},{96,160},{128,192},{160,224},{192,0},{224,... | collective-permute-start | bytes 688136 | tf_op jit(solution)/shard_map/ppermute | solution.py:106
  49.4 13.0 %collective-permute-start.7 = (bf16[896,128]{1,0:T(8,128)(2,1)S(1)}, bf16[896,128]{1,0:T(8,128)(2,1)S(1)}, u32[]{:S(2)}, u32[]{:S(2)}) collective-permute-start(bf16[896,128]{1,0:T(8,128)(2,1)S(1)} %collective-permute-done.3.refs_5_), channel_id=1, source_target_pairs={{0,192},{32,224},{64,0},{96,32},{128,64},{160,96},{192,128},{224,1... | collective-permute-start | bytes 688136 | tf_op jit(solution)/shard_map/ppermute | solution.py:106
  54.3 8.1 %collective-permute-start.9 = (bf16[896,128]{1,0:T(8,128)(2,1)S(1)}, bf16[896,128]{1,0:T(8,128)(2,1)S(1)}, u32[]{:S(2)}, u32[]{:S(2)}) collective-permute-start(bf16[896,128]{1,0:T(8,128)(2,1)S(1)} %collective-permute-done.1.refs_3_), channel_id=1, source_target_pairs={{0,32},{32,0},{64,96},{96,64},{128,160},{160,128},{192,224},{224,1... | collective-permute-start | bytes 688136 | tf_op jit(solution)/shard_map/ppermute | solution.py:106
  54.8 8.6 %collective-permute-start.12 = (bf16[896,128]{1,0:T(8,128)(2,1)S(1)}, bf16[896,128]{1,0:T(8,128)(2,1)S(1)}, u32[]{:S(2)}, u32[]{:S(2)}) collective-permute-start(bf16[896,128]{1,0:T(8,128)(2,1)S(1)} %collective-permute-done.8.refs_2_), channel_id=1, source_target_pairs={{0,64},{32,96},{64,128},{96,160},{128,192},{160,224},{192,0},{224,... | collective-permute-start | bytes 688136 | tf_op jit(solution)/shard_map/ppermute | solution.py:106
  54.8 8.6 %collective-permute-start.13 = (bf16[896,128]{1,0:T(8,128)(2,1)S(1)}, bf16[896,128]{1,0:T(8,128)(2,1)S(1)}, u32[]{:S(2)}, u32[]{:S(2)}) collective-permute-start(bf16[896,128]{1,0:T(8,128)(2,1)S(1)} %collective-permute-done.11.refs_5_), channel_id=1, source_target_pairs={{0,192},{32,224},{64,0},{96,32},{128,64},{160,96},{192,128},{224,1... | collective-permute-start | bytes 688136 | tf_op jit(solution)/shard_map/ppermute | solution.py:106
  57.5 2.0 %copy-start = (bf16[1,1792,1024]{2,1,0:T(8,128)(2,1)S(1)}, bf16[1,1792,1024]{2,1,0:T(8,128)(2,1)}, u32[]{:S(2)}) copy-start(bf16[1,1792,1024]{2,1,0:T(8,128)(2,1)} %param.7) | copy-start | bytes 11010052

commit v4 on v3

--- a/solution.py
+++ b/solution.py
@@ -15,7 +15,7 @@
 WIDTH = 1024
 BAND = 448
 SPLIT = 896
-FIRST = 4
+FIRST = 5
 MOVES = [(0, 0), (-1, 0), (1, 0), (0, 1), (2, 0), (-1, 1), (1, 1), (2, 1)]
 
 
@@ -191,14 +191,15 @@
 
 def gather(own):
     own_a, own_b = own[:SPLIT], own[SPLIT:]
-    beside_a, beside_b = shifted(own_a, dz=1), shifted(own_b, dz=1)
     below_a, above_b = shifted(own_a, dy=1), shifted(own_b, dy=-1)
+    beside = shifted(own, dz=1)
     below_b, above_a = shifted(own_b, dy=1), shifted(own_a, dy=-1)
-    bb_a, ba_b = shifted(beside_a, dy=1), shifted(beside_b, dy=-1)
     far_a, far_b = shifted(below_a, dy=1), shifted(above_b, dy=-1)
-    bb_b, ba_a = shifted(below_b, dz=1), shifted(above_a, dz=1)
-    fz_a, fz_b = shifted(bb_a, dy=1), shifted(ba_b, dy=-1)
-    parts = [[own_a, own_b], [below_a, below_b], [above_a, above_b], [beside_a, beside_b], [far_a, far_b], [bb_a, bb_b], [ba_a, ba_b], [fz_a, fz_b]]
+    up, below_b = lax.optimization_barrier((beside, below_b))
+    down, above_a = lax.optimization_barrier((beside, above_a))
+    bb, ba = shifted(up, dy=1), shifted(down, dy=-1)
+    fz_a, fz_b = shifted(far_a, dz=1), shifted(far_b, dz=1)
+    parts = [[own_a, own_b], [below_a, below_b], [above_a, above_b], [beside], [far_a, far_b], [bb], [ba], [fz_a, fz_b]]
     spans = []
     for pieces in parts:
         ends = [sum(piece.shape[0] for piece in pieces[:n]) for n in range(len(pieces) + 1)]

time: 65.1 us -> 64 us (0.983)
  starting transfers between devices: 17.1 us -> 12.4 us
  waiting for transfers between devices: 8.99 us -> 12.7 us
    ppermute x14 -> x11, starting transfers between devices: 17.1 us -> 12.4 us  [shifted(): return lax.ppermute(block, 'rollout', pairs)]
    ppermute x14 -> x11, waiting for transfers between devices: 8.99 us -> 12.7 us  [shifted(): return lax.ppermute(block, 'rollout', pairs)]
  transfers between devices with their start and end apart: 14 -> 11, of which waited for: 5 -> 5; matrix products, arithmetic and copies ran while one was open for 0% -> 0% of each run, Pallas kernels for 4% -> 4%
where the time goes in v4:
time: 64 us; the launch traced here: 63.5 us
  blocking collectives  28.5 us (45%)
  waiting for transfers between devices  12.7 us (20%)
  starting transfers between devices  12.4 us (19%)
  Pallas kernels  7.86 us (12%)
  local copies, waits for them, and re-layouts  2.08 us (3%)
    all_to_all x1, blocking collectives, exchange(): lax.all_to_all(values, ('rollout', 'shard'), split_axis=0, concat_axis=0,...  28.5 us
    ppermute x11, waiting for transfers between devices, shifted(): return lax.ppermute(block, 'rollout', pairs)  12.7 us
    ppermute x11, starting transfers between devices, shifted(): return lax.ppermute(block, 'rollout', pairs)  12.4 us
    pallas_call x1, Pallas kernels, encode(): pl.pallas_call(encode_kernel, in_specs=[pl.BlockSpec(memory_space=pl.ANY)...  3.85 us
    pallas_call x1, Pallas kernels, add(): pl.pallas_call(functools.partial(add_kernel, spans), grid=(OWNED // BAND,...  2.79 us
    unnamed x2, local copies, waits for them, and re-layouts  2.04 us
  transfers between devices with their start and end apart: 11, of which 5 were waited for; matrix products, arithmetic and copies ran while one was open for 0% of the time, Pallas kernels for 4%

profile of v4, /device:TPU:1, one launch (start us, length us, event | category | flops | bytes accessed | tf_op | source)
XLA Modules:
  0.0 63.5 jit_solution(16958506844138230523)
XLA Ops:
  0.0 3.8 %encode.1 = bf16[8,224,128]{2,1,0:T(8,128)(2,1)} custom-call(s32[8]{0:T(128)} %ids_hbm.1, s32[8]{0:T(128)} %owner_hbm.1, bf16[12,224,128]{2,1,0:T(8,128)(2,1)} %fresh_hbm.1, bf16[12,224,128]{2,1,0:T(8,128)(2,1)} %older_hbm.1), custom_call_target="tpu_custom_call" | custom-call | tf_op jit(solution)/shard_map/encode/pallas_call | solution.py:68
  3.9 28.5 %all_to_all.5 = bf16[32,56,128]{2,1,0:T(8,128)(2,1)S(1)} all-to-all(bf16[32,56,128]{2,1,0:T(8,128)(2,1)} %bitcast.14), channel_id=1, replica_groups={{0,1,2,3,4,5,6,7,40,41,42,43,44,45,46,47,48,49,50,51,52,53,54,55,24,25,..., dimensions={0} | all-to-all | bytes 917504 | tf_op jit(solution)/shard_map/all_to_all | solution.py:96
  32.4 0.9 %collective-permute-start.1 = (bf16[1792,128]{1,0:T(8,128)(2,1)S(1)}, bf16[1792,128]{1,0:T(8,128)(2,1)S(1)}, u32[]{:S(2)}, u32[]{:S(2)}) collective-permute-start(bf16[1792,128]{1,0:T(8,128)(2,1)S(1)} %bitcast.13), channel_id=1, source_target_pairs={{0,32},{32,0},{64,96},{96,64},{128,160},{160,128},{192,224},{224,1... | collective-permute-start | bytes 1376264 | tf_op jit(solution)/shard_map/ppermute | solution.py:106
  33.4 1.4 %collective-permute-start = (bf16[896,128]{1,0:T(8,128)(2,1)S(1)}, bf16[896,128]{1,0:T(8,128)(2,1)S(1)}, u32[]{:S(2)}, u32[]{:S(2)}) collective-permute-start(bf16[896,128]{1,0:T(8,128)(2,1)S(1)} %bitcast.10), channel_id=1, source_target_pairs={{0,64},{32,96},{64,128},{96,160},{128,192},{160,224},{192,0},{224,... | collective-permute-start | bytes 688136 | tf_op jit(solution)/shard_map/ppermute | solution.py:106
  34.8 1.5 %collective-permute-start.4 = (bf16[896,128]{1,0:T(8,128)(2,1)S(1)}, bf16[896,128]{1,0:T(8,128)(2,1)S(1)}, u32[]{:S(2)}, u32[]{:S(2)}) collective-permute-start(bf16[896,128]{1,0:T(8,128)(2,1)S(1)} %bitcast.7), channel_id=1, source_target_pairs={{0,192},{32,224},{64,0},{96,32},{128,64},{160,96},{192,128},{224,1... | collective-permute-start | bytes 688136 | tf_op jit(solution)/shard_map/ppermute | solution.py:106
  36.3 1.4 %collective-permute-start.3 = (bf16[896,128]{1,0:T(8,128)(2,1)S(1)}, bf16[896,128]{1,0:T(8,128)(2,1)S(1)}, u32[]{:S(2)}, u32[]{:S(2)}) collective-permute-start(bf16[896,128]{1,0:T(8,128)(2,1)S(1)} %bitcast.11), channel_id=1, source_target_pairs={{0,192},{32,224},{64,0},{96,32},{128,64},{160,96},{192,128},{224,1... | collective-permute-start | bytes 688136 | tf_op jit(solution)/shard_map/ppermute | solution.py:106
  37.7 0.1 collective-permute-start.2
  37.8 4.3 %collective-permute-done.refs_2_ = bf16[896,128]{1,0:T(8,128)(2,1)S(1)} collective-permute-done((bf16[896,128]{1,0:T(8,128)(2,1)S(1)}, bf16[896,128]{1,0:T(8,128)(2,1)S(1)}, u32[]{:S(2)}, u32[]{:S(2)}) %collective-permute-start) | collective-permute-done | bytes 229408 | tf_op jit(solution)/shard_map/ppermute | solution.py:106
  42.1 0.0 collective-permute-start.5
  42.1 0.0 collective-permute-done.4.refs_5_
  42.1 2.6 %collective-permute-start.6 = (bf16[896,128]{1,0:T(8,128)(2,1)S(1)}, bf16[896,128]{1,0:T(8,128)(2,1)S(1)}, u32[]{:S(2)}, u32[]{:S(2)}) collective-permute-start(bf16[896,128]{1,0:T(8,128)(2,1)S(1)} %collective-permute-done.4.refs_5_), channel_id=1, source_target_pairs={{0,192},{32,224},{64,0},{96,32},{128,64},{160,96},{192,128},{224,1... | collective-permute-start | bytes 688136 | tf_op jit(solution)/shard_map/ppermute | solution.py:106
  44.7 2.0 %collective-permute-done.3.refs_4_ = bf16[896,128]{1,0:T(8,128)(2,1)S(1)} collective-permute-done((bf16[896,128]{1,0:T(8,128)(2,1)S(1)}, bf16[896,128]{1,0:T(8,128)(2,1)S(1)}, u32[]{:S(2)}, u32[]{:S(2)}) %collective-permute-start.3) | collective-permute-done | bytes 229408 | tf_op jit(solution)/shard_map/ppermute | solution.py:106
  46.7 0.0 collective-permute-done.1.refs_6_
  46.7 0.1 collective-permute-done.2.refs_3_
  46.8 1.2 %collective-permute-start.7 = (bf16[1792,128]{1,0:T(8,128)(2,1)S(1)}, bf16[1792,128]{1,0:T(8,128)(2,1)S(1)}, u32[]{:S(2)}, u32[]{:S(2)}) collective-permute-start(bf16[1792,128]{1,0:T(8,128)(2,1)S(1)} %collective-permute-done.1.refs_6_), channel_id=1, source_target_pairs={{0,64},{32,96},{64,128},{96,160},{128,192},{160,224},{192,0},{224,... | collective-permute-start | bytes 1376264 | tf_op jit(solution)/shard_map/ppermute | solution.py:106
  48.0 1.7 %collective-permute-start.8 = (bf16[1792,128]{1,0:T(8,128)(2,1)S(1)}, bf16[1792,128]{1,0:T(8,128)(2,1)S(1)}, u32[]{:S(2)}, u32[]{:S(2)}) collective-permute-start(bf16[1792,128]{1,0:T(8,128)(2,1)S(1)} %collective-permute-done.1.refs_6_), channel_id=1, source_target_pairs={{0,192},{32,224},{64,0},{96,32},{128,64},{160,96},{192,128},{224,1... | collective-permute-start | bytes 1376264 | tf_op jit(solution)/shard_map/ppermute | solution.py:106
  49.7 2.0 %collective-permute-done.5.refs_7_ = bf16[896,128]{1,0:T(8,128)(2,1)S(1)} collective-permute-done((bf16[896,128]{1,0:T(8,128)(2,1)S(1)}, bf16[896,128]{1,0:T(8,128)(2,1)S(1)}, u32[]{:S(2)}, u32[]{:S(2)}) %collective-permute-start.5) | collective-permute-done | bytes 229408 | tf_op jit(solution)/shard_map/ppermute | solution.py:106
  51.7 0.5 collective-permute-start.9
  52.2 0.0 collective-permute-done.6.refs_8_
  52.2 0.9 %collective-permute-start.10 = (bf16[896,128]{1,0:T(8,128)(2,1)S(1)}, bf16[896,128]{1,0:T(8,128)(2,1)S(1)}, u32[]{:S(2)}, u32[]{:S(2)}) collective-permute-start(bf16[896,128]{1,0:T(8,128)(2,1)S(1)} %collective-permute-done.6.refs_8_), channel_id=1, source_target_pairs={{0,32},{32,0},{64,96},{96,64},{128,160},{160,128},{192,224},{224,1... | collective-permute-start | bytes 688136 | tf_op jit(solution)/shard_map/ppermute | solution.py:106
  53.2 0.0 copy-start
  53.2 2.0 %copy-done = bf16[1,1792,1024]{2,1,0:T(8,128)(2,1)S(1)} copy-done((bf16[1,1792,1024]{2,1,0:T(8,128)(2,1)S(1)}, bf16[1,1792,1024]{2,1,0:T(8,128)(2,1)}, u32[]{:S(2)}) %copy-start) | copy-done | bytes 3670040
  55.2 2.8 %add.1 = (bf16[1792,1024]{1,0:T(8,128)(2,1)}, bf16[3,1792,128]{2,1,0:T(8,128)(2,1)S(1)}) custom-call(bf16[1792,1024]{1,0:T(8,128)(2,1)S(1)} %bitcast.6, bf16[896,128]{1,0:T(8,128)(2,1)S(1)} %bitcast.12, bf16[896,128]{1,0:T(8,128)(2,1)S(1)} %bitcast.9, bf16[896,128]{1,0:T(8,128)(2,1)S(1)} %collective-permute-done.refs_2_, ...), custom_call_target="tpu_custom_call" | custom-call | flops 1835008 | bytes 11010048 | tf_op jit(solution)/shard_map/add/pallas_call | solution.py:146
  58.0 0.0 collective-permute-done.9.refs_2_
  58.0 4.3 %collective-permute-done.10.refs_3_ = bf16[896,128]{1,0:T(8,128)(2,1)S(1)} collective-permute-done((bf16[896,128]{1,0:T(8,128)(2,1)S(1)}, bf16[896,128]{1,0:T(8,128)(2,1)S(1)}, u32[]{:S(2)}, u32[]{:S(2)}) %collective-permute-start.10) | collective-permute-done | bytes 229408 | tf_op jit(solution)/shard_map/ppermute | solution.py:106
  62.3 0.0 collective-permute-done.7.refs_0_
  62.3 0.0 collective-permute-done.8.refs_1_
  62.3 1.2 %finish.1 = bf16[1792,1024]{1,0:T(8,128)(2,1)} custom-call(bf16[3,1792,128]{2,1,0:T(8,128)(2,1)S(1)} %get-tuple-element.13.rest_ref, bf16[1792,128]{1,0:T(8,128)(2,1)S(1)} %collective-permute-done.7.refs_0_, bf16[1792,128]{1,0:T(8,128)(2,1)S(1)} %collective-permute-done.8.refs_1_, ...), custom_call_target="tpu_custom_call", output_to_operand_aliasing={{}: (5, {})} | custom-call | tf_op jit(solution)/shard_map/finish/pallas_call | solution.py:180
  (1 shorter events, 0.0 us)
Async XLA Ops:
  32.4 14.3 %collective-permute-start.1 = (bf16[1792,128]{1,0:T(8,128)(2,1)S(1)}, bf16[1792,128]{1,0:T(8,128)(2,1)S(1)}, u32[]{:S(2)}, u32[]{:S(2)}) collective-permute-start(bf16[1792,128]{1,0:T(8,128)(2,1)S(1)} %bitcast.13), channel_id=1, source_target_pairs={{0,32},{32,0},{64,96},{96,64},{128,160},{160,128},{192,224},{224,1... | collective-permute-start | bytes 1376264 | tf_op jit(solution)/shard_map/ppermute | solution.py:106
  33.4 8.7 %collective-permute-start = (bf16[896,128]{1,0:T(8,128)(2,1)S(1)}, bf16[896,128]{1,0:T(8,128)(2,1)S(1)}, u32[]{:S(2)}, u32[]{:S(2)}) collective-permute-start(bf16[896,128]{1,0:T(8,128)(2,1)S(1)} %bitcast.10), channel_id=1, source_target_pairs={{0,64},{32,96},{64,128},{96,160},{128,192},{160,224},{192,0},{224,... | collective-permute-start | bytes 688136 | tf_op jit(solution)/shard_map/ppermute | solution.py:106
  34.8 7.3 %collective-permute-start.4 = (bf16[896,128]{1,0:T(8,128)(2,1)S(1)}, bf16[896,128]{1,0:T(8,128)(2,1)S(1)}, u32[]{:S(2)}, u32[]{:S(2)}) collective-permute-start(bf16[896,128]{1,0:T(8,128)(2,1)S(1)} %bitcast.7), channel_id=1, source_target_pairs={{0,192},{32,224},{64,0},{96,32},{128,64},{160,96},{192,128},{224,1... | collective-permute-start | bytes 688136 | tf_op jit(solution)/shard_map/ppermute | solution.py:106
  36.3 10.4 %collective-permute-start.3 = (bf16[896,128]{1,0:T(8,128)(2,1)S(1)}, bf16[896,128]{1,0:T(8,128)(2,1)S(1)}, u32[]{:S(2)}, u32[]{:S(2)}) collective-permute-start(bf16[896,128]{1,0:T(8,128)(2,1)S(1)} %bitcast.11), channel_id=1, source_target_pairs={{0,192},{32,224},{64,0},{96,32},{128,64},{160,96},{192,128},{224,1... | collective-permute-start | bytes 688136 | tf_op jit(solution)/shard_map/ppermute | solution.py:106
  37.7 9.1 %collective-permute-start.2 = (bf16[896,128]{1,0:T(8,128)(2,1)S(1)}, bf16[896,128]{1,0:T(8,128)(2,1)S(1)}, u32[]{:S(2)}, u32[]{:S(2)}) collective-permute-start(bf16[896,128]{1,0:T(8,128)(2,1)S(1)} %bitcast.8), channel_id=1, source_target_pairs={{0,64},{32,96},{64,128},{96,160},{128,192},{160,224},{192,0},{224,... | collective-permute-start | bytes 688136 | tf_op jit(solution)/shard_map/ppermute | solution.py:106
  42.1 9.6 %collective-permute-start.5 = (bf16[896,128]{1,0:T(8,128)(2,1)S(1)}, bf16[896,128]{1,0:T(8,128)(2,1)S(1)}, u32[]{:S(2)}, u32[]{:S(2)}) collective-permute-start(bf16[896,128]{1,0:T(8,128)(2,1)S(1)} %collective-permute-done.refs_2_), channel_id=1, source_target_pairs={{0,64},{32,96},{64,128},{96,160},{128,192},{160,224},{192,0},{224,... | collective-permute-start | bytes 688136 | tf_op jit(solution)/shard_map/ppermute | solution.py:106
  42.1 10.1 %collective-permute-start.6 = (bf16[896,128]{1,0:T(8,128)(2,1)S(1)}, bf16[896,128]{1,0:T(8,128)(2,1)S(1)}, u32[]{:S(2)}, u32[]{:S(2)}) collective-permute-start(bf16[896,128]{1,0:T(8,128)(2,1)S(1)} %collective-permute-done.4.refs_5_), channel_id=1, source_target_pairs={{0,192},{32,224},{64,0},{96,32},{128,64},{160,96},{192,128},{224,1... | collective-permute-start | bytes 688136 | tf_op jit(solution)/shard_map/ppermute | solution.py:106
  46.8 15.5 %collective-permute-start.7 = (bf16[1792,128]{1,0:T(8,128)(2,1)S(1)}, bf16[1792,128]{1,0:T(8,128)(2,1)S(1)}, u32[]{:S(2)}, u32[]{:S(2)}) collective-permute-start(bf16[1792,128]{1,0:T(8,128)(2,1)S(1)} %collective-permute-done.1.refs_6_), channel_id=1, source_target_pairs={{0,64},{32,96},{64,128},{96,160},{128,192},{160,224},{192,0},{224,... | collective-permute-start | bytes 1376264 | tf_op jit(solution)/shard_map/ppermute | solution.py:106
  48.0 14.3 %collective-permute-start.8 = (bf16[1792,128]{1,0:T(8,128)(2,1)S(1)}, bf16[1792,128]{1,0:T(8,128)(2,1)S(1)}, u32[]{:S(2)}, u32[]{:S(2)}) collective-permute-start(bf16[1792,128]{1,0:T(8,128)(2,1)S(1)} %collective-permute-done.1.refs_6_), channel_id=1, source_target_pairs={{0,192},{32,224},{64,0},{96,32},{128,64},{160,96},{192,128},{224,1... | collective-permute-start | bytes 1376264 | tf_op jit(solution)/shard_map/ppermute | solution.py:106
  51.7 6.3 %collective-permute-start.9 = (bf16[896,128]{1,0:T(8,128)(2,1)S(1)}, bf16[896,128]{1,0:T(8,128)(2,1)S(1)}, u32[]{:S(2)}, u32[]{:S(2)}) collective-permute-start(bf16[896,128]{1,0:T(8,128)(2,1)S(1)} %collective-permute-done.5.refs_7_), channel_id=1, source_target_pairs={{0,32},{32,0},{64,96},{96,64},{128,160},{160,128},{192,224},{224,1... | collective-permute-start | bytes 688136 | tf_op jit(solution)/shard_map/ppermute | solution.py:106
  52.2 10.1 %collective-permute-start.10 = (bf16[896,128]{1,0:T(8,128)(2,1)S(1)}, bf16[896,128]{1,0:T(8,128)(2,1)S(1)}, u32[]{:S(2)}, u32[]{:S(2)}) collective-permute-start(bf16[896,128]{1,0:T(8,128)(2,1)S(1)} %collective-permute-done.6.refs_8_), channel_id=1, source_target_pairs={{0,32},{32,0},{64,96},{96,64},{128,160},{160,128},{192,224},{224,1... | collective-permute-start | bytes 688136 | tf_op jit(solution)/shard_map/ppermute | solution.py:106
  53.2 2.0 %copy-start = (bf16[1,1792,1024]{2,1,0:T(8,128)(2,1)S(1)}, bf16[1,1792,1024]{2,1,0:T(8,128)(2,1)}, u32[]{:S(2)}) copy-start(bf16[1,1792,1024]{2,1,0:T(8,128)(2,1)} %param.7) | copy-start | bytes 11010052

commit v5 on v4

--- a/solution.py
+++ b/solution.py
@@ -40,43 +40,57 @@
     return jnp.where(delta < 0.0, -rounded, rounded)
 
 
-def encode_kernel(ids_hbm, owner_hbm, fresh_hbm, older_hbm, value_ref, ids_ref, owner_ref, fresh_ref, older_ref, sems, few):
+def encode_kernel(ids_hbm, owner_hbm, fresh_hbm, older_hbm, out_hbm, ids_ref, owner_ref, place_ref, fresh_ref, older_ref, value_ref, sems, few, sent):
+    slots = fresh_ref.shape[0]
     ids = pltpu.make_async_copy(ids_hbm, ids_ref, few.at[0])
     owner = pltpu.make_async_copy(owner_hbm, owner_ref, few.at[1])
     ids.start()
     owner.start()
-    slots = fresh_ref.shape[0]
     copies = []
     for slot in range(slots):
         fresh = pltpu.make_async_copy(fresh_hbm.at[slot], fresh_ref.at[slot], sems.at[0, slot])
         older = pltpu.make_async_copy(older_hbm.at[slot], older_ref.at[slot], sems.at[1, slot])
         fresh.start()
         older.start()
-        copies += [fresh, older]
+        copies.append((fresh, older))
+    for slot in range(slots):
+        place_ref[slot] = -1
     ids.wait()
     owner.wait()
-    for copy in copies:
-        copy.wait()
-
-    @pl.loop(0, EXPERTS)
-    def _(e):
-        slot = ids_ref[e]
-        value_ref[owner_ref[e]] = quantize(fresh_ref[slot], older_ref[slot]).astype(jnp.bfloat16)
+    for e in range(EXPERTS):
+        place_ref[ids_ref[e]] = owner_ref[e]
+    for slot, (fresh, older) in enumerate(copies):
+        fresh.wait()
+        older.wait()
+        place = place_ref[slot]
+
+        @pl.when(place >= 0)
+        def _():
+            value_ref[place] = quantize(fresh_ref[slot], older_ref[slot]).astype(jnp.bfloat16)
+            pltpu.make_async_copy(value_ref.at[place], out_hbm.at[place], sent.at[place]).start()
+
+    for e in range(EXPERTS):
+        pltpu.make_async_copy(value_ref.at[e], out_hbm.at[e], sent.at[e]).wait()
 
 
 def encode(updated, trainer_base, sync_ids, owner_map):
+    slots = updated.shape[0]
+    anywhere = pl.BlockSpec(memory_space=pl.ANY)
     return pl.pallas_call(
         encode_kernel,
-        in_specs=[pl.BlockSpec(memory_space=pl.ANY)] * 4,
-        out_specs=pl.BlockSpec(memory_space=pltpu.VMEM),
+        in_specs=[anywhere] * 4,
+        out_specs=anywhere,
         out_shape=jax.ShapeDtypeStruct((EXPERTS, ROWS, BLOCK), jnp.bfloat16),
         scratch_shapes=[
             pltpu.SMEM((EXPERTS,), jnp.int32),
             pltpu.SMEM((EXPERTS,), jnp.int32),
+            pltpu.SMEM((slots,), jnp.int32),
             pltpu.VMEM(updated.shape, jnp.bfloat16),
             pltpu.VMEM(updated.shape, jnp.bfloat16),
-            pltpu.SemaphoreType.DMA((2, updated.shape[0])),
+            pltpu.VMEM((EXPERTS, ROWS, BLOCK), jnp.bfloat16),
+            pltpu.SemaphoreType.DMA((2, slots)),
             pltpu.SemaphoreType.DMA((2,)),
+            pltpu.SemaphoreType.DMA((EXPERTS,)),
         ],
         name="encode",
     )(sync_ids, owner_map, updated, trainer_base)

time: 64 us -> 63.5 us (level)
  no operation moved by 1% of the time
where the time goes in v5:
time: 63.5 us; the launch traced here: 63.1 us
  blocking collectives  28.5 us (45%)
  waiting for transfers between devices  12.7 us (20%)
  starting transfers between devices  12.4 us (20%)
  Pallas kernels  7.37 us (12%)
  local copies, waits for them, and re-layouts  2.08 us (3%)
    all_to_all x1, blocking collectives, exchange(): lax.all_to_all(values, ('rollout', 'shard'), split_axis=0, concat_axis=0,...  28.5 us
    ppermute x11, waiting for transfers between devices, shifted(): return lax.ppermute(block, 'rollout', pairs)  12.7 us
    ppermute x11, starting transfers between devices, shifted(): return lax.ppermute(block, 'rollout', pairs)  12.4 us
    pallas_call x1, Pallas kernels, encode(): pl.pallas_call(encode_kernel, in_specs=[anywhere] * 4, out_specs=anywhere...  3.36 us
    pallas_call x1, Pallas kernels, add(): pl.pallas_call(functools.partial(add_kernel, spans), grid=(OWNED // BAND,...  2.79 us
    unnamed x2, local copies, waits for them, and re-layouts  2.04 us
  transfers between devices with their start and end apart: 11, of which 5 were waited for; matrix products, arithmetic and copies ran while one was open for 0% of the time, Pallas kernels for 4%

profile of v5, /device:TPU:1, one launch (start us, length us, event | category | flops | bytes accessed | tf_op | source)
XLA Modules:
  0.0 63.1 jit_solution(12538205524443470119)
XLA Ops:
  0.0 3.4 %encode.1 = bf16[8,224,128]{2,1,0:T(8,128)(2,1)} custom-call(s32[8]{0:T(128)} %ids_hbm.1, s32[8]{0:T(128)} %owner_hbm.1, bf16[12,224,128]{2,1,0:T(8,128)(2,1)} %fresh_hbm.1, bf16[12,224,128]{2,1,0:T(8,128)(2,1)} %older_hbm.1), custom_call_target="tpu_custom_call" | custom-call | tf_op jit(solution)/shard_map/encode/pallas_call | solution.py:79
  3.4 28.5 %all_to_all.5 = bf16[32,56,128]{2,1,0:T(8,128)(2,1)S(1)} all-to-all(bf16[32,56,128]{2,1,0:T(8,128)(2,1)} %bitcast.14), channel_id=1, replica_groups={{0,1,2,3,4,5,6,7,40,41,42,43,44,45,46,47,48,49,50,51,52,53,54,55,24,25,..., dimensions={0} | all-to-all | bytes 917504 | tf_op jit(solution)/shard_map/all_to_all | solution.py:110
  31.9 0.9 %collective-permute-start.1 = (bf16[1792,128]{1,0:T(8,128)(2,1)S(1)}, bf16[1792,128]{1,0:T(8,128)(2,1)S(1)}, u32[]{:S(2)}, u32[]{:S(2)}) collective-permute-start(bf16[1792,128]{1,0:T(8,128)(2,1)S(1)} %bitcast.13), channel_id=1, source_target_pairs={{0,32},{32,0},{64,96},{96,64},{128,160},{160,128},{192,224},{224,1... | collective-permute-start | bytes 1376264 | tf_op jit(solution)/shard_map/ppermute | solution.py:120
  32.9 1.4 %collective-permute-start = (bf16[896,128]{1,0:T(8,128)(2,1)S(1)}, bf16[896,128]{1,0:T(8,128)(2,1)S(1)}, u32[]{:S(2)}, u32[]{:S(2)}) collective-permute-start(bf16[896,128]{1,0:T(8,128)(2,1)S(1)} %bitcast.10), channel_id=1, source_target_pairs={{0,64},{32,96},{64,128},{96,160},{128,192},{160,224},{192,0},{224,... | collective-permute-start | bytes 688136 | tf_op jit(solution)/shard_map/ppermute | solution.py:120
  34.3 1.5 %collective-permute-start.4 = (bf16[896,128]{1,0:T(8,128)(2,1)S(1)}, bf16[896,128]{1,0:T(8,128)(2,1)S(1)}, u32[]{:S(2)}, u32[]{:S(2)}) collective-permute-start(bf16[896,128]{1,0:T(8,128)(2,1)S(1)} %bitcast.7), channel_id=1, source_target_pairs={{0,192},{32,224},{64,0},{96,32},{128,64},{160,96},{192,128},{224,1... | collective-permute-start | bytes 688136 | tf_op jit(solution)/shard_map/ppermute | solution.py:120
  35.8 1.4 %collective-permute-start.3 = (bf16[896,128]{1,0:T(8,128)(2,1)S(1)}, bf16[896,128]{1,0:T(8,128)(2,1)S(1)}, u32[]{:S(2)}, u32[]{:S(2)}) collective-permute-start(bf16[896,128]{1,0:T(8,128)(2,1)S(1)} %bitcast.11), channel_id=1, source_target_pairs={{0,192},{32,224},{64,0},{96,32},{128,64},{160,96},{192,128},{224,1... | collective-permute-start | bytes 688136 | tf_op jit(solution)/shard_map/ppermute | solution.py:120
  37.2 0.1 collective-permute-start.2
  37.3 4.3 %collective-permute-done.refs_2_ = bf16[896,128]{1,0:T(8,128)(2,1)S(1)} collective-permute-done((bf16[896,128]{1,0:T(8,128)(2,1)S(1)}, bf16[896,128]{1,0:T(8,128)(2,1)S(1)}, u32[]{:S(2)}, u32[]{:S(2)}) %collective-permute-start) | collective-permute-done | bytes 229408 | tf_op jit(solution)/shard_map/ppermute | solution.py:120
  41.6 0.0 collective-permute-start.5
  41.6 0.0 collective-permute-done.4.refs_5_
  41.6 2.6 %collective-permute-start.6 = (bf16[896,128]{1,0:T(8,128)(2,1)S(1)}, bf16[896,128]{1,0:T(8,128)(2,1)S(1)}, u32[]{:S(2)}, u32[]{:S(2)}) collective-permute-start(bf16[896,128]{1,0:T(8,128)(2,1)S(1)} %collective-permute-done.4.refs_5_), channel_id=1, source_target_pairs={{0,192},{32,224},{64,0},{96,32},{128,64},{160,96},{192,128},{224,1... | collective-permute-start | bytes 688136 | tf_op jit(solution)/shard_map/ppermute | solution.py:120
  44.2 2.0 %collective-permute-done.3.refs_4_ = bf16[896,128]{1,0:T(8,128)(2,1)S(1)} collective-permute-done((bf16[896,128]{1,0:T(8,128)(2,1)S(1)}, bf16[896,128]{1,0:T(8,128)(2,1)S(1)}, u32[]{:S(2)}, u32[]{:S(2)}) %collective-permute-start.3) | collective-permute-done | bytes 229408 | tf_op jit(solution)/shard_map/ppermute | solution.py:120
  46.2 0.0 collective-permute-done.1.refs_6_
  46.2 0.1 collective-permute-done.2.refs_3_
  46.3 1.2 %collective-permute-start.7 = (bf16[1792,128]{1,0:T(8,128)(2,1)S(1)}, bf16[1792,128]{1,0:T(8,128)(2,1)S(1)}, u32[]{:S(2)}, u32[]{:S(2)}) collective-permute-start(bf16[1792,128]{1,0:T(8,128)(2,1)S(1)} %collective-permute-done.1.refs_6_), channel_id=1, source_target_pairs={{0,64},{32,96},{64,128},{96,160},{128,192},{160,224},{192,0},{224,... | collective-permute-start | bytes 1376264 | tf_op jit(solution)/shard_map/ppermute | solution.py:120
  47.5 1.7 %collective-permute-start.8 = (bf16[1792,128]{1,0:T(8,128)(2,1)S(1)}, bf16[1792,128]{1,0:T(8,128)(2,1)S(1)}, u32[]{:S(2)}, u32[]{:S(2)}) collective-permute-start(bf16[1792,128]{1,0:T(8,128)(2,1)S(1)} %collective-permute-done.1.refs_6_), channel_id=1, source_target_pairs={{0,192},{32,224},{64,0},{96,32},{128,64},{160,96},{192,128},{224,1... | collective-permute-start | bytes 1376264 | tf_op jit(solution)/shard_map/ppermute | solution.py:120
  49.2 2.0 %collective-permute-done.5.refs_7_ = bf16[896,128]{1,0:T(8,128)(2,1)S(1)} collective-permute-done((bf16[896,128]{1,0:T(8,128)(2,1)S(1)}, bf16[896,128]{1,0:T(8,128)(2,1)S(1)}, u32[]{:S(2)}, u32[]{:S(2)}) %collective-permute-start.5) | collective-permute-done | bytes 229408 | tf_op jit(solution)/shard_map/ppermute | solution.py:120
  51.2 0.5 collective-permute-start.9
  51.7 0.0 collective-permute-done.6.refs_8_
  51.7 0.9 %collective-permute-start.10 = (bf16[896,128]{1,0:T(8,128)(2,1)S(1)}, bf16[896,128]{1,0:T(8,128)(2,1)S(1)}, u32[]{:S(2)}, u32[]{:S(2)}) collective-permute-start(bf16[896,128]{1,0:T(8,128)(2,1)S(1)} %collective-permute-done.6.refs_8_), channel_id=1, source_target_pairs={{0,32},{32,0},{64,96},{96,64},{128,160},{160,128},{192,224},{224,1... | collective-permute-start | bytes 688136 | tf_op jit(solution)/shard_map/ppermute | solution.py:120
  52.7 0.0 copy-start
  52.7 2.0 %copy-done = bf16[1,1792,1024]{2,1,0:T(8,128)(2,1)S(1)} copy-done((bf16[1,1792,1024]{2,1,0:T(8,128)(2,1)S(1)}, bf16[1,1792,1024]{2,1,0:T(8,128)(2,1)}, u32[]{:S(2)}) %copy-start) | copy-done | bytes 3670040
  54.7 2.8 %add.1 = (bf16[1792,1024]{1,0:T(8,128)(2,1)}, bf16[3,1792,128]{2,1,0:T(8,128)(2,1)S(1)}) custom-call(bf16[1792,1024]{1,0:T(8,128)(2,1)S(1)} %bitcast.6, bf16[896,128]{1,0:T(8,128)(2,1)S(1)} %bitcast.12, bf16[896,128]{1,0:T(8,128)(2,1)S(1)} %bitcast.9, bf16[896,128]{1,0:T(8,128)(2,1)S(1)} %collective-permute-done.refs_2_, ...), custom_call_target="tpu_custom_call" | custom-call | flops 1835008 | bytes 11010048 | tf_op jit(solution)/shard_map/add/pallas_call | solution.py:160
  57.5 0.0 collective-permute-done.9.refs_2_
  57.5 4.3 %collective-permute-done.10.refs_3_ = bf16[896,128]{1,0:T(8,128)(2,1)S(1)} collective-permute-done((bf16[896,128]{1,0:T(8,128)(2,1)S(1)}, bf16[896,128]{1,0:T(8,128)(2,1)S(1)}, u32[]{:S(2)}, u32[]{:S(2)}) %collective-permute-start.10) | collective-permute-done | bytes 229408 | tf_op jit(solution)/shard_map/ppermute | solution.py:120
  61.8 0.0 collective-permute-done.7.refs_0_
  61.8 0.0 collective-permute-done.8.refs_1_
  61.8 1.2 %finish.1 = bf16[1792,1024]{1,0:T(8,128)(2,1)} custom-call(bf16[3,1792,128]{2,1,0:T(8,128)(2,1)S(1)} %get-tuple-element.13.rest_ref, bf16[1792,128]{1,0:T(8,128)(2,1)S(1)} %collective-permute-done.7.refs_0_, bf16[1792,128]{1,0:T(8,128)(2,1)S(1)} %collective-permute-done.8.refs_1_, ...), custom_call_target="tpu_custom_call", output_to_operand_aliasing={{}: (5, {})} | custom-call | tf_op jit(solution)/shard_map/finish/pallas_call | solution.py:194
  (1 shorter events, 0.0 us)
Async XLA Ops:
  31.9 14.3 %collective-permute-start.1 = (bf16[1792,128]{1,0:T(8,128)(2,1)S(1)}, bf16[1792,128]{1,0:T(8,128)(2,1)S(1)}, u32[]{:S(2)}, u32[]{:S(2)}) collective-permute-start(bf16[1792,128]{1,0:T(8,128)(2,1)S(1)} %bitcast.13), channel_id=1, source_target_pairs={{0,32},{32,0},{64,96},{96,64},{128,160},{160,128},{192,224},{224,1... | collective-permute-start | bytes 1376264 | tf_op jit(solution)/shard_map/ppermute | solution.py:120
  32.9 8.7 %collective-permute-start = (bf16[896,128]{1,0:T(8,128)(2,1)S(1)}, bf16[896,128]{1,0:T(8,128)(2,1)S(1)}, u32[]{:S(2)}, u32[]{:S(2)}) collective-permute-start(bf16[896,128]{1,0:T(8,128)(2,1)S(1)} %bitcast.10), channel_id=1, source_target_pairs={{0,64},{32,96},{64,128},{96,160},{128,192},{160,224},{192,0},{224,... | collective-permute-start | bytes 688136 | tf_op jit(solution)/shard_map/ppermute | solution.py:120
  34.3 7.3 %collective-permute-start.4 = (bf16[896,128]{1,0:T(8,128)(2,1)S(1)}, bf16[896,128]{1,0:T(8,128)(2,1)S(1)}, u32[]{:S(2)}, u32[]{:S(2)}) collective-permute-start(bf16[896,128]{1,0:T(8,128)(2,1)S(1)} %bitcast.7), channel_id=1, source_target_pairs={{0,192},{32,224},{64,0},{96,32},{128,64},{160,96},{192,128},{224,1... | collective-permute-start | bytes 688136 | tf_op jit(solution)/shard_map/ppermute | solution.py:120
  35.8 10.4 %collective-permute-start.3 = (bf16[896,128]{1,0:T(8,128)(2,1)S(1)}, bf16[896,128]{1,0:T(8,128)(2,1)S(1)}, u32[]{:S(2)}, u32[]{:S(2)}) collective-permute-start(bf16[896,128]{1,0:T(8,128)(2,1)S(1)} %bitcast.11), channel_id=1, source_target_pairs={{0,192},{32,224},{64,0},{96,32},{128,64},{160,96},{192,128},{224,1... | collective-permute-start | bytes 688136 | tf_op jit(solution)/shard_map/ppermute | solution.py:120
  37.2 9.1 %collective-permute-start.2 = (bf16[896,128]{1,0:T(8,128)(2,1)S(1)}, bf16[896,128]{1,0:T(8,128)(2,1)S(1)}, u32[]{:S(2)}, u32[]{:S(2)}) collective-permute-start(bf16[896,128]{1,0:T(8,128)(2,1)S(1)} %bitcast.8), channel_id=1, source_target_pairs={{0,64},{32,96},{64,128},{96,160},{128,192},{160,224},{192,0},{224,... | collective-permute-start | bytes 688136 | tf_op jit(solution)/shard_map/ppermute | solution.py:120
  41.6 9.6 %collective-permute-start.5 = (bf16[896,128]{1,0:T(8,128)(2,1)S(1)}, bf16[896,128]{1,0:T(8,128)(2,1)S(1)}, u32[]{:S(2)}, u32[]{:S(2)}) collective-permute-start(bf16[896,128]{1,0:T(8,128)(2,1)S(1)} %collective-permute-done.refs_2_), channel_id=1, source_target_pairs={{0,64},{32,96},{64,128},{96,160},{128,192},{160,224},{192,0},{224,... | collective-permute-start | bytes 688136 | tf_op jit(solution)/shard_map/ppermute | solution.py:120
  41.6 10.1 %collective-permute-start.6 = (bf16[896,128]{1,0:T(8,128)(2,1)S(1)}, bf16[896,128]{1,0:T(8,128)(2,1)S(1)}, u32[]{:S(2)}, u32[]{:S(2)}) collective-permute-start(bf16[896,128]{1,0:T(8,128)(2,1)S(1)} %collective-permute-done.4.refs_5_), channel_id=1, source_target_pairs={{0,192},{32,224},{64,0},{96,32},{128,64},{160,96},{192,128},{224,1... | collective-permute-start | bytes 688136 | tf_op jit(solution)/shard_map/ppermute | solution.py:120
  46.3 15.5 %collective-permute-start.7 = (bf16[1792,128]{1,0:T(8,128)(2,1)S(1)}, bf16[1792,128]{1,0:T(8,128)(2,1)S(1)}, u32[]{:S(2)}, u32[]{:S(2)}) collective-permute-start(bf16[1792,128]{1,0:T(8,128)(2,1)S(1)} %collective-permute-done.1.refs_6_), channel_id=1, source_target_pairs={{0,64},{32,96},{64,128},{96,160},{128,192},{160,224},{192,0},{224,... | collective-permute-start | bytes 1376264 | tf_op jit(solution)/shard_map/ppermute | solution.py:120
  47.5 14.3 %collective-permute-start.8 = (bf16[1792,128]{1,0:T(8,128)(2,1)S(1)}, bf16[1792,128]{1,0:T(8,128)(2,1)S(1)}, u32[]{:S(2)}, u32[]{:S(2)}) collective-permute-start(bf16[1792,128]{1,0:T(8,128)(2,1)S(1)} %collective-permute-done.1.refs_6_), channel_id=1, source_target_pairs={{0,192},{32,224},{64,0},{96,32},{128,64},{160,96},{192,128},{224,1... | collective-permute-start | bytes 1376264 | tf_op jit(solution)/shard_map/ppermute | solution.py:120
  51.2 6.3 %collective-permute-start.9 = (bf16[896,128]{1,0:T(8,128)(2,1)S(1)}, bf16[896,128]{1,0:T(8,128)(2,1)S(1)}, u32[]{:S(2)}, u32[]{:S(2)}) collective-permute-start(bf16[896,128]{1,0:T(8,128)(2,1)S(1)} %collective-permute-done.5.refs_7_), channel_id=1, source_target_pairs={{0,32},{32,0},{64,96},{96,64},{128,160},{160,128},{192,224},{224,1... | collective-permute-start | bytes 688136 | tf_op jit(solution)/shard_map/ppermute | solution.py:120
  51.7 10.1 %collective-permute-start.10 = (bf16[896,128]{1,0:T(8,128)(2,1)S(1)}, bf16[896,128]{1,0:T(8,128)(2,1)S(1)}, u32[]{:S(2)}, u32[]{:S(2)}) collective-permute-start(bf16[896,128]{1,0:T(8,128)(2,1)S(1)} %collective-permute-done.6.refs_8_), channel_id=1, source_target_pairs={{0,32},{32,0},{64,96},{96,64},{128,160},{160,128},{192,224},{224,1... | collective-permute-start | bytes 688136 | tf_op jit(solution)/shard_map/ppermute | solution.py:120
  52.7 2.0 %copy-start = (bf16[1,1792,1024]{2,1,0:T(8,128)(2,1)S(1)}, bf16[1,1792,1024]{2,1,0:T(8,128)(2,1)}, u32[]{:S(2)}) copy-start(bf16[1,1792,1024]{2,1,0:T(8,128)(2,1)} %param.7) | copy-start | bytes 11010052

commit v6 on v5

--- a/solution.py
+++ b/solution.py
@@ -16,7 +16,7 @@
 BAND = 448
 SPLIT = 896
 FIRST = 5
-MOVES = [(0, 0), (-1, 0), (1, 0), (0, 1), (2, 0), (-1, 1), (1, 1), (2, 1)]
+MOVES = [(0, 0), (1, 0), (0, 1), (-1, 0), (2, 0), (-1, 1), (1, 1), (2, 1)]
 
 
 def floor_power(magnitude):
@@ -203,22 +203,45 @@
     )(rest, *parts, made)
 
 
+def join_kernel(a_ref, b_ref, below_ref, above_ref, whole_ref):
+    whole_ref[:SPLIT] = a_ref[...]
+    whole_ref[SPLIT:] = b_ref[...]
+
+
+def joined(a, b, below, above):
+    block = pl.BlockSpec(memory_space=pltpu.VMEM)
+    anywhere = pl.BlockSpec(memory_space=pl.ANY)
+    return pl.pallas_call(
+        join_kernel,
+        in_specs=[block, block, anywhere, anywhere],
+        out_specs=block,
+        out_shape=jax.ShapeDtypeStruct((OWNED, BLOCK), jnp.bfloat16),
+        compiler_params=pltpu.CompilerParams(vmem_limit_bytes=2 * 2**20),
+        name="joined",
+    )(a, b, below, above)
+
+
 def gather(own):
     own_a, own_b = own[:SPLIT], own[SPLIT:]
     below_a, above_b = shifted(own_a, dy=1), shifted(own_b, dy=-1)
-    beside = shifted(own, dz=1)
+    beside_a, beside_b = shifted(own_a, dz=1), shifted(own_b, dz=1)
     below_b, above_a = shifted(own_b, dy=1), shifted(own_a, dy=-1)
     far_a, far_b = shifted(below_a, dy=1), shifted(above_b, dy=-1)
-    up, below_b = lax.optimization_barrier((beside, below_b))
-    down, above_a = lax.optimization_barrier((beside, above_a))
-    bb, ba = shifted(up, dy=1), shifted(down, dy=-1)
+    beside = joined(beside_a, beside_b, below_b, above_a)
+    bb, ba = shifted(beside, dy=1), shifted(beside, dy=-1)
     fz_a, fz_b = shifted(far_a, dz=1), shifted(far_b, dz=1)
-    parts = [[own_a, own_b], [below_a, below_b], [above_a, above_b], [beside], [far_a, far_b], [bb], [ba], [fz_a, fz_b]]
-    spans = []
-    for pieces in parts:
-        ends = [sum(piece.shape[0] for piece in pieces[:n]) for n in range(len(pieces) + 1)]
-        spans.append(list(zip(ends[:-1], ends[1:])))
-    return parts, spans
+    parts = [
+        [(own_a, 0), (own_b, SPLIT)],
+        [(above_a, 0), (above_b, SPLIT)],
+        [(beside, 0)],
+        [(below_a, 0), (below_b, SPLIT)],
+        [(far_a, 0), (far_b, SPLIT)],
+        [(bb, 0)],
+        [(ba, 0)],
+        [(fz_a, 0), (fz_b, SPLIT)],
+    ]
+    spans = [[(start, start + piece.shape[0]) for piece, start in pieces] for pieces in parts]
+    return [[piece for piece, _ in pieces] for pieces in parts], spans
 
 
 def per_device(updated, trainer_base, rollout_base, sync_ids, owner_map):

time: 63.5 us -> 62.8 us (0.989)
  waiting for transfers between devices: 12.7 us -> 12 us
    ppermute x11 -> x12, waiting for transfers between devices: 12.7 us -> 12 us  [shifted(): return lax.ppermute(block, 'rollout', pairs)]
    ppermute x11 -> x12, starting transfers between devices: 12.4 us -> 12.1 us  [shifted(): return lax.ppermute(block, 'rollout', pairs)]
  transfers between devices with their start and end apart: 11 -> 12, of which waited for: 5 -> 7; matrix products, arithmetic and copies ran while one was open for 0% -> 0% of each run, Pallas kernels for 4% -> 5%
where the time goes in v6:
time: 62.8 us; the launch traced here: 62.2 us
  blocking collectives  28.5 us (45%)
  starting transfers between devices  12.1 us (19%)
  waiting for transfers between devices  12 us (19%)
  Pallas kernels  7.41 us (12%)
  local copies, waits for them, and re-layouts  2.08 us (3%)
    all_to_all x1, blocking collectives, exchange(): lax.all_to_all(values, ('rollout', 'shard'), split_axis=0, concat_axis=0,...  28.5 us
    ppermute x12, starting transfers between devices, shifted(): return lax.ppermute(block, 'rollout', pairs)  12.1 us
    ppermute x12, waiting for transfers between devices, shifted(): return lax.ppermute(block, 'rollout', pairs)  12 us
    pallas_call x1, Pallas kernels, encode(): pl.pallas_call(encode_kernel, in_specs=[anywhere] * 4, out_specs=anywhere...  3.37 us
    pallas_call x1, Pallas kernels, add(): pl.pallas_call(functools.partial(add_kernel, spans), grid=(OWNED // BAND,...  2.79 us
    unnamed x2, local copies, waits for them, and re-layouts  2.04 us
  transfers between devices with their start and end apart: 12, of which 7 were waited for; matrix products, arithmetic and copies ran while one was open for 0% of the time, Pallas kernels for 5%

profile of v6, /device:TPU:1, one launch (start us, length us, event | category | flops | bytes accessed | tf_op | source)
XLA Modules:
  0.0 62.2 jit_solution(11237120173237580584)
XLA Ops:
  0.0 3.4 %encode.1 = bf16[8,224,128]{2,1,0:T(8,128)(2,1)} custom-call(s32[8]{0:T(128)} %ids_hbm.1, s32[8]{0:T(128)} %owner_hbm.1, bf16[12,224,128]{2,1,0:T(8,128)(2,1)} %fresh_hbm.1, bf16[12,224,128]{2,1,0:T(8,128)(2,1)} %older_hbm.1), custom_call_target="tpu_custom_call" | custom-call | tf_op jit(solution)/shard_map/encode/pallas_call | solution.py:79
  3.4 28.5 %all_to_all.5 = bf16[32,56,128]{2,1,0:T(8,128)(2,1)S(1)} all-to-all(bf16[32,56,128]{2,1,0:T(8,128)(2,1)} %bitcast.14), channel_id=1, replica_groups={{0,1,2,3,4,5,6,7,40,41,42,43,44,45,46,47,48,49,50,51,52,53,54,55,24,25,..., dimensions={0} | all-to-all | bytes 917504 | tf_op jit(solution)/shard_map/all_to_all | solution.py:110
  32.0 1.4 %collective-permute-start.5 = (bf16[896,128]{1,0:T(8,128)(2,1)S(1)}, bf16[896,128]{1,0:T(8,128)(2,1)S(1)}, u32[]{:S(2)}, u32[]{:S(2)}) collective-permute-start(bf16[896,128]{1,0:T(8,128)(2,1)S(1)} %bitcast.10), channel_id=1, source_target_pairs={{0,64},{32,96},{64,128},{96,160},{128,192},{160,224},{192,0},{224,... | collective-permute-start | bytes 688136 | tf_op jit(solution)/shard_map/ppermute | solution.py:120
  33.3 0.9 %collective-permute-start.2 = (bf16[896,128]{1,0:T(8,128)(2,1)S(1)}, bf16[896,128]{1,0:T(8,128)(2,1)S(1)}, u32[]{:S(2)}, u32[]{:S(2)}) collective-permute-start(bf16[896,128]{1,0:T(8,128)(2,1)S(1)} %bitcast.11), channel_id=1, source_target_pairs={{0,32},{32,0},{64,96},{96,64},{128,160},{160,128},{192,224},{224,1... | collective-permute-start | bytes 688136 | tf_op jit(solution)/shard_map/ppermute | solution.py:120
  34.3 1.5 %collective-permute-start.1 = (bf16[896,128]{1,0:T(8,128)(2,1)S(1)}, bf16[896,128]{1,0:T(8,128)(2,1)S(1)}, u32[]{:S(2)}, u32[]{:S(2)}) collective-permute-start(bf16[896,128]{1,0:T(8,128)(2,1)S(1)} %bitcast.6), channel_id=1, source_target_pairs={{0,192},{32,224},{64,0},{96,32},{128,64},{160,96},{192,128},{224,1... | collective-permute-start | bytes 688136 | tf_op jit(solution)/shard_map/ppermute | solution.py:120
  35.8 1.4 %collective-permute-start = (bf16[896,128]{1,0:T(8,128)(2,1)S(1)}, bf16[896,128]{1,0:T(8,128)(2,1)S(1)}, u32[]{:S(2)}, u32[]{:S(2)}) collective-permute-start(bf16[896,128]{1,0:T(8,128)(2,1)S(1)} %bitcast.12), channel_id=1, source_target_pairs={{0,192},{32,224},{64,0},{96,32},{128,64},{160,96},{192,128},{224,1... | collective-permute-start | bytes 688136 | tf_op jit(solution)/shard_map/ppermute | solution.py:120
  37.2 0.1 collective-permute-start.4
  37.3 3.6 %collective-permute-done.5.refs_5_ = bf16[896,128]{1,0:T(8,128)(2,1)S(1)} collective-permute-done((bf16[896,128]{1,0:T(8,128)(2,1)S(1)}, bf16[896,128]{1,0:T(8,128)(2,1)S(1)}, u32[]{:S(2)}, u32[]{:S(2)}) %collective-permute-start.5) | collective-permute-done | bytes 229408 | tf_op jit(solution)/shard_map/ppermute | solution.py:120
  40.9 0.9 %collective-permute-start.3 = (bf16[896,128]{1,0:T(8,128)(2,1)S(1)}, bf16[896,128]{1,0:T(8,128)(2,1)S(1)}, u32[]{:S(2)}, u32[]{:S(2)}) collective-permute-start(bf16[896,128]{1,0:T(8,128)(2,1)S(1)} %bitcast.8), channel_id=1, source_target_pairs={{0,32},{32,0},{64,96},{96,64},{128,160},{160,128},{192,224},{224,1... | collective-permute-start | bytes 688136 | tf_op jit(solution)/shard_map/ppermute | solution.py:120
  41.9 0.0 collective-permute-done.2.a_ref
  41.9 0.1 collective-permute-start.6
  41.9 0.0 collective-permute-done.1.refs_3_
  41.9 2.6 %collective-permute-start.7 = (bf16[896,128]{1,0:T(8,128)(2,1)S(1)}, bf16[896,128]{1,0:T(8,128)(2,1)S(1)}, u32[]{:S(2)}, u32[]{:S(2)}) collective-permute-start(bf16[896,128]{1,0:T(8,128)(2,1)S(1)} %collective-permute-done.1.refs_3_), channel_id=1, source_target_pairs={{0,192},{32,224},{64,0},{96,32},{128,64},{160,96},{192,128},{224,1... | collective-permute-start | bytes 688136 | tf_op jit(solution)/shard_map/ppermute | solution.py:120
  44.5 1.7 %collective-permute-done.above_ref.refs_2_ = bf16[896,128]{1,0:T(8,128)(2,1)S(1)} collective-permute-done((bf16[896,128]{1,0:T(8,128)(2,1)S(1)}, bf16[896,128]{1,0:T(8,128)(2,1)S(1)}, u32[]{:S(2)}, u32[]{:S(2)}) %collective-permute-start) | collective-permute-done | bytes 229408 | tf_op jit(solution)/shard_map/ppermute | solution.py:120
  46.2 0.0 collective-permute-done.4.below_ref.refs_6_
  46.2 1.5 %collective-permute-done.3.b_ref = bf16[896,128]{1,0:T(8,128)(2,1)S(1)} collective-permute-done((bf16[896,128]{1,0:T(8,128)(2,1)S(1)}, bf16[896,128]{1,0:T(8,128)(2,1)S(1)}, u32[]{:S(2)}, u32[]{:S(2)}) %collective-permute-start.3) | collective-permute-done | bytes 229408 | tf_op jit(solution)/shard_map/ppermute | solution.py:120
  47.7 1.5 %collective-permute-start.9 = (bf16[1792,128]{1,0:T(8,128)(2,1)S(1)}, bf16[1792,128]{1,0:T(8,128)(2,1)S(1)}, u32[]{:S(2)}, u32[]{:S(2)}) collective-permute-start(bf16[1792,128]{1,0:T(8,128)(2,1)S(1)} %joined.1.refs_4_), channel_id=1, source_target_pairs={{0,192},{32,224},{64,0},{96,32},{128,64},{160,96},{192,128},{224,1... | collective-permute-start | bytes 1376264 | tf_op jit(solution)/shard_map/ppermute | solution.py:120
  49.3 0.0 collective-permute-start.8
  49.3 0.7 %collective-permute-done.6.refs_7_ = bf16[896,128]{1,0:T(8,128)(2,1)S(1)} collective-permute-done((bf16[896,128]{1,0:T(8,128)(2,1)S(1)}, bf16[896,128]{1,0:T(8,128)(2,1)S(1)}, u32[]{:S(2)}, u32[]{:S(2)}) %collective-permute-start.6) | collective-permute-done | bytes 229408 | tf_op jit(solution)/shard_map/ppermute | solution.py:120
  50.0 1.1 %collective-permute-start.10 = (bf16[896,128]{1,0:T(8,128)(2,1)S(1)}, bf16[896,128]{1,0:T(8,128)(2,1)S(1)}, u32[]{:S(2)}, u32[]{:S(2)}) collective-permute-start(bf16[896,128]{1,0:T(8,128)(2,1)S(1)} %collective-permute-done.6.refs_7_), channel_id=1, source_target_pairs={{0,32},{32,0},{64,96},{96,64},{128,160},{160,128},{192,224},{224,1... | collective-permute-start | bytes 688136 | tf_op jit(solution)/shard_map/ppermute | solution.py:120
  51.0 0.1 collective-permute-done.7.refs_8_
  51.1 0.5 collective-permute-start.11
  51.7 0.0 copy-start
  51.7 2.0 %copy-done = bf16[1,1792,1024]{2,1,0:T(8,128)(2,1)S(1)} copy-done((bf16[1,1792,1024]{2,1,0:T(8,128)(2,1)S(1)}, bf16[1,1792,1024]{2,1,0:T(8,128)(2,1)}, u32[]{:S(2)}) %copy-start) | copy-done | bytes 3670040
  53.7 2.8 %add.1 = (bf16[1792,1024]{1,0:T(8,128)(2,1)}, bf16[3,1792,128]{2,1,0:T(8,128)(2,1)S(1)}) custom-call(bf16[1792,1024]{1,0:T(8,128)(2,1)S(1)} %bitcast.5, bf16[896,128]{1,0:T(8,128)(2,1)S(1)} %bitcast.13, bf16[896,128]{1,0:T(8,128)(2,1)S(1)} %bitcast.9, bf16[896,128]{1,0:T(8,128)(2,1)S(1)} %collective-permute-done.above_ref.refs_2_, ...), custom_call_target="tpu_custom_call" | custom-call | flops 1835008 | bytes 11010048 | tf_op jit(solution)/shard_map/add/pallas_call | solution.py:160
  56.5 0.0 collective-permute-done.10.refs_2_
  56.5 4.1 %collective-permute-done.11.refs_3_ = bf16[896,128]{1,0:T(8,128)(2,1)S(1)} collective-permute-done((bf16[896,128]{1,0:T(8,128)(2,1)S(1)}, bf16[896,128]{1,0:T(8,128)(2,1)S(1)}, u32[]{:S(2)}, u32[]{:S(2)}) %collective-permute-start.11) | collective-permute-done | bytes 229408 | tf_op jit(solution)/shard_map/ppermute | solution.py:120
  60.6 0.3 collective-permute-done.9.refs_1_
  61.0 0.0 collective-permute-done.8.refs_0_
  61.0 1.2 %finish.1 = bf16[1792,1024]{1,0:T(8,128)(2,1)} custom-call(bf16[3,1792,128]{2,1,0:T(8,128)(2,1)S(1)} %get-tuple-element.7.rest_ref, bf16[1792,128]{1,0:T(8,128)(2,1)S(1)} %collective-permute-done.8.refs_0_, bf16[1792,128]{1,0:T(8,128)(2,1)S(1)} %collective-permute-done.9.refs_1_, ...), custom_call_target="tpu_custom_call", output_to_operand_aliasing={{}: (5, {})} | custom-call | tf_op jit(solution)/shard_map/finish/pallas_call | solution.py:194
  (2 shorter events, 0.1 us)
Async XLA Ops:
  32.0 9.0 %collective-permute-start.5 = (bf16[896,128]{1,0:T(8,128)(2,1)S(1)}, bf16[896,128]{1,0:T(8,128)(2,1)S(1)}, u32[]{:S(2)}, u32[]{:S(2)}) collective-permute-start(bf16[896,128]{1,0:T(8,128)(2,1)S(1)} %bitcast.10), channel_id=1, source_target_pairs={{0,64},{32,96},{64,128},{96,160},{128,192},{160,224},{192,0},{224,... | collective-permute-start | bytes 688136 | tf_op jit(solution)/shard_map/ppermute | solution.py:120
  33.3 8.5 %collective-permute-start.2 = (bf16[896,128]{1,0:T(8,128)(2,1)S(1)}, bf16[896,128]{1,0:T(8,128)(2,1)S(1)}, u32[]{:S(2)}, u32[]{:S(2)}) collective-permute-start(bf16[896,128]{1,0:T(8,128)(2,1)S(1)} %bitcast.11), channel_id=1, source_target_pairs={{0,32},{32,0},{64,96},{96,64},{128,160},{160,128},{192,224},{224,1... | collective-permute-start | bytes 688136 | tf_op jit(solution)/shard_map/ppermute | solution.py:120
  34.3 7.6 %collective-permute-start.1 = (bf16[896,128]{1,0:T(8,128)(2,1)S(1)}, bf16[896,128]{1,0:T(8,128)(2,1)S(1)}, u32[]{:S(2)}, u32[]{:S(2)}) collective-permute-start(bf16[896,128]{1,0:T(8,128)(2,1)S(1)} %bitcast.6), channel_id=1, source_target_pairs={{0,192},{32,224},{64,0},{96,32},{128,64},{160,96},{192,128},{224,1... | collective-permute-start | bytes 688136 | tf_op jit(solution)/shard_map/ppermute | solution.py:120
  35.8 10.4 %collective-permute-start = (bf16[896,128]{1,0:T(8,128)(2,1)S(1)}, bf16[896,128]{1,0:T(8,128)(2,1)S(1)}, u32[]{:S(2)}, u32[]{:S(2)}) collective-permute-start(bf16[896,128]{1,0:T(8,128)(2,1)S(1)} %bitcast.12), channel_id=1, source_target_pairs={{0,192},{32,224},{64,0},{96,32},{128,64},{160,96},{192,128},{224,1... | collective-permute-start | bytes 688136 | tf_op jit(solution)/shard_map/ppermute | solution.py:120
  37.2 9.0 %collective-permute-start.4 = (bf16[896,128]{1,0:T(8,128)(2,1)S(1)}, bf16[896,128]{1,0:T(8,128)(2,1)S(1)}, u32[]{:S(2)}, u32[]{:S(2)}) collective-permute-start(bf16[896,128]{1,0:T(8,128)(2,1)S(1)} %bitcast.7), channel_id=1, source_target_pairs={{0,64},{32,96},{64,128},{96,160},{128,192},{160,224},{192,0},{224,... | collective-permute-start | bytes 688136 | tf_op jit(solution)/shard_map/ppermute | solution.py:120
  40.9 6.8 %collective-permute-start.3 = (bf16[896,128]{1,0:T(8,128)(2,1)S(1)}, bf16[896,128]{1,0:T(8,128)(2,1)S(1)}, u32[]{:S(2)}, u32[]{:S(2)}) collective-permute-start(bf16[896,128]{1,0:T(8,128)(2,1)S(1)} %bitcast.8), channel_id=1, source_target_pairs={{0,32},{32,0},{64,96},{96,64},{128,160},{160,128},{192,224},{224,1... | collective-permute-start | bytes 688136 | tf_op jit(solution)/shard_map/ppermute | solution.py:120
  41.9 8.1 %collective-permute-start.6 = (bf16[896,128]{1,0:T(8,128)(2,1)S(1)}, bf16[896,128]{1,0:T(8,128)(2,1)S(1)}, u32[]{:S(2)}, u32[]{:S(2)}) collective-permute-start(bf16[896,128]{1,0:T(8,128)(2,1)S(1)} %collective-permute-done.5.refs_5_), channel_id=1, source_target_pairs={{0,64},{32,96},{64,128},{96,160},{128,192},{160,224},{192,0},{224,... | collective-permute-start | bytes 688136 | tf_op jit(solution)/shard_map/ppermute | solution.py:120
  41.9 9.2 %collective-permute-start.7 = (bf16[896,128]{1,0:T(8,128)(2,1)S(1)}, bf16[896,128]{1,0:T(8,128)(2,1)S(1)}, u32[]{:S(2)}, u32[]{:S(2)}) collective-permute-start(bf16[896,128]{1,0:T(8,128)(2,1)S(1)} %collective-permute-done.1.refs_3_), channel_id=1, source_target_pairs={{0,192},{32,224},{64,0},{96,32},{128,64},{160,96},{192,128},{224,1... | collective-permute-start | bytes 688136 | tf_op jit(solution)/shard_map/ppermute | solution.py:120
  47.7 13.2 %collective-permute-start.9 = (bf16[1792,128]{1,0:T(8,128)(2,1)S(1)}, bf16[1792,128]{1,0:T(8,128)(2,1)S(1)}, u32[]{:S(2)}, u32[]{:S(2)}) collective-permute-start(bf16[1792,128]{1,0:T(8,128)(2,1)S(1)} %joined.1.refs_4_), channel_id=1, source_target_pairs={{0,192},{32,224},{64,0},{96,32},{128,64},{160,96},{192,128},{224,1... | collective-permute-start | bytes 1376264 | tf_op jit(solution)/shard_map/ppermute | solution.py:120
  49.3 11.7 %collective-permute-start.8 = (bf16[1792,128]{1,0:T(8,128)(2,1)S(1)}, bf16[1792,128]{1,0:T(8,128)(2,1)S(1)}, u32[]{:S(2)}, u32[]{:S(2)}) collective-permute-start(bf16[1792,128]{1,0:T(8,128)(2,1)S(1)} %joined.1.refs_4_), channel_id=1, source_target_pairs={{0,64},{32,96},{64,128},{96,160},{128,192},{160,224},{192,0},{224,... | collective-permute-start | bytes 1376264 | tf_op jit(solution)/shard_map/ppermute | solution.py:120
  50.0 6.5 %collective-permute-start.10 = (bf16[896,128]{1,0:T(8,128)(2,1)S(1)}, bf16[896,128]{1,0:T(8,128)(2,1)S(1)}, u32[]{:S(2)}, u32[]{:S(2)}) collective-permute-start(bf16[896,128]{1,0:T(8,128)(2,1)S(1)} %collective-permute-done.6.refs_7_), channel_id=1, source_target_pairs={{0,32},{32,0},{64,96},{96,64},{128,160},{160,128},{192,224},{224,1... | collective-permute-start | bytes 688136 | tf_op jit(solution)/shard_map/ppermute | solution.py:120
  51.1 9.5 %collective-permute-start.11 = (bf16[896,128]{1,0:T(8,128)(2,1)S(1)}, bf16[896,128]{1,0:T(8,128)(2,1)S(1)}, u32[]{:S(2)}, u32[]{:S(2)}) collective-permute-start(bf16[896,128]{1,0:T(8,128)(2,1)S(1)} %collective-permute-done.7.refs_8_), channel_id=1, source_target_pairs={{0,32},{32,0},{64,96},{96,64},{128,160},{160,128},{192,224},{224,1... | collective-permute-start | bytes 688136 | tf_op jit(solution)/shard_map/ppermute | solution.py:120
  51.7 2.0 %copy-start = (bf16[1,1792,1024]{2,1,0:T(8,128)(2,1)S(1)}, bf16[1,1792,1024]{2,1,0:T(8,128)(2,1)}, u32[]{:S(2)}) copy-start(bf16[1,1792,1024]{2,1,0:T(8,128)(2,1)} %param.7) | copy-start | bytes 11010052

commit v7 on v6

--- a/solution.py
+++ b/solution.py
@@ -16,28 +16,28 @@
 BAND = 448
 SPLIT = 896
 FIRST = 5
-MOVES = [(0, 0), (1, 0), (0, 1), (-1, 0), (2, 0), (-1, 1), (1, 1), (2, 1)]
-
-
-def floor_power(magnitude):
+MOVES = [(0, 0), (1, 0), (0, 1), (-1, 0), (2, 0), (1, 1), (-1, 1), (2, 1)]
+
+
+def leading(magnitude):
     spread = magnitude * (2.0**23 + 1.0)
-    power = spread - (spread - magnitude)
-    return jnp.where(power > magnitude, power * 0.5, power)
+    return spread - (spread - magnitude)
 
 
 def quantize(fresh, older):
     delta = fresh.astype(jnp.float32) - older.astype(jnp.float32)
     magnitude = jnp.abs(delta)
     largest = jnp.max(magnitude, axis=-1, keepdims=True)
-    power = floor_power(largest)
-    scale = jnp.where(largest > 1.75 * power, power * 2.0**-7, power * 2.0**-8)
-    scale = jnp.maximum(scale, 2.0**-24)
-    binade = jnp.maximum(floor_power(magnitude), scale * 2.0**-6)
+    power = leading(largest)
+    least = jnp.where(largest > 0.875 * power, power * 2.0**-14, power * 2.0**-15)
+    least = jnp.maximum(least, 2.0**-30)
+    power = leading(magnitude)
+    binade = jnp.maximum(jnp.where(power > magnitude, power * 0.5, power), least)
     shift = binade * (1.5 * 2.0**20)
-    rounded = (magnitude + shift) - shift
-    tie = (magnitude - rounded) >= binade * 2.0**-4
-    rounded = jnp.where(tie, rounded + binade * 2.0**-3, rounded)
-    return jnp.where(delta < 0.0, -rounded, rounded)
+    rounded = (delta + shift) - shift
+    error = delta - rounded
+    short = (magnitude - jnp.abs(rounded)) >= binade * 2.0**-4
+    return jnp.where(short, delta + error, rounded)
 
 
 def encode_kernel(ids_hbm, owner_hbm, fresh_hbm, older_hbm, out_hbm, ids_ref, owner_ref, place_ref, fresh_ref, older_ref, value_ref, sems, few, sent):
@@ -236,8 +236,8 @@
         [(beside, 0)],
         [(below_a, 0), (below_b, SPLIT)],
         [(far_a, 0), (far_b, SPLIT)],
+        [(ba, 0)],
         [(bb, 0)],
-        [(ba, 0)],
         [(fz_a, 0), (fz_b, SPLIT)],
     ]
     spans = [[(start, start + piece.shape[0]) for piece, start in pieces] for pieces in parts]

time: 62.8 us -> 62.4 us (level)
  waiting for transfers between devices: 12 us -> 10.7 us
  starting transfers between devices: 12.1 us -> 13.2 us
    ppermute x12, waiting for transfers between devices: 12 us -> 10.7 us  [shifted(): return lax.ppermute(block, 'rollout', pairs)]
    ppermute x12, starting transfers between devices: 12.1 us -> 13.2 us  [shifted(): return lax.ppermute(block, 'rollout', pairs)]
  transfers between devices with their start and end apart: 12 -> 12, of which waited for: 7 -> 4; matrix products, arithmetic and copies ran while one was open for 0% -> 0% of each run, Pallas kernels for 5% -> 5%
where the time goes in v7:
time: 62.4 us; the launch traced here: 61.7 us
  blocking collectives  28.5 us (46%)
  starting transfers between devices  13.2 us (21%)
  waiting for transfers between devices  10.7 us (17%)
  Pallas kernels  7.19 us (12%)
  local copies, waits for them, and re-layouts  2.08 us (3%)
    all_to_all x1, blocking collectives, exchange(): lax.all_to_all(values, ('rollout', 'shard'), split_axis=0, concat_axis=0,...  28.5 us
    ppermute x12, starting transfers between devices, shifted(): return lax.ppermute(block, 'rollout', pairs)  13.2 us
    ppermute x12, waiting for transfers between devices, shifted(): return lax.ppermute(block, 'rollout', pairs)  10.7 us
    pallas_call x1, Pallas kernels, encode(): pl.pallas_call(encode_kernel, in_specs=[anywhere] * 4, out_specs=anywhere...  3.15 us
    pallas_call x1, Pallas kernels, add(): pl.pallas_call(functools.partial(add_kernel, spans), grid=(OWNED // BAND,...  2.79 us
    unnamed x2, local copies, waits for them, and re-layouts  2.04 us
  transfers between devices with their start and end apart: 12, of which 4 were waited for; matrix products, arithmetic and copies ran while one was open for 0% of the time, Pallas kernels for 5%

profile of v7, /device:TPU:1, one launch (start us, length us, event | category | flops | bytes accessed | tf_op | source)
XLA Modules:
  0.0 61.7 jit_solution(12094694203085996613)
XLA Ops:
  0.0 3.2 %encode.1 = bf16[8,224,128]{2,1,0:T(8,128)(2,1)} custom-call(s32[8]{0:T(128)} %ids_hbm.1, s32[8]{0:T(128)} %owner_hbm.1, bf16[12,224,128]{2,1,0:T(8,128)(2,1)} %fresh_hbm.1, bf16[12,224,128]{2,1,0:T(8,128)(2,1)} %older_hbm.1), custom_call_target="tpu_custom_call" | custom-call | tf_op jit(solution)/shard_map/encode/pallas_call | solution.py:79
  3.2 28.5 %all_to_all.5 = bf16[32,56,128]{2,1,0:T(8,128)(2,1)S(1)} all-to-all(bf16[32,56,128]{2,1,0:T(8,128)(2,1)} %bitcast.14), channel_id=1, replica_groups={{0,1,2,3,4,5,6,7,40,41,42,43,44,45,46,47,48,49,50,51,52,53,54,55,24,25,..., dimensions={0} | all-to-all | bytes 917504 | tf_op jit(solution)/shard_map/all_to_all | solution.py:110
  31.7 1.4 %collective-permute-start.5 = (bf16[896,128]{1,0:T(8,128)(2,1)S(1)}, bf16[896,128]{1,0:T(8,128)(2,1)S(1)}, u32[]{:S(2)}, u32[]{:S(2)}) collective-permute-start(bf16[896,128]{1,0:T(8,128)(2,1)S(1)} %bitcast.10), channel_id=1, source_target_pairs={{0,64},{32,96},{64,128},{96,160},{128,192},{160,224},{192,0},{224,... | collective-permute-start | bytes 688136 | tf_op jit(solution)/shard_map/ppermute | solution.py:120
  33.1 0.9 %collective-permute-start.2 = (bf16[896,128]{1,0:T(8,128)(2,1)S(1)}, bf16[896,128]{1,0:T(8,128)(2,1)S(1)}, u32[]{:S(2)}, u32[]{:S(2)}) collective-permute-start(bf16[896,128]{1,0:T(8,128)(2,1)S(1)} %bitcast.11), channel_id=1, source_target_pairs={{0,32},{32,0},{64,96},{96,64},{128,160},{160,128},{192,224},{224,1... | collective-permute-start | bytes 688136 | tf_op jit(solution)/shard_map/ppermute | solution.py:120
  34.1 1.5 %collective-permute-start.1 = (bf16[896,128]{1,0:T(8,128)(2,1)S(1)}, bf16[896,128]{1,0:T(8,128)(2,1)S(1)}, u32[]{:S(2)}, u32[]{:S(2)}) collective-permute-start(bf16[896,128]{1,0:T(8,128)(2,1)S(1)} %bitcast.6), channel_id=1, source_target_pairs={{0,192},{32,224},{64,0},{96,32},{128,64},{160,96},{192,128},{224,1... | collective-permute-start | bytes 688136 | tf_op jit(solution)/shard_map/ppermute | solution.py:120
  35.6 1.4 %collective-permute-start = (bf16[896,128]{1,0:T(8,128)(2,1)S(1)}, bf16[896,128]{1,0:T(8,128)(2,1)S(1)}, u32[]{:S(2)}, u32[]{:S(2)}) collective-permute-start(bf16[896,128]{1,0:T(8,128)(2,1)S(1)} %bitcast.12), channel_id=1, source_target_pairs={{0,192},{32,224},{64,0},{96,32},{128,64},{160,96},{192,128},{224,1... | collective-permute-start | bytes 688136 | tf_op jit(solution)/shard_map/ppermute | solution.py:120
  37.0 0.1 collective-permute-start.4
  37.1 3.6 %collective-permute-done.5.refs_5_ = bf16[896,128]{1,0:T(8,128)(2,1)S(1)} collective-permute-done((bf16[896,128]{1,0:T(8,128)(2,1)S(1)}, bf16[896,128]{1,0:T(8,128)(2,1)S(1)}, u32[]{:S(2)}, u32[]{:S(2)}) %collective-permute-start.5) | collective-permute-done | bytes 229408 | tf_op jit(solution)/shard_map/ppermute | solution.py:120
  40.7 0.9 %collective-permute-start.3 = (bf16[896,128]{1,0:T(8,128)(2,1)S(1)}, bf16[896,128]{1,0:T(8,128)(2,1)S(1)}, u32[]{:S(2)}, u32[]{:S(2)}) collective-permute-start(bf16[896,128]{1,0:T(8,128)(2,1)S(1)} %bitcast.8), channel_id=1, source_target_pairs={{0,32},{32,0},{64,96},{96,64},{128,160},{160,128},{192,224},{224,1... | collective-permute-start | bytes 688136 | tf_op jit(solution)/shard_map/ppermute | solution.py:120
  41.6 0.0 collective-permute-done.2.a_ref
  41.6 0.1 collective-permute-start.6
  41.7 0.0 collective-permute-done.1.refs_3_
  41.7 2.6 %collective-permute-start.7 = (bf16[896,128]{1,0:T(8,128)(2,1)S(1)}, bf16[896,128]{1,0:T(8,128)(2,1)S(1)}, u32[]{:S(2)}, u32[]{:S(2)}) collective-permute-start(bf16[896,128]{1,0:T(8,128)(2,1)S(1)} %collective-permute-done.1.refs_3_), channel_id=1, source_target_pairs={{0,192},{32,224},{64,0},{96,32},{128,64},{160,96},{192,128},{224,1... | collective-permute-start | bytes 688136 | tf_op jit(solution)/shard_map/ppermute | solution.py:120
  44.3 1.7 %collective-permute-done.above_ref.refs_2_ = bf16[896,128]{1,0:T(8,128)(2,1)S(1)} collective-permute-done((bf16[896,128]{1,0:T(8,128)(2,1)S(1)}, bf16[896,128]{1,0:T(8,128)(2,1)S(1)}, u32[]{:S(2)}, u32[]{:S(2)}) %collective-permute-start) | collective-permute-done | bytes 229408 | tf_op jit(solution)/shard_map/ppermute | solution.py:120
  46.0 0.0 collective-permute-done.4.below_ref.refs_6_
  46.0 1.5 %collective-permute-done.3.b_ref = bf16[896,128]{1,0:T(8,128)(2,1)S(1)} collective-permute-done((bf16[896,128]{1,0:T(8,128)(2,1)S(1)}, bf16[896,128]{1,0:T(8,128)(2,1)S(1)}, u32[]{:S(2)}, u32[]{:S(2)}) %collective-permute-start.3) | collective-permute-done | bytes 229408 | tf_op jit(solution)/shard_map/ppermute | solution.py:120
  47.5 0.1 collective-permute-start.9
  47.6 2.7 %collective-permute-start.8 = (bf16[1792,128]{1,0:T(8,128)(2,1)S(1)}, bf16[1792,128]{1,0:T(8,128)(2,1)S(1)}, u32[]{:S(2)}, u32[]{:S(2)}) collective-permute-start(bf16[1792,128]{1,0:T(8,128)(2,1)S(1)} %joined.1.refs_4_), channel_id=1, source_target_pairs={{0,192},{32,224},{64,0},{96,32},{128,64},{160,96},{192,128},{224,1... | collective-permute-start | bytes 1376264 | tf_op jit(solution)/shard_map/ppermute | solution.py:120
  50.3 0.0 collective-permute-done.6.refs_7_
  50.3 0.9 %collective-permute-start.10 = (bf16[896,128]{1,0:T(8,128)(2,1)S(1)}, bf16[896,128]{1,0:T(8,128)(2,1)S(1)}, u32[]{:S(2)}, u32[]{:S(2)}) collective-permute-start(bf16[896,128]{1,0:T(8,128)(2,1)S(1)} %collective-permute-done.6.refs_7_), channel_id=1, source_target_pairs={{0,32},{32,0},{64,96},{96,64},{128,160},{160,128},{192,224},{224,1... | collective-permute-start | bytes 688136 | tf_op jit(solution)/shard_map/ppermute | solution.py:120
  51.2 0.0 collective-permute-done.7.refs_8_
  51.2 0.6 collective-permute-start.11
  51.7 0.0 copy-start
  51.7 2.0 %copy-done = bf16[1,1792,1024]{2,1,0:T(8,128)(2,1)S(1)} copy-done((bf16[1,1792,1024]{2,1,0:T(8,128)(2,1)S(1)}, bf16[1,1792,1024]{2,1,0:T(8,128)(2,1)}, u32[]{:S(2)}) %copy-start) | copy-done | bytes 3670040
  53.8 2.8 %add.1 = (bf16[1792,1024]{1,0:T(8,128)(2,1)}, bf16[3,1792,128]{2,1,0:T(8,128)(2,1)S(1)}) custom-call(bf16[1792,1024]{1,0:T(8,128)(2,1)S(1)} %bitcast.5, bf16[896,128]{1,0:T(8,128)(2,1)S(1)} %bitcast.13, bf16[896,128]{1,0:T(8,128)(2,1)S(1)} %bitcast.9, bf16[896,128]{1,0:T(8,128)(2,1)S(1)} %collective-permute-done.above_ref.refs_2_, ...), custom_call_target="tpu_custom_call" | custom-call | flops 1835008 | bytes 11010048 | tf_op jit(solution)/shard_map/add/pallas_call | solution.py:160
  56.6 0.0 collective-permute-done.10.refs_2_
  56.6 3.9 %collective-permute-done.11.refs_3_ = bf16[896,128]{1,0:T(8,128)(2,1)S(1)} collective-permute-done((bf16[896,128]{1,0:T(8,128)(2,1)S(1)}, bf16[896,128]{1,0:T(8,128)(2,1)S(1)}, u32[]{:S(2)}, u32[]{:S(2)}) %collective-permute-start.11) | collective-permute-done | bytes 229408 | tf_op jit(solution)/shard_map/ppermute | solution.py:120
  60.5 0.0 collective-permute-done.9.refs_1_
  60.5 0.0 collective-permute-done.8.refs_0_
  60.5 1.2 %finish.1 = bf16[1792,1024]{1,0:T(8,128)(2,1)} custom-call(bf16[3,1792,128]{2,1,0:T(8,128)(2,1)S(1)} %get-tuple-element.7.rest_ref, bf16[1792,128]{1,0:T(8,128)(2,1)S(1)} %collective-permute-done.8.refs_0_, bf16[1792,128]{1,0:T(8,128)(2,1)S(1)} %collective-permute-done.9.refs_1_, ...), custom_call_target="tpu_custom_call", output_to_operand_aliasing={{}: (5, {})} | custom-call | tf_op jit(solution)/shard_map/finish/pallas_call | solution.py:194
  (2 shorter events, 0.1 us)
Async XLA Ops:
  31.7 9.0 %collective-permute-start.5 = (bf16[896,128]{1,0:T(8,128)(2,1)S(1)}, bf16[896,128]{1,0:T(8,128)(2,1)S(1)}, u32[]{:S(2)}, u32[]{:S(2)}) collective-permute-start(bf16[896,128]{1,0:T(8,128)(2,1)S(1)} %bitcast.10), channel_id=1, source_target_pairs={{0,64},{32,96},{64,128},{96,160},{128,192},{160,224},{192,0},{224,... | collective-permute-start | bytes 688136 | tf_op jit(solution)/shard_map/ppermute | solution.py:120
  33.1 8.5 %collective-permute-start.2 = (bf16[896,128]{1,0:T(8,128)(2,1)S(1)}, bf16[896,128]{1,0:T(8,128)(2,1)S(1)}, u32[]{:S(2)}, u32[]{:S(2)}) collective-permute-start(bf16[896,128]{1,0:T(8,128)(2,1)S(1)} %bitcast.11), channel_id=1, source_target_pairs={{0,32},{32,0},{64,96},{96,64},{128,160},{160,128},{192,224},{224,1... | collective-permute-start | bytes 688136 | tf_op jit(solution)/shard_map/ppermute | solution.py:120
  34.1 7.6 %collective-permute-start.1 = (bf16[896,128]{1,0:T(8,128)(2,1)S(1)}, bf16[896,128]{1,0:T(8,128)(2,1)S(1)}, u32[]{:S(2)}, u32[]{:S(2)}) collective-permute-start(bf16[896,128]{1,0:T(8,128)(2,1)S(1)} %bitcast.6), channel_id=1, source_target_pairs={{0,192},{32,224},{64,0},{96,32},{128,64},{160,96},{192,128},{224,1... | collective-permute-start | bytes 688136 | tf_op jit(solution)/shard_map/ppermute | solution.py:120
  35.6 10.4 %collective-permute-start = (bf16[896,128]{1,0:T(8,128)(2,1)S(1)}, bf16[896,128]{1,0:T(8,128)(2,1)S(1)}, u32[]{:S(2)}, u32[]{:S(2)}) collective-permute-start(bf16[896,128]{1,0:T(8,128)(2,1)S(1)} %bitcast.12), channel_id=1, source_target_pairs={{0,192},{32,224},{64,0},{96,32},{128,64},{160,96},{192,128},{224,1... | collective-permute-start | bytes 688136 | tf_op jit(solution)/shard_map/ppermute | solution.py:120
  37.0 9.0 %collective-permute-start.4 = (bf16[896,128]{1,0:T(8,128)(2,1)S(1)}, bf16[896,128]{1,0:T(8,128)(2,1)S(1)}, u32[]{:S(2)}, u32[]{:S(2)}) collective-permute-start(bf16[896,128]{1,0:T(8,128)(2,1)S(1)} %bitcast.7), channel_id=1, source_target_pairs={{0,64},{32,96},{64,128},{96,160},{128,192},{160,224},{192,0},{224,... | collective-permute-start | bytes 688136 | tf_op jit(solution)/shard_map/ppermute | solution.py:120
  40.7 6.8 %collective-permute-start.3 = (bf16[896,128]{1,0:T(8,128)(2,1)S(1)}, bf16[896,128]{1,0:T(8,128)(2,1)S(1)}, u32[]{:S(2)}, u32[]{:S(2)}) collective-permute-start(bf16[896,128]{1,0:T(8,128)(2,1)S(1)} %bitcast.8), channel_id=1, source_target_pairs={{0,32},{32,0},{64,96},{96,64},{128,160},{160,128},{192,224},{224,1... | collective-permute-start | bytes 688136 | tf_op jit(solution)/shard_map/ppermute | solution.py:120
  41.6 8.6 %collective-permute-start.6 = (bf16[896,128]{1,0:T(8,128)(2,1)S(1)}, bf16[896,128]{1,0:T(8,128)(2,1)S(1)}, u32[]{:S(2)}, u32[]{:S(2)}) collective-permute-start(bf16[896,128]{1,0:T(8,128)(2,1)S(1)} %collective-permute-done.5.refs_5_), channel_id=1, source_target_pairs={{0,64},{32,96},{64,128},{96,160},{128,192},{160,224},{192,0},{224,... | collective-permute-start | bytes 688136 | tf_op jit(solution)/shard_map/ppermute | solution.py:120
  41.7 9.5 %collective-permute-start.7 = (bf16[896,128]{1,0:T(8,128)(2,1)S(1)}, bf16[896,128]{1,0:T(8,128)(2,1)S(1)}, u32[]{:S(2)}, u32[]{:S(2)}) collective-permute-start(bf16[896,128]{1,0:T(8,128)(2,1)S(1)} %collective-permute-done.1.refs_3_), channel_id=1, source_target_pairs={{0,192},{32,224},{64,0},{96,32},{128,64},{160,96},{192,128},{224,1... | collective-permute-start | bytes 688136 | tf_op jit(solution)/shard_map/ppermute | solution.py:120
  47.5 13.0 %collective-permute-start.9 = (bf16[1792,128]{1,0:T(8,128)(2,1)S(1)}, bf16[1792,128]{1,0:T(8,128)(2,1)S(1)}, u32[]{:S(2)}, u32[]{:S(2)}) collective-permute-start(bf16[1792,128]{1,0:T(8,128)(2,1)S(1)} %joined.1.refs_4_), channel_id=1, source_target_pairs={{0,64},{32,96},{64,128},{96,160},{128,192},{160,224},{192,0},{224,... | collective-permute-start | bytes 1376264 | tf_op jit(solution)/shard_map/ppermute | solution.py:120
  47.6 12.9 %collective-permute-start.8 = (bf16[1792,128]{1,0:T(8,128)(2,1)S(1)}, bf16[1792,128]{1,0:T(8,128)(2,1)S(1)}, u32[]{:S(2)}, u32[]{:S(2)}) collective-permute-start(bf16[1792,128]{1,0:T(8,128)(2,1)S(1)} %joined.1.refs_4_), channel_id=1, source_target_pairs={{0,192},{32,224},{64,0},{96,32},{128,64},{160,96},{192,128},{224,1... | collective-permute-start | bytes 1376264 | tf_op jit(solution)/shard_map/ppermute | solution.py:120
  50.3 6.3 %collective-permute-start.10 = (bf16[896,128]{1,0:T(8,128)(2,1)S(1)}, bf16[896,128]{1,0:T(8,128)(2,1)S(1)}, u32[]{:S(2)}, u32[]{:S(2)}) collective-permute-start(bf16[896,128]{1,0:T(8,128)(2,1)S(1)} %collective-permute-done.6.refs_7_), channel_id=1, source_target_pairs={{0,32},{32,0},{64,96},{96,64},{128,160},{160,128},{192,224},{224,1... | collective-permute-start | bytes 688136 | tf_op jit(solution)/shard_map/ppermute | solution.py:120
  51.2 9.3 %collective-permute-start.11 = (bf16[896,128]{1,0:T(8,128)(2,1)S(1)}, bf16[896,128]{1,0:T(8,128)(2,1)S(1)}, u32[]{:S(2)}, u32[]{:S(2)}) collective-permute-start(bf16[896,128]{1,0:T(8,128)(2,1)S(1)} %collective-permute-done.7.refs_8_), channel_id=1, source_target_pairs={{0,32},{32,0},{64,96},{96,64},{128,160},{160,128},{192,224},{224,1... | collective-permute-start | bytes 688136 | tf_op jit(solution)/shard_map/ppermute | solution.py:120
  51.7 2.0 %copy-start = (bf16[1,1792,1024]{2,1,0:T(8,128)(2,1)S(1)}, bf16[1,1792,1024]{2,1,0:T(8,128)(2,1)}, u32[]{:S(2)}) copy-start(bf16[1,1792,1024]{2,1,0:T(8,128)(2,1)} %param.7) | copy-start | bytes 11010052

commit v8 on v7

--- a/solution.py
+++ b/solution.py
@@ -15,6 +15,7 @@
 WIDTH = 1024
 BAND = 448
 SPLIT = 896
+EDGE = 256
 FIRST = 5
 MOVES = [(0, 0), (1, 0), (0, 1), (-1, 0), (2, 0), (1, 1), (-1, 1), (2, 1)]
 
@@ -228,17 +229,21 @@
     below_b, above_a = shifted(own_b, dy=1), shifted(own_a, dy=-1)
     far_a, far_b = shifted(below_a, dy=1), shifted(above_b, dy=-1)
     beside = joined(beside_a, beside_b, below_b, above_a)
-    bb, ba = shifted(beside, dy=1), shifted(beside, dy=-1)
-    fz_a, fz_b = shifted(far_a, dz=1), shifted(far_b, dz=1)
+    bb, ba = shifted(beside[:-EDGE], dy=1), shifted(beside[EDGE:], dy=-1)
+    beside, first, last = lax.optimization_barrier((beside, above_a[:EDGE], below_b[-EDGE:]))
+    edges = shifted(jnp.concatenate([first, last], axis=0), dz=1)
+    top, bottom = edges[:EDGE], edges[EDGE:]
+    fz_top, fz_bottom = shifted(top, dy=-1), shifted(bottom, dy=1)
+    middle = shifted(jnp.concatenate([far_a[EDGE:], far_b[:-EDGE]], axis=0), dz=1)
     parts = [
         [(own_a, 0), (own_b, SPLIT)],
         [(above_a, 0), (above_b, SPLIT)],
         [(beside, 0)],
         [(below_a, 0), (below_b, SPLIT)],
         [(far_a, 0), (far_b, SPLIT)],
-        [(ba, 0)],
-        [(bb, 0)],
-        [(fz_a, 0), (fz_b, SPLIT)],
+        [(top, 0), (ba, EDGE)],
+        [(bb, 0), (bottom, OWNED - EDGE)],
+        [(fz_top, 0), (middle, EDGE), (fz_bottom, OWNED - EDGE)],
     ]
     spans = [[(start, start + piece.shape[0]) for piece, start in pieces] for pieces in parts]
     return [[piece for piece, _ in pieces] for pieces in parts], spans

time: 62.4 us -> 62.9 us (level)
  starting transfers between devices: 13.2 us -> 16 us
  local copies, waits for them, and re-layouts: 2.08 us -> 0.14 us
  waiting for transfers between devices: 10.7 us -> 9.48 us
    ppermute x12 -> x14, starting transfers between devices: 13.2 us -> 16 us  [shifted(): return lax.ppermute(block, 'rollout', pairs)]
    unnamed x2, local copies, waits for them, and re-layouts: 2.04 us -> 0.01 us
    ppermute x12 -> x14, waiting for transfers between devices: 10.7 us -> 9.48 us  [shifted(): return lax.ppermute(block, 'rollout', pairs)]
  transfers between devices with their start and end apart: 12 -> 14, of which waited for: 4 -> 4; matrix products, arithmetic and copies ran while one was open for 0% -> 0% of each run, Pallas kernels for 5% -> 5%
where the time goes in v8:
time: 62.9 us; the launch traced here: 61.8 us
  blocking collectives  28.8 us (46%)
  starting transfers between devices  16 us (25%)
  waiting for transfers between devices  9.48 us (15%)
  Pallas kernels  7.21 us (11%)
    all_to_all x1, blocking collectives, exchange(): lax.all_to_all(values, ('rollout', 'shard'), split_axis=0, concat_axis=0,...  28.8 us
    ppermute x14, starting transfers between devices, shifted(): return lax.ppermute(block, 'rollout', pairs)  16 us
    ppermute x14, waiting for transfers between devices, shifted(): return lax.ppermute(block, 'rollout', pairs)  9.48 us
    pallas_call x1, Pallas kernels, encode(): pl.pallas_call(encode_kernel, in_specs=[anywhere] * 4, out_specs=anywhere...  3.15 us
    pallas_call x1, Pallas kernels, add(): pl.pallas_call(functools.partial(add_kernel, spans), grid=(OWNED // BAND,...  2.79 us
  transfers between devices with their start and end apart: 14, of which 4 were waited for; matrix products, arithmetic and copies ran while one was open for 0% of the time, Pallas kernels for 5%

profile of v8, /device:TPU:1, one launch (start us, length us, event | category | flops | bytes accessed | tf_op | source)
XLA Modules:
  0.0 61.8 jit_solution(8518437971621690475)
XLA Ops:
  0.0 3.1 %encode.1 = bf16[8,224,128]{2,1,0:T(8,128)(2,1)} custom-call(s32[8]{0:T(128)} %ids_hbm.1, s32[8]{0:T(128)} %owner_hbm.1, bf16[12,224,128]{2,1,0:T(8,128)(2,1)} %fresh_hbm.1, bf16[12,224,128]{2,1,0:T(8,128)(2,1)} %older_hbm.1), custom_call_target="tpu_custom_call" | custom-call | tf_op jit(solution)/shard_map/encode/pallas_call | solution.py:80
  3.2 0.0 copy-start
  3.2 28.8 %all_to_all.5 = bf16[32,56,128]{2,1,0:T(8,128)(2,1)S(1)} all-to-all(bf16[32,56,128]{2,1,0:T(8,128)(2,1)} %bitcast.14), channel_id=1, replica_groups={{0,1,2,3,4,5,6,7,40,41,42,43,44,45,46,47,48,49,50,51,52,53,54,55,24,25,..., dimensions={0} | all-to-all | bytes 917504 | tf_op jit(solution)/shard_map/all_to_all | solution.py:111
  32.0 1.4 %collective-permute-start.5 = (bf16[896,128]{1,0:T(8,128)(2,1)S(1)}, bf16[896,128]{1,0:T(8,128)(2,1)S(1)}, u32[]{:S(2)}, u32[]{:S(2)}) collective-permute-start(bf16[896,128]{1,0:T(8,128)(2,1)S(1)} %bitcast.10), channel_id=1, source_target_pairs={{0,64},{32,96},{64,128},{96,160},{128,192},{160,224},{192,0},{224,... | collective-permute-start | bytes 688136 | tf_op jit(solution)/shard_map/ppermute | solution.py:121
  33.4 0.9 %collective-permute-start.2 = (bf16[896,128]{1,0:T(8,128)(2,1)S(1)}, bf16[896,128]{1,0:T(8,128)(2,1)S(1)}, u32[]{:S(2)}, u32[]{:S(2)}) collective-permute-start(bf16[896,128]{1,0:T(8,128)(2,1)S(1)} %bitcast.11), channel_id=1, source_target_pairs={{0,32},{32,0},{64,96},{96,64},{128,160},{160,128},{192,224},{224,1... | collective-permute-start | bytes 688136 | tf_op jit(solution)/shard_map/ppermute | solution.py:121
  34.3 1.5 %collective-permute-start.1 = (bf16[896,128]{1,0:T(8,128)(2,1)S(1)}, bf16[896,128]{1,0:T(8,128)(2,1)S(1)}, u32[]{:S(2)}, u32[]{:S(2)}) collective-permute-start(bf16[896,128]{1,0:T(8,128)(2,1)S(1)} %bitcast.6), channel_id=1, source_target_pairs={{0,192},{32,224},{64,0},{96,32},{128,64},{160,96},{192,128},{224,1... | collective-permute-start | bytes 688136 | tf_op jit(solution)/shard_map/ppermute | solution.py:121
  35.9 1.4 %collective-permute-start = (bf16[896,128]{1,0:T(8,128)(2,1)S(1)}, bf16[896,128]{1,0:T(8,128)(2,1)S(1)}, u32[]{:S(2)}, u32[]{:S(2)}) collective-permute-start(bf16[896,128]{1,0:T(8,128)(2,1)S(1)} %bitcast.12), channel_id=1, source_target_pairs={{0,192},{32,224},{64,0},{96,32},{128,64},{160,96},{192,128},{224,1... | collective-permute-start | bytes 688136 | tf_op jit(solution)/shard_map/ppermute | solution.py:121
  37.2 0.1 collective-permute-start.4
  37.3 3.6 %collective-permute-done.5.refs_5_ = bf16[896,128]{1,0:T(8,128)(2,1)S(1)} collective-permute-done((bf16[896,128]{1,0:T(8,128)(2,1)S(1)}, bf16[896,128]{1,0:T(8,128)(2,1)S(1)}, u32[]{:S(2)}, u32[]{:S(2)}) %collective-permute-start.5) | collective-permute-done | bytes 229408 | tf_op jit(solution)/shard_map/ppermute | solution.py:121
  41.0 0.9 %collective-permute-start.3 = (bf16[896,128]{1,0:T(8,128)(2,1)S(1)}, bf16[896,128]{1,0:T(8,128)(2,1)S(1)}, u32[]{:S(2)}, u32[]{:S(2)}) collective-permute-start(bf16[896,128]{1,0:T(8,128)(2,1)S(1)} %bitcast.8), channel_id=1, source_target_pairs={{0,32},{32,0},{64,96},{96,64},{128,160},{160,128},{192,224},{224,1... | collective-permute-start | bytes 688136 | tf_op jit(solution)/shard_map/ppermute | solution.py:121
  41.9 0.0 collective-permute-done.2.a_ref
  41.9 0.1 collective-permute-start.6
  42.0 0.0 collective-permute-done.1.refs_3_
  42.0 2.6 %collective-permute-start.7 = (bf16[896,128]{1,0:T(8,128)(2,1)S(1)}, bf16[896,128]{1,0:T(8,128)(2,1)S(1)}, u32[]{:S(2)}, u32[]{:S(2)}) collective-permute-start(bf16[896,128]{1,0:T(8,128)(2,1)S(1)} %collective-permute-done.1.refs_3_), channel_id=1, source_target_pairs={{0,192},{32,224},{64,0},{96,32},{128,64},{160,96},{192,128},{224,1... | collective-permute-start | bytes 688136 | tf_op jit(solution)/shard_map/ppermute | solution.py:121
  44.6 1.7 %collective-permute-done.above_ref.refs_2_ = bf16[896,128]{1,0:T(8,128)(2,1)S(1)} collective-permute-done((bf16[896,128]{1,0:T(8,128)(2,1)S(1)}, bf16[896,128]{1,0:T(8,128)(2,1)S(1)}, u32[]{:S(2)}, u32[]{:S(2)}) %collective-permute-start) | collective-permute-done | bytes 229408 | tf_op jit(solution)/shard_map/ppermute | solution.py:121
  46.3 0.0 collective-permute-done.4.below_ref.refs_6_
  46.3 1.5 %collective-permute-done.3.b_ref = bf16[896,128]{1,0:T(8,128)(2,1)S(1)} collective-permute-done((bf16[896,128]{1,0:T(8,128)(2,1)S(1)}, bf16[896,128]{1,0:T(8,128)(2,1)S(1)}, u32[]{:S(2)}, u32[]{:S(2)}) %collective-permute-start.3) | collective-permute-done | bytes 229408 | tf_op jit(solution)/shard_map/ppermute | solution.py:121
  47.8 0.1 fusion
  47.9 1.0 %collective-permute-start.8 = (bf16[512,128]{1,0:T(8,128)(2,1)S(1)}, bf16[512,128]{1,0:T(8,128)(2,1)S(1)}, u32[]{:S(2)}, u32[]{:S(2)}) collective-permute-start(bf16[512,128]{1,0:T(8,128)(2,1)S(1)} %pad_maximum_fusion.1), channel_id=1, source_target_pairs={{0,32},{32,0},{64,96},{96,64},{128,160},{160,128},{192,224},{224,1... | collective-permute-start | bytes 393224 | tf_op jit(solution)/shard_map/ppermute | solution.py:121
  48.9 0.0 collective-permute-start.10
  48.9 2.7 %collective-permute-start.9 = (bf16[1536,128]{1,0:T(8,128)(2,1)S(1)}, bf16[1536,128]{1,0:T(8,128)(2,1)S(1)}, u32[]{:S(2)}, u32[]{:S(2)}) collective-permute-start(bf16[1536,128]{1,0:T(8,128)(2,1)S(1)} %get-tuple-element.16), channel_id=1, source_target_pairs={{0,192},{32,224},{64,0},{96,32},{128,64},{160,96},{192,128},{224,1... | collective-permute-start | bytes 1179656 | tf_op jit(solution)/shard_map/ppermute | solution.py:121
  51.5 0.0 collective-permute-done.6.refs_7_
  51.6 0.0 collective-permute-done.7.refs_8_
  51.6 0.7 %collective-permute-start.12 = (bf16[1280,128]{1,0:T(8,128)(2,1)S(1)}, bf16[1280,128]{1,0:T(8,128)(2,1)S(1)}, u32[]{:S(2)}, u32[]{:S(2)}) collective-permute-start(bf16[1280,128]{1,0:T(8,128)(2,1)S(1)} %pad_maximum_fusion), channel_id=1, source_target_pairs={{0,32},{32,0},{64,96},{96,64},{128,160},{160,128},{192,224},{224,1... | collective-permute-start | bytes 983048 | tf_op jit(solution)/shard_map/ppermute | solution.py:121
  52.3 0.0 collective-permute-done.8
  52.3 0.9 %collective-permute-start.13 = (bf16[256,128]{1,0:T(8,128)(2,1)S(1)}, bf16[256,128]{1,0:T(8,128)(2,1)S(1)}, u32[]{:S(2)}, u32[]{:S(2)}) collective-permute-start(bf16[256,128]{1,0:T(8,128)(2,1)S(1)} %get-tuple-element.19.refs_3_), channel_id=1, source_target_pairs={{0,64},{32,96},{64,128},{96,160},{128,192},{160,224},{192,0},{224,... | collective-permute-start | bytes 196616 | tf_op jit(solution)/shard_map/ppermute | solution.py:121
  53.3 1.8 %collective-permute-start.11 = (bf16[256,128]{1,0:T(8,128)(2,1)S(1)}, bf16[256,128]{1,0:T(8,128)(2,1)S(1)}, u32[]{:S(2)}, u32[]{:S(2)}) collective-permute-start(bf16[256,128]{1,0:T(8,128)(2,1)S(1)} %get-tuple-element.20.refs_0_), channel_id=1, source_target_pairs={{0,192},{32,224},{64,0},{96,32},{128,64},{160,96},{192,128},{224,1... | collective-permute-start | bytes 196616 | tf_op jit(solution)/shard_map/ppermute | solution.py:121
  55.1 0.0 copy-done
  55.1 2.8 %add.1 = (bf16[1792,1024]{1,0:T(8,128)(2,1)}, bf16[3,1792,128]{2,1,0:T(8,128)(2,1)S(1)}) custom-call(bf16[1792,1024]{1,0:T(8,128)(2,1)S(1)} %bitcast.5, bf16[896,128]{1,0:T(8,128)(2,1)S(1)} %bitcast.13, bf16[896,128]{1,0:T(8,128)(2,1)S(1)} %bitcast.9, bf16[896,128]{1,0:T(8,128)(2,1)S(1)} %collective-permute-done.above_ref.refs_2_, ...), custom_call_target="tpu_custom_call" | custom-call | flops 1835008 | bytes 11010048 | tf_op jit(solution)/shard_map/add/pallas_call | solution.py:161
  57.9 2.7 %collective-permute-done.13.refs_6_ = bf16[256,128]{1,0:T(8,128)(2,1)S(1)} collective-permute-done((bf16[256,128]{1,0:T(8,128)(2,1)S(1)}, bf16[256,128]{1,0:T(8,128)(2,1)S(1)}, u32[]{:S(2)}, u32[]{:S(2)}) %collective-permute-start.13) | collective-permute-done | bytes 65568 | tf_op jit(solution)/shard_map/ppermute | solution.py:121
  60.5 0.0 collective-permute-done.11.refs_4_
  60.5 0.0 collective-permute-done.10.refs_2_
  60.5 0.0 collective-permute-done.9.refs_1_
  60.5 0.0 collective-permute-done.12.refs_5_
  60.6 1.2 %finish.1 = bf16[1792,1024]{1,0:T(8,128)(2,1)} custom-call(bf16[3,1792,128]{2,1,0:T(8,128)(2,1)S(1)} %get-tuple-element.11.rest_ref, bf16[256,128]{1,0:T(8,128)(2,1)S(1)} %get-tuple-element.20.refs_0_, bf16[1536,128]{1,0:T(8,128)(2,1)S(1)} %collective-permute-done.9.refs_1_, ...), custom_call_target="tpu_custom_call", output_to_operand_aliasing={{}: (8, {})} | custom-call | tf_op jit(solution)/shard_map/finish/pallas_call | solution.py:195
  (9 shorter events, 0.1 us)
Async XLA Ops:
  3.2 51.9 %copy-start = (bf16[1,1792,1024]{2,1,0:T(8,128)(2,1)S(1)}, bf16[1,1792,1024]{2,1,0:T(8,128)(2,1)}, u32[]{:S(2)}) copy-start(bf16[1,1792,1024]{2,1,0:T(8,128)(2,1)} %param.7) | copy-start | bytes 11010052
  32.0 9.0 %collective-permute-start.5 = (bf16[896,128]{1,0:T(8,128)(2,1)S(1)}, bf16[896,128]{1,0:T(8,128)(2,1)S(1)}, u32[]{:S(2)}, u32[]{:S(2)}) collective-permute-start(bf16[896,128]{1,0:T(8,128)(2,1)S(1)} %bitcast.10), channel_id=1, source_target_pairs={{0,64},{32,96},{64,128},{96,160},{128,192},{160,224},{192,0},{224,... | collective-permute-start | bytes 688136 | tf_op jit(solution)/shard_map/ppermute | solution.py:121
  33.4 8.5 %collective-permute-start.2 = (bf16[896,128]{1,0:T(8,128)(2,1)S(1)}, bf16[896,128]{1,0:T(8,128)(2,1)S(1)}, u32[]{:S(2)}, u32[]{:S(2)}) collective-permute-start(bf16[896,128]{1,0:T(8,128)(2,1)S(1)} %bitcast.11), channel_id=1, source_target_pairs={{0,32},{32,0},{64,96},{96,64},{128,160},{160,128},{192,224},{224,1... | collective-permute-start | bytes 688136 | tf_op jit(solution)/shard_map/ppermute | solution.py:121
  34.3 7.6 %collective-permute-start.1 = (bf16[896,128]{1,0:T(8,128)(2,1)S(1)}, bf16[896,128]{1,0:T(8,128)(2,1)S(1)}, u32[]{:S(2)}, u32[]{:S(2)}) collective-permute-start(bf16[896,128]{1,0:T(8,128)(2,1)S(1)} %bitcast.6), channel_id=1, source_target_pairs={{0,192},{32,224},{64,0},{96,32},{128,64},{160,96},{192,128},{224,1... | collective-permute-start | bytes 688136 | tf_op jit(solution)/shard_map/ppermute | solution.py:121
  35.9 10.4 %collective-permute-start = (bf16[896,128]{1,0:T(8,128)(2,1)S(1)}, bf16[896,128]{1,0:T(8,128)(2,1)S(1)}, u32[]{:S(2)}, u32[]{:S(2)}) collective-permute-start(bf16[896,128]{1,0:T(8,128)(2,1)S(1)} %bitcast.12), channel_id=1, source_target_pairs={{0,192},{32,224},{64,0},{96,32},{128,64},{160,96},{192,128},{224,1... | collective-permute-start | bytes 688136 | tf_op jit(solution)/shard_map/ppermute | solution.py:121
  37.2 9.0 %collective-permute-start.4 = (bf16[896,128]{1,0:T(8,128)(2,1)S(1)}, bf16[896,128]{1,0:T(8,128)(2,1)S(1)}, u32[]{:S(2)}, u32[]{:S(2)}) collective-permute-start(bf16[896,128]{1,0:T(8,128)(2,1)S(1)} %bitcast.7), channel_id=1, source_target_pairs={{0,64},{32,96},{64,128},{96,160},{128,192},{160,224},{192,0},{224,... | collective-permute-start | bytes 688136 | tf_op jit(solution)/shard_map/ppermute | solution.py:121
  41.0 6.8 %collective-permute-start.3 = (bf16[896,128]{1,0:T(8,128)(2,1)S(1)}, bf16[896,128]{1,0:T(8,128)(2,1)S(1)}, u32[]{:S(2)}, u32[]{:S(2)}) collective-permute-start(bf16[896,128]{1,0:T(8,128)(2,1)S(1)} %bitcast.8), channel_id=1, source_target_pairs={{0,32},{32,0},{64,96},{96,64},{128,160},{160,128},{192,224},{224,1... | collective-permute-start | bytes 688136 | tf_op jit(solution)/shard_map/ppermute | solution.py:121
  41.9 9.6 %collective-permute-start.6 = (bf16[896,128]{1,0:T(8,128)(2,1)S(1)}, bf16[896,128]{1,0:T(8,128)(2,1)S(1)}, u32[]{:S(2)}, u32[]{:S(2)}) collective-permute-start(bf16[896,128]{1,0:T(8,128)(2,1)S(1)} %collective-permute-done.5.refs_5_), channel_id=1, source_target_pairs={{0,64},{32,96},{64,128},{96,160},{128,192},{160,224},{192,0},{224,... | collective-permute-start | bytes 688136 | tf_op jit(solution)/shard_map/ppermute | solution.py:121
  42.0 9.6 %collective-permute-start.7 = (bf16[896,128]{1,0:T(8,128)(2,1)S(1)}, bf16[896,128]{1,0:T(8,128)(2,1)S(1)}, u32[]{:S(2)}, u32[]{:S(2)}) collective-permute-start(bf16[896,128]{1,0:T(8,128)(2,1)S(1)} %collective-permute-done.1.refs_3_), channel_id=1, source_target_pairs={{0,192},{32,224},{64,0},{96,32},{128,64},{160,96},{192,128},{224,1... | collective-permute-start | bytes 688136 | tf_op jit(solution)/shard_map/ppermute | solution.py:121
  47.9 4.4 %collective-permute-start.8 = (bf16[512,128]{1,0:T(8,128)(2,1)S(1)}, bf16[512,128]{1,0:T(8,128)(2,1)S(1)}, u32[]{:S(2)}, u32[]{:S(2)}) collective-permute-start(bf16[512,128]{1,0:T(8,128)(2,1)S(1)} %pad_maximum_fusion.1), channel_id=1, source_target_pairs={{0,32},{32,0},{64,96},{96,64},{128,160},{160,128},{192,224},{224,1... | collective-permute-start | bytes 393224 | tf_op jit(solution)/shard_map/ppermute | solution.py:121
  48.9 11.7 %collective-permute-start.10 = (bf16[1536,128]{1,0:T(8,128)(2,1)S(1)}, bf16[1536,128]{1,0:T(8,128)(2,1)S(1)}, u32[]{:S(2)}, u32[]{:S(2)}) collective-permute-start(bf16[1536,128]{1,0:T(8,128)(2,1)S(1)} %get-tuple-element.15), channel_id=1, source_target_pairs={{0,64},{32,96},{64,128},{96,160},{128,192},{160,224},{192,0},{224,... | collective-permute-start | bytes 1179656 | tf_op jit(solution)/shard_map/ppermute | solution.py:121
  48.9 11.7 %collective-permute-start.9 = (bf16[1536,128]{1,0:T(8,128)(2,1)S(1)}, bf16[1536,128]{1,0:T(8,128)(2,1)S(1)}, u32[]{:S(2)}, u32[]{:S(2)}) collective-permute-start(bf16[1536,128]{1,0:T(8,128)(2,1)S(1)} %get-tuple-element.16), channel_id=1, source_target_pairs={{0,192},{32,224},{64,0},{96,32},{128,64},{160,96},{192,128},{224,1... | collective-permute-start | bytes 1179656 | tf_op jit(solution)/shard_map/ppermute | solution.py:121
  51.6 8.9 %collective-permute-start.12 = (bf16[1280,128]{1,0:T(8,128)(2,1)S(1)}, bf16[1280,128]{1,0:T(8,128)(2,1)S(1)}, u32[]{:S(2)}, u32[]{:S(2)}) collective-permute-start(bf16[1280,128]{1,0:T(8,128)(2,1)S(1)} %pad_maximum_fusion), channel_id=1, source_target_pairs={{0,32},{32,0},{64,96},{96,64},{128,160},{160,128},{192,224},{224,1... | collective-permute-start | bytes 983048 | tf_op jit(solution)/shard_map/ppermute | solution.py:121
  52.3 8.2 %collective-permute-start.13 = (bf16[256,128]{1,0:T(8,128)(2,1)S(1)}, bf16[256,128]{1,0:T(8,128)(2,1)S(1)}, u32[]{:S(2)}, u32[]{:S(2)}) collective-permute-start(bf16[256,128]{1,0:T(8,128)(2,1)S(1)} %get-tuple-element.19.refs_3_), channel_id=1, source_target_pairs={{0,64},{32,96},{64,128},{96,160},{128,192},{160,224},{192,0},{224,... | collective-permute-start | bytes 196616 | tf_op jit(solution)/shard_map/ppermute | solution.py:121
  53.3 7.3 %collective-permute-start.11 = (bf16[256,128]{1,0:T(8,128)(2,1)S(1)}, bf16[256,128]{1,0:T(8,128)(2,1)S(1)}, u32[]{:S(2)}, u32[]{:S(2)}) collective-permute-start(bf16[256,128]{1,0:T(8,128)(2,1)S(1)} %get-tuple-element.20.refs_0_), channel_id=1, source_target_pairs={{0,192},{32,224},{64,0},{96,32},{128,64},{160,96},{192,128},{224,1... | collective-permute-start | bytes 196616 | tf_op jit(solution)/shard_map/ppermute | solution.py:121

commit v9 on v7

--- a/solution.py
+++ b/solution.py
@@ -97,7 +97,7 @@
 
 
 def swaps(zh):
-    return (zh + 1) // 2 % 2
+    return zh // 2 % 2
 
 
 def exchange(values):

time: 62.4 us -> 62.7 us (level)
  transfers between devices with their start and end apart: 12 -> 12, of which waited for: 4 -> 5; matrix products, arithmetic and copies ran while one was open for 0% -> 0% of each run, Pallas kernels for 5% -> 5%
where the time goes in v9:
time: 62.7 us; the launch traced here: 61.7 us
  blocking collectives  28.8 us (46%)
  starting transfers between devices  13 us (21%)
  waiting for transfers between devices  10.5 us (17%)
  Pallas kernels  7.19 us (11%)
  local copies, waits for them, and re-layouts  2.08 us (3%)
    all_to_all x1, blocking collectives, exchange(): lax.all_to_all(values, ('rollout', 'shard'), split_axis=0, concat_axis=0,...  28.8 us
    ppermute x12, starting transfers between devices, shifted(): return lax.ppermute(block, 'rollout', pairs)  13 us
    ppermute x12, waiting for transfers between devices, shifted(): return lax.ppermute(block, 'rollout', pairs)  10.5 us
    pallas_call x1, Pallas kernels, encode(): pl.pallas_call(encode_kernel, in_specs=[anywhere] * 4, out_specs=anywhere...  3.15 us
    pallas_call x1, Pallas kernels, add(): pl.pallas_call(functools.partial(add_kernel, spans), grid=(OWNED // BAND,...  2.79 us
    unnamed x2, local copies, waits for them, and re-layouts  2.04 us
  transfers between devices with their start and end apart: 12, of which 5 were waited for; matrix products, arithmetic and copies ran while one was open for 0% of the time, Pallas kernels for 5%

profile of v9, /device:TPU:1, one launch (start us, length us, event | category | flops | bytes accessed | tf_op | source)
XLA Modules:
  0.0 61.7 jit_solution(2232872108239805860)
XLA Ops:
  0.0 3.1 %encode.1 = bf16[8,224,128]{2,1,0:T(8,128)(2,1)} custom-call(s32[8]{0:T(128)} %ids_hbm.1, s32[8]{0:T(128)} %owner_hbm.1, bf16[12,224,128]{2,1,0:T(8,128)(2,1)} %fresh_hbm.1, bf16[12,224,128]{2,1,0:T(8,128)(2,1)} %older_hbm.1), custom_call_target="tpu_custom_call" | custom-call | tf_op jit(solution)/shard_map/encode/pallas_call | solution.py:79
  3.2 28.8 %all_to_all.5 = bf16[32,56,128]{2,1,0:T(8,128)(2,1)S(1)} all-to-all(bf16[32,56,128]{2,1,0:T(8,128)(2,1)} %bitcast.14), channel_id=1, replica_groups={{0,1,2,3,4,5,6,7,8,9,10,11,12,13,14,15,48,49,50,51,52,53,54,55,56,57,58..., dimensions={0} | all-to-all | bytes 917504 | tf_op jit(solution)/shard_map/all_to_all | solution.py:110
  32.0 1.4 %collective-permute-start.5 = (bf16[896,128]{1,0:T(8,128)(2,1)S(1)}, bf16[896,128]{1,0:T(8,128)(2,1)S(1)}, u32[]{:S(2)}, u32[]{:S(2)}) collective-permute-start(bf16[896,128]{1,0:T(8,128)(2,1)S(1)} %bitcast.10), channel_id=1, source_target_pairs={{0,64},{32,96},{64,128},{96,160},{128,192},{160,224},{192,0},{224,... | collective-permute-start | bytes 688136 | tf_op jit(solution)/shard_map/ppermute | solution.py:120
  33.4 0.7 %collective-permute-start.2 = (bf16[896,128]{1,0:T(8,128)(2,1)S(1)}, bf16[896,128]{1,0:T(8,128)(2,1)S(1)}, u32[]{:S(2)}, u32[]{:S(2)}) collective-permute-start(bf16[896,128]{1,0:T(8,128)(2,1)S(1)} %bitcast.11), channel_id=1, source_target_pairs={{0,32},{32,0},{64,96},{96,64},{128,160},{160,128},{192,224},{224,1... | collective-permute-start | bytes 688136 | tf_op jit(solution)/shard_map/ppermute | solution.py:120
  34.1 1.5 %collective-permute-start.1 = (bf16[896,128]{1,0:T(8,128)(2,1)S(1)}, bf16[896,128]{1,0:T(8,128)(2,1)S(1)}, u32[]{:S(2)}, u32[]{:S(2)}) collective-permute-start(bf16[896,128]{1,0:T(8,128)(2,1)S(1)} %bitcast.6), channel_id=1, source_target_pairs={{0,192},{32,224},{64,0},{96,32},{128,64},{160,96},{192,128},{224,1... | collective-permute-start | bytes 688136 | tf_op jit(solution)/shard_map/ppermute | solution.py:120
  35.6 1.4 %collective-permute-start = (bf16[896,128]{1,0:T(8,128)(2,1)S(1)}, bf16[896,128]{1,0:T(8,128)(2,1)S(1)}, u32[]{:S(2)}, u32[]{:S(2)}) collective-permute-start(bf16[896,128]{1,0:T(8,128)(2,1)S(1)} %bitcast.12), channel_id=1, source_target_pairs={{0,192},{32,224},{64,0},{96,32},{128,64},{160,96},{192,128},{224,1... | collective-permute-start | bytes 688136 | tf_op jit(solution)/shard_map/ppermute | solution.py:120
  37.0 0.1 collective-permute-start.4
  37.1 3.6 %collective-permute-done.5.refs_5_ = bf16[896,128]{1,0:T(8,128)(2,1)S(1)} collective-permute-done((bf16[896,128]{1,0:T(8,128)(2,1)S(1)}, bf16[896,128]{1,0:T(8,128)(2,1)S(1)}, u32[]{:S(2)}, u32[]{:S(2)}) %collective-permute-start.5) | collective-permute-done | bytes 229408 | tf_op jit(solution)/shard_map/ppermute | solution.py:120
  40.6 0.8 %collective-permute-start.3 = (bf16[896,128]{1,0:T(8,128)(2,1)S(1)}, bf16[896,128]{1,0:T(8,128)(2,1)S(1)}, u32[]{:S(2)}, u32[]{:S(2)}) collective-permute-start(bf16[896,128]{1,0:T(8,128)(2,1)S(1)} %bitcast.8), channel_id=1, source_target_pairs={{0,32},{32,0},{64,96},{96,64},{128,160},{160,128},{192,224},{224,1... | collective-permute-start | bytes 688136 | tf_op jit(solution)/shard_map/ppermute | solution.py:120
  41.4 0.0 collective-permute-done.2.a_ref
  41.4 0.7 %collective-permute-start.6 = (bf16[896,128]{1,0:T(8,128)(2,1)S(1)}, bf16[896,128]{1,0:T(8,128)(2,1)S(1)}, u32[]{:S(2)}, u32[]{:S(2)}) collective-permute-start(bf16[896,128]{1,0:T(8,128)(2,1)S(1)} %collective-permute-done.5.refs_5_), channel_id=1, source_target_pairs={{0,64},{32,96},{64,128},{96,160},{128,192},{160,224},{192,0},{224,... | collective-permute-start | bytes 688136 | tf_op jit(solution)/shard_map/ppermute | solution.py:120
  42.2 0.0 collective-permute-done.1.refs_3_
  42.2 2.0 %collective-permute-start.7 = (bf16[896,128]{1,0:T(8,128)(2,1)S(1)}, bf16[896,128]{1,0:T(8,128)(2,1)S(1)}, u32[]{:S(2)}, u32[]{:S(2)}) collective-permute-start(bf16[896,128]{1,0:T(8,128)(2,1)S(1)} %collective-permute-done.1.refs_3_), channel_id=1, source_target_pairs={{0,192},{32,224},{64,0},{96,32},{128,64},{160,96},{192,128},{224,1... | collective-permute-start | bytes 688136 | tf_op jit(solution)/shard_map/ppermute | solution.py:120
  44.2 2.0 %collective-permute-done.above_ref.refs_2_ = bf16[896,128]{1,0:T(8,128)(2,1)S(1)} collective-permute-done((bf16[896,128]{1,0:T(8,128)(2,1)S(1)}, bf16[896,128]{1,0:T(8,128)(2,1)S(1)}, u32[]{:S(2)}, u32[]{:S(2)}) %collective-permute-start) | collective-permute-done | bytes 229408 | tf_op jit(solution)/shard_map/ppermute | solution.py:120
  46.2 0.0 collective-permute-done.4.below_ref.refs_6_
  46.2 1.2 %collective-permute-done.3.b_ref = bf16[896,128]{1,0:T(8,128)(2,1)S(1)} collective-permute-done((bf16[896,128]{1,0:T(8,128)(2,1)S(1)}, bf16[896,128]{1,0:T(8,128)(2,1)S(1)}, u32[]{:S(2)}, u32[]{:S(2)}) %collective-permute-start.3) | collective-permute-done | bytes 229408 | tf_op jit(solution)/shard_map/ppermute | solution.py:120
  47.5 0.8 %collective-permute-start.9 = (bf16[1792,128]{1,0:T(8,128)(2,1)S(1)}, bf16[1792,128]{1,0:T(8,128)(2,1)S(1)}, u32[]{:S(2)}, u32[]{:S(2)}) collective-permute-start(bf16[1792,128]{1,0:T(8,128)(2,1)S(1)} %joined.1.refs_4_), channel_id=1, source_target_pairs={{0,64},{32,96},{64,128},{96,160},{128,192},{160,224},{192,0},{224,... | collective-permute-start | bytes 1376264 | tf_op jit(solution)/shard_map/ppermute | solution.py:120
  48.2 2.0 %collective-permute-start.8 = (bf16[1792,128]{1,0:T(8,128)(2,1)S(1)}, bf16[1792,128]{1,0:T(8,128)(2,1)S(1)}, u32[]{:S(2)}, u32[]{:S(2)}) collective-permute-start(bf16[1792,128]{1,0:T(8,128)(2,1)S(1)} %joined.1.refs_4_), channel_id=1, source_target_pairs={{0,192},{32,224},{64,0},{96,32},{128,64},{160,96},{192,128},{224,1... | collective-permute-start | bytes 1376264 | tf_op jit(solution)/shard_map/ppermute | solution.py:120
  50.2 0.0 collective-permute-done.6.refs_7_
  50.2 0.8 %collective-permute-start.10 = (bf16[896,128]{1,0:T(8,128)(2,1)S(1)}, bf16[896,128]{1,0:T(8,128)(2,1)S(1)}, u32[]{:S(2)}, u32[]{:S(2)}) collective-permute-start(bf16[896,128]{1,0:T(8,128)(2,1)S(1)} %collective-permute-done.6.refs_7_), channel_id=1, source_target_pairs={{0,32},{32,0},{64,96},{96,64},{128,160},{160,128},{192,224},{224,1... | collective-permute-start | bytes 688136 | tf_op jit(solution)/shard_map/ppermute | solution.py:120
  51.0 0.1 collective-permute-done.7.refs_8_
  51.1 0.9 %collective-permute-start.11 = (bf16[896,128]{1,0:T(8,128)(2,1)S(1)}, bf16[896,128]{1,0:T(8,128)(2,1)S(1)}, u32[]{:S(2)}, u32[]{:S(2)}) collective-permute-start(bf16[896,128]{1,0:T(8,128)(2,1)S(1)} %collective-permute-done.7.refs_8_), channel_id=1, source_target_pairs={{0,32},{32,0},{64,96},{96,64},{128,160},{160,128},{192,224},{224,1... | collective-permute-start | bytes 688136 | tf_op jit(solution)/shard_map/ppermute | solution.py:120
  52.0 0.0 copy-start
  52.0 2.0 %copy-done = bf16[1,1792,1024]{2,1,0:T(8,128)(2,1)S(1)} copy-done((bf16[1,1792,1024]{2,1,0:T(8,128)(2,1)S(1)}, bf16[1,1792,1024]{2,1,0:T(8,128)(2,1)}, u32[]{:S(2)}) %copy-start) | copy-done | bytes 3670040
  54.0 2.8 %add.1 = (bf16[1792,1024]{1,0:T(8,128)(2,1)}, bf16[3,1792,128]{2,1,0:T(8,128)(2,1)S(1)}) custom-call(bf16[1792,1024]{1,0:T(8,128)(2,1)S(1)} %bitcast.5, bf16[896,128]{1,0:T(8,128)(2,1)S(1)} %bitcast.13, bf16[896,128]{1,0:T(8,128)(2,1)S(1)} %bitcast.9, bf16[896,128]{1,0:T(8,128)(2,1)S(1)} %collective-permute-done.above_ref.refs_2_, ...), custom_call_target="tpu_custom_call" | custom-call | flops 1835008 | bytes 11010048 | tf_op jit(solution)/shard_map/add/pallas_call | solution.py:160
  56.8 0.0 collective-permute-done.10.refs_2_
  56.8 3.6 %collective-permute-done.11.refs_3_ = bf16[896,128]{1,0:T(8,128)(2,1)S(1)} collective-permute-done((bf16[896,128]{1,0:T(8,128)(2,1)S(1)}, bf16[896,128]{1,0:T(8,128)(2,1)S(1)}, u32[]{:S(2)}, u32[]{:S(2)}) %collective-permute-start.11) | collective-permute-done | bytes 229408 | tf_op jit(solution)/shard_map/ppermute | solution.py:120
  60.4 0.0 collective-permute-done.9.refs_1_
  60.4 0.0 collective-permute-done.8.refs_0_
  60.4 1.2 %finish.1 = bf16[1792,1024]{1,0:T(8,128)(2,1)} custom-call(bf16[3,1792,128]{2,1,0:T(8,128)(2,1)S(1)} %get-tuple-element.7.rest_ref, bf16[1792,128]{1,0:T(8,128)(2,1)S(1)} %collective-permute-done.8.refs_0_, bf16[1792,128]{1,0:T(8,128)(2,1)S(1)} %collective-permute-done.9.refs_1_, ...), custom_call_target="tpu_custom_call", output_to_operand_aliasing={{}: (5, {})} | custom-call | tf_op jit(solution)/shard_map/finish/pallas_call | solution.py:194
  (2 shorter events, 0.1 us)
Async XLA Ops:
  32.0 8.6 %collective-permute-start.5 = (bf16[896,128]{1,0:T(8,128)(2,1)S(1)}, bf16[896,128]{1,0:T(8,128)(2,1)S(1)}, u32[]{:S(2)}, u32[]{:S(2)}) collective-permute-start(bf16[896,128]{1,0:T(8,128)(2,1)S(1)} %bitcast.10), channel_id=1, source_target_pairs={{0,64},{32,96},{64,128},{96,160},{128,192},{160,224},{192,0},{224,... | collective-permute-start | bytes 688136 | tf_op jit(solution)/shard_map/ppermute | solution.py:120
  33.4 8.0 %collective-permute-start.2 = (bf16[896,128]{1,0:T(8,128)(2,1)S(1)}, bf16[896,128]{1,0:T(8,128)(2,1)S(1)}, u32[]{:S(2)}, u32[]{:S(2)}) collective-permute-start(bf16[896,128]{1,0:T(8,128)(2,1)S(1)} %bitcast.11), channel_id=1, source_target_pairs={{0,32},{32,0},{64,96},{96,64},{128,160},{160,128},{192,224},{224,1... | collective-permute-start | bytes 688136 | tf_op jit(solution)/shard_map/ppermute | solution.py:120
  34.1 8.1 %collective-permute-start.1 = (bf16[896,128]{1,0:T(8,128)(2,1)S(1)}, bf16[896,128]{1,0:T(8,128)(2,1)S(1)}, u32[]{:S(2)}, u32[]{:S(2)}) collective-permute-start(bf16[896,128]{1,0:T(8,128)(2,1)S(1)} %bitcast.6), channel_id=1, source_target_pairs={{0,192},{32,224},{64,0},{96,32},{128,64},{160,96},{192,128},{224,1... | collective-permute-start | bytes 688136 | tf_op jit(solution)/shard_map/ppermute | solution.py:120
  35.6 10.6 %collective-permute-start = (bf16[896,128]{1,0:T(8,128)(2,1)S(1)}, bf16[896,128]{1,0:T(8,128)(2,1)S(1)}, u32[]{:S(2)}, u32[]{:S(2)}) collective-permute-start(bf16[896,128]{1,0:T(8,128)(2,1)S(1)} %bitcast.12), channel_id=1, source_target_pairs={{0,192},{32,224},{64,0},{96,32},{128,64},{160,96},{192,128},{224,1... | collective-permute-start | bytes 688136 | tf_op jit(solution)/shard_map/ppermute | solution.py:120
  37.0 9.2 %collective-permute-start.4 = (bf16[896,128]{1,0:T(8,128)(2,1)S(1)}, bf16[896,128]{1,0:T(8,128)(2,1)S(1)}, u32[]{:S(2)}, u32[]{:S(2)}) collective-permute-start(bf16[896,128]{1,0:T(8,128)(2,1)S(1)} %bitcast.7), channel_id=1, source_target_pairs={{0,64},{32,96},{64,128},{96,160},{128,192},{160,224},{192,0},{224,... | collective-permute-start | bytes 688136 | tf_op jit(solution)/shard_map/ppermute | solution.py:120
  40.6 6.8 %collective-permute-start.3 = (bf16[896,128]{1,0:T(8,128)(2,1)S(1)}, bf16[896,128]{1,0:T(8,128)(2,1)S(1)}, u32[]{:S(2)}, u32[]{:S(2)}) collective-permute-start(bf16[896,128]{1,0:T(8,128)(2,1)S(1)} %bitcast.8), channel_id=1, source_target_pairs={{0,32},{32,0},{64,96},{96,64},{128,160},{160,128},{192,224},{224,1... | collective-permute-start | bytes 688136 | tf_op jit(solution)/shard_map/ppermute | solution.py:120
  41.4 8.8 %collective-permute-start.6 = (bf16[896,128]{1,0:T(8,128)(2,1)S(1)}, bf16[896,128]{1,0:T(8,128)(2,1)S(1)}, u32[]{:S(2)}, u32[]{:S(2)}) collective-permute-start(bf16[896,128]{1,0:T(8,128)(2,1)S(1)} %collective-permute-done.5.refs_5_), channel_id=1, source_target_pairs={{0,64},{32,96},{64,128},{96,160},{128,192},{160,224},{192,0},{224,... | collective-permute-start | bytes 688136 | tf_op jit(solution)/shard_map/ppermute | solution.py:120
  42.2 8.9 %collective-permute-start.7 = (bf16[896,128]{1,0:T(8,128)(2,1)S(1)}, bf16[896,128]{1,0:T(8,128)(2,1)S(1)}, u32[]{:S(2)}, u32[]{:S(2)}) collective-permute-start(bf16[896,128]{1,0:T(8,128)(2,1)S(1)} %collective-permute-done.1.refs_3_), channel_id=1, source_target_pairs={{0,192},{32,224},{64,0},{96,32},{128,64},{160,96},{192,128},{224,1... | collective-permute-start | bytes 688136 | tf_op jit(solution)/shard_map/ppermute | solution.py:120
  47.5 13.0 %collective-permute-start.9 = (bf16[1792,128]{1,0:T(8,128)(2,1)S(1)}, bf16[1792,128]{1,0:T(8,128)(2,1)S(1)}, u32[]{:S(2)}, u32[]{:S(2)}) collective-permute-start(bf16[1792,128]{1,0:T(8,128)(2,1)S(1)} %joined.1.refs_4_), channel_id=1, source_target_pairs={{0,64},{32,96},{64,128},{96,160},{128,192},{160,224},{192,0},{224,... | collective-permute-start | bytes 1376264 | tf_op jit(solution)/shard_map/ppermute | solution.py:120
  48.2 12.2 %collective-permute-start.8 = (bf16[1792,128]{1,0:T(8,128)(2,1)S(1)}, bf16[1792,128]{1,0:T(8,128)(2,1)S(1)}, u32[]{:S(2)}, u32[]{:S(2)}) collective-permute-start(bf16[1792,128]{1,0:T(8,128)(2,1)S(1)} %joined.1.refs_4_), channel_id=1, source_target_pairs={{0,192},{32,224},{64,0},{96,32},{128,64},{160,96},{192,128},{224,1... | collective-permute-start | bytes 1376264 | tf_op jit(solution)/shard_map/ppermute | solution.py:120
  50.2 6.6 %collective-permute-start.10 = (bf16[896,128]{1,0:T(8,128)(2,1)S(1)}, bf16[896,128]{1,0:T(8,128)(2,1)S(1)}, u32[]{:S(2)}, u32[]{:S(2)}) collective-permute-start(bf16[896,128]{1,0:T(8,128)(2,1)S(1)} %collective-permute-done.6.refs_7_), channel_id=1, source_target_pairs={{0,32},{32,0},{64,96},{96,64},{128,160},{160,128},{192,224},{224,1... | collective-permute-start | bytes 688136 | tf_op jit(solution)/shard_map/ppermute | solution.py:120
  51.1 9.3 %collective-permute-start.11 = (bf16[896,128]{1,0:T(8,128)(2,1)S(1)}, bf16[896,128]{1,0:T(8,128)(2,1)S(1)}, u32[]{:S(2)}, u32[]{:S(2)}) collective-permute-start(bf16[896,128]{1,0:T(8,128)(2,1)S(1)} %collective-permute-done.7.refs_8_), channel_id=1, source_target_pairs={{0,32},{32,0},{64,96},{96,64},{128,160},{160,128},{192,224},{224,1... | collective-permute-start | bytes 688136 | tf_op jit(solution)/shard_map/ppermute | solution.py:120
  52.0 2.0 %copy-start = (bf16[1,1792,1024]{2,1,0:T(8,128)(2,1)S(1)}, bf16[1,1792,1024]{2,1,0:T(8,128)(2,1)}, u32[]{:S(2)}) copy-start(bf16[1,1792,1024]{2,1,0:T(8,128)(2,1)} %param.7) | copy-start | bytes 11010052
